TPU v7x, 32 devices: a whole 2x2x4 slice. The times are simulated.
32 devices in a mesh: group: 8 (over z, y), inner: 4 (over x, core).
Axes of the slice: x: 2, y: 2, z: 4, core: 2. Of those that a mesh axis runs over, the one named last changes fastest.
Arguments:
- tokens: bfloat16 [4096, 7168], P(('group', 'inner')), may hold values from -6 to 6
- target: int32 [4096], P(('group', 'inner')), may hold values from 0 to 8, as said below
- gate_scale: float32 [4096], P(('group', 'inner')), may hold values from 0.25 to 2.5
- gate_weight: bfloat16 [8, 7168, 2048], P('group', None, 'inner'), may hold values from -0.0625 to 0.0625
- up_weight: bfloat16 [8, 7168, 2048], P('group', None, 'inner'), may hold values from -0.0625 to 0.0625
- down_weight: bfloat16 [8, 2048, 7168], P('group', 'inner'), may hold values from -0.125 to 0.125
Outputs:
- routed_out: bfloat16 [4096, 7168], P(('group', 'inner'))
Inputs may be any that keep to these rules, and one draw needn't show every extreme that they name: 8 means that the token uses no expert of this round. Among the 128 tokens of one device at most 20 target any one group, and in every device some group is targeted by exactly 20 of them.
All inputs are finite; a program needn't handle non-finite values.
Results may differ from a plain program's by a relative error of at most 0.0095.
Values may be sent and summed in bfloat16 or wider, within the bound.
No kernel may reach another device: no remote copies, remote signals or barrier semaphores. Data moves between devices by JAX's collectives and lax.ppermute only.
A program may use at most 192 MiB of HBM per device.

v0:
```python
import jax
import jax.numpy as jnp
from jax import lax
from jax.sharding import PartitionSpec as P


def expert_part(rows_in, gate_mat, up_mat, down_mat):
    gate_pre = jnp.dot(rows_in, gate_mat, preferred_element_type=jnp.float32)
    up_pre = jnp.dot(rows_in, up_mat, preferred_element_type=jnp.float32)
    hidden = (jax.nn.silu(gate_pre) * up_pre).astype(jnp.bfloat16)
    return jnp.dot(hidden, down_mat, preferred_element_type=jnp.float32)


def body(tokens, target, gate_scale, gate_weight, up_weight, down_weight):
    groups = lax.axis_size("group")
    tok_count = tokens.shape[0]
    model_width = tokens.shape[1]
    capacity = tok_count * 5 // (4 * groups)
    slot_count = groups * capacity
    onehot = (target[:, None] == jnp.arange(groups, dtype=jnp.int32)[None, :]).astype(jnp.int32)
    rank_in = jnp.sum((jnp.cumsum(onehot, axis=0) - onehot) * onehot, axis=1)
    slot_of = jnp.where(target < groups, target * capacity + rank_in, slot_count)
    dispatch = (slot_of[None, :] == jnp.arange(slot_count, dtype=jnp.int32)[:, None]).astype(
        jnp.bfloat16
    )
    outbound = jnp.dot(dispatch, tokens, preferred_element_type=jnp.float32).astype(jnp.bfloat16)
    gate_mat = gate_weight[0]
    up_mat = up_weight[0]
    down_mat = down_weight[0]
    arrived = lax.all_to_all(
        outbound.reshape(groups, capacity, model_width),
        "group",
        split_axis=0,
        concat_axis=0,
        tiled=True,
    )
    partial_value = expert_part(
        lax.all_gather(arrived.reshape(slot_count, model_width), "inner", axis=0, tiled=True),
        gate_mat,
        up_mat,
        down_mat,
    ).astype(jnp.bfloat16)
    reduced = (
        lax.psum_scatter(partial_value, "inner", scatter_dimension=0, tiled=True)
        .astype(jnp.float32)
        .astype(jnp.bfloat16)
    )
    finished = lax.all_to_all(
        reduced.reshape(groups, capacity, model_width),
        "group",
        split_axis=0,
        concat_axis=0,
        tiled=True,
    )
    back_rows = finished.reshape(slot_count, model_width)
    expert_out = lax.dot_general(
        dispatch, back_rows, (((0,), (0,)), ((), ())), preferred_element_type=jnp.float32
    )
    return (gate_scale[:, None] * expert_out).astype(jnp.bfloat16)


def solution(mesh):
    in_specs = (
        P(("group", "inner"), None),
        P(("group", "inner")),
        P(("group", "inner")),
        P("group", None, "inner"),
        P("group", None, "inner"),
        P("group", "inner", None),
    )
    out_specs = P(("group", "inner"), None)
    return jax.shard_map(body, mesh=mesh, in_specs=in_specs, out_specs=out_specs, check_vma=False)
```

profile of v0, /device:TPU:0, one launch (start us, length us, event | category | flops | bytes accessed | tf_op | source)
XLA Modules:
  0.0 340.4 jit_solution(123887995572340022)
XLA Ops:
  6.5 0.0 copy-start
  6.5 0.0 all-gather.2.cloned.1.call-start
  6.5 0.9 fusion.12
  7.4 0.2 reduce_window_sum.11
  7.6 0.8 select_reduce_fusion
  8.4 0.7 compare_select_fusion
  9.1 2.2 convolution_convert_fusion.1
  11.3 4.1 %reshape.15 = bf16[8,20,7168]{2,1,0:T(8,128)(2,1)} reshape(bf16[160,7168]{1,0:T(8,128)(2,1)} %convolution_convert_fusion.1) | data formatting | bytes 4587520 | tf_op jit(solution)/shard_map/reshape | solution.py:31
  15.4 70.0 %all_to_all.10 = bf16[8,20,7168]{2,1,0:T(8,128)(2,1)} all-to-all(bf16[8,20,7168]{2,1,0:T(8,128)(2,1)} %reshape.15), channel_id=1, replica_groups=mesh['group'=8,'inner'=4] {'group'}, dimensions={0} | all-to-all | bytes 4587520 | tf_op jit(solution)/shard_map/all_to_all | solution.py:30
  85.4 4.2 %reshape.16 = bf16[160,7168]{1,0:T(8,128)(2,1)} reshape(bf16[8,20,7168]{2,1,0:T(8,128)(2,1)} %all_to_all.10) | data formatting | bytes 4587520 | tf_op jit(solution)/shard_map/reshape | solution.py:38
  89.6 0.0 all-gather.2.cloned.1.call-update
  89.6 0.0 reduce-scatter.2.cloned.1.call-start
  89.7 61.5 %all-gather.2.cloned.1.call-done = bf16[640,7168]{1,0:T(8,128)(2,1)} async-done(((bf16[160,7168]{1,0:T(8,128)(2,1)}), bf16[640,7168]{1,0:T(8,128)(2,1)}) %all-gather.2.cloned.1.call-update) | async-done | bytes 9175056 | tf_op jit(solution)/shard_map/all_gather | solution.py:38
  151.2 9.7 %fusion.4 = f32[640,512]{1,0:T(8,128)S(1)} fusion(bf16[640,7168]{1,0:T(8,128)(2,1)} %all-gather.2.cloned.1.call-done, bf16[1,7168,512]{2,1,0:T(8,128)(2,1)} %param.9), kind=kOutput, calls=%fused_computation.7 | convolution fusion | flops 4697620480 | bytes 17825792 | tf_op jit(solution)/shard_map/dot_general | solution.py:8
  160.8 0.0 copy-done.2
  160.9 0.0 slice-start.1
  160.9 8.2 %fusion.9 = bf16[640,512]{1,0:T(8,128)(2,1)S(1)} fusion(bf16[640,7168]{1,0:T(8,128)(2,1)S(1)} %copy-done.2, bf16[1,7168,512]{2,1,0:T(8,128)(2,1)} %param.10, f32[640,512]{1,0:T(8,128)S(1)} %fusion.4), kind=kOutput, calls=%fused_computation.10 | convolution fusion | flops 4699586560 | bytes 18481152 | tf_op jit(solution)/shard_map/dot_general | solution.py:9
  169.2 7.3 %convolution_convert_fusion = bf16[640,7168]{1,0:T(8,128)(2,1)} fusion(bf16[640,512]{1,0:T(8,128)(2,1)S(1)} %fusion.9, bf16[1,512,7168]{2,1,0:T(8,128)(2,1)S(1)} %bitcast.19), kind=kOutput, calls=%fused_computation | convolution fusion | flops 4702208000 | bytes 17170432 | tf_op jit(solution)/shard_map/dot_general | solution.py:11
  176.5 0.0 reduce-scatter.2.cloned.1.call-update
  176.5 76.9 %reduce-scatter.2.cloned.1.call-done = bf16[160,7168]{1,0:T(8,128)(2,1)} async-done(((bf16[640,7168]{1,0:T(8,128)(2,1)}), bf16[160,7168]{1,0:T(8,128)(2,1)}) %reduce-scatter.2.cloned.1.call-update) | async-done | bytes 2293776 | tf_op jit(solution)/shard_map/reduce_scatter | solution.py:44
  253.4 4.1 %reshape.17 = bf16[8,20,7168]{2,1,0:T(8,128)(2,1)} reshape(bf16[160,7168]{1,0:T(8,128)(2,1)} %reduce-scatter.2.cloned.1.call-done) | data formatting | bytes 4587520 | tf_op jit(solution)/shard_map/reshape | solution.py:49
  257.5 68.2 %all_to_all.11 = bf16[8,20,7168]{2,1,0:T(8,128)(2,1)} all-to-all(bf16[8,20,7168]{2,1,0:T(8,128)(2,1)} %reshape.17), channel_id=1, replica_groups=mesh['group'=8,'inner'=4] {'group'}, dimensions={0} | all-to-all | bytes 4587520 | tf_op jit(solution)/shard_map/all_to_all | solution.py:48
  325.8 4.2 %reshape.18 = bf16[160,7168]{1,0:T(8,128)(2,1)} reshape(bf16[8,20,7168]{2,1,0:T(8,128)(2,1)} %all_to_all.11) | data formatting | bytes 4587520 | tf_op jit(solution)/shard_map/reshape | solution.py:55
  330.0 3.6 %fusion = bf16[128,7168]{1,0:T(8,128)(2,1)} fusion(bf16[160,7168]{1,0:T(8,128)(2,1)} %reshape.18, f32[128]{0:T(128)S(1)} %copy-done.1, s32[128]{0:T(128)S(1)} %compare_select_fusion), kind=kOutput, calls=%fused_computation.3 | convolution fusion | flops 295456768 | bytes 4129792 | tf_op jit(solution)/shard_map/dot_general | solution.py:56
  (8 shorter events, 0.0 us)
Async XLA Ops:
  6.5 2.6 copy-start
  6.5 144.6 %all-gather.2.cloned.1.call-start = ((), (), s32[]{:S(2)}) async-start(), calls=%async_computation.3 | async-start | bytes 11468800 | tf_op jit(solution)/shard_map/all_gather | solution.py:38
  89.6 163.8 %reduce-scatter.2.cloned.1.call-start = ((), (), s32[]{:S(2)}) async-start(), calls=%async_computation.4 | async-start | bytes 11468800 | tf_op jit(solution)/shard_map/reduce_scatter | solution.py:44
  151.2 9.7 %copy-start.2 = (bf16[640,7168]{1,0:T(8,128)(2,1)S(1)}, bf16[640,7168]{1,0:T(8,128)(2,1)}, u32[]{:S(2)}) copy-start(bf16[640,7168]{1,0:T(8,128)(2,1)} %all-gather.2.cloned.1.call-done) | copy-start | bytes 27525124
  151.2 18.0 %slice-start = ((s8[7340032]{0:T(1024)(128)(4,1)}), s8[4194304]{0:T(1024)(128)(4,1)S(1)}, s32[]{:S(2)}) async-start(s8[7340032]{0:T(1024)(128)(4,1)} %bitcast.18), calls=%async_computation.5 | async-start | bytes 8388608
  160.9 8.3 %slice-start.1 = ((s8[7340032]{0:T(1024)(128)(4,1)}), s8[3145728]{0:T(1024)(128)(4,1)S(1)}, s32[]{:S(2)}) async-start(s8[7340032]{0:T(1024)(128)(4,1)} %bitcast.18), calls=%async_computation.6 | async-start | bytes 6291456
  325.8 4.2 %copy-start.1 = (f32[128]{0:T(128)S(1)}, f32[128]{0:T(128)}, u32[]{:S(2)}) copy-start(f32[128]{0:T(128)} %param.8) | copy-start | bytes 1540
Sparse Core Ops, SparseCore 0:
  89.7 61.3 all-gather.1
  176.6 76.7 reduce-scatter.1
where the time goes:
time: 341 us; the launch traced here: 340 us
  blocking collectives  138 us (40%)
  waiting for transfers between devices  138 us (40%)
  matrix products  31 us (9%)
  local copies, waits for them, and re-layouts  16.6 us (5%)
  between operations  13.5 us (4%)
    reduce_scatter x1, waiting for transfers between devices, body(): lax.psum_scatter(partial_value, 'inner', scatter_dimension=0, tiled=True)  76.9 us
    all_to_all x1, blocking collectives, body(): lax.all_to_all(outbound.reshape(groups, capacity, model_width), 'group',...  70 us
    all_to_all x1, blocking collectives, body(): lax.all_to_all(reduced.reshape(groups, capacity, model_width), 'group', s...  68.2 us
    all_gather x1, waiting for transfers between devices, body(): lax.all_gather(arrived.reshape(slot_count, model_width), 'inner', axis=0,...  61.5 us
    dot_general x1, matrix products, expert_part(): gate_pre = jnp.dot(rows_in, gate_mat, preferred_element_type=jnp.float32)  9.68 us
    dot_general x1, matrix products, expert_part(): up_pre = jnp.dot(rows_in, up_mat, preferred_element_type=jnp.float32)  8.25 us
    dot_general x1, matrix products, expert_part(): return jnp.dot(hidden, down_mat, preferred_element_type=jnp.float32)  7.32 us
  transfers between devices with their start and end apart: 2, of which 2 were waited for; matrix products, arithmetic and copies ran while one was open for 0% of the time, Pallas kernels for 0%

commit v1 on v0

v1 whole, which is shorter than its diff:
```python
import functools

import jax
import jax.numpy as jnp
from jax import lax
from jax.experimental import pallas as pl
from jax.experimental.pallas import tpu as pltpu
from jax.sharding import PartitionSpec as P

FOLD = 4
CHUNKS = 4
VMEM_LIMIT = 48 * 1024 * 1024


def slots_of(target_row, me, groups, main):
    tok = target_row.shape[1]
    group_id = lax.broadcasted_iota(jnp.int32, (groups, tok), 0)
    hit = (group_id == target_row).astype(jnp.float32)
    earlier = lax.broadcasted_iota(jnp.int32, (tok, tok), 0) < lax.broadcasted_iota(
        jnp.int32, (tok, tok), 1
    )
    before = jnp.dot(
        hit.astype(jnp.bfloat16),
        earlier.astype(jnp.float32).astype(jnp.bfloat16),
        preferred_element_type=jnp.float32,
    )
    rank = jnp.sum(hit * before, axis=0, keepdims=True).astype(jnp.int32)
    valid = target_row < groups
    base = (target_row ^ me) * main
    main_slot = jnp.where(valid & (rank < main), base + rank, -1)
    tail_slot = jnp.where(valid & (rank >= main), base + rank - main, -(10**6))
    return main_slot, tail_slot


def onehot_rows(slot, rows):
    index = lax.broadcasted_iota(jnp.int32, (rows, slot.shape[1]), 0)
    return (index == slot).astype(jnp.float32).astype(jnp.bfloat16)


def dispatch_kernel(groups, main, me_ref, target_ref, tokens_ref, *out_refs):
    unit = main // FOLD
    rows = groups * main
    width = tokens_ref.shape[1]
    piece = width // FOLD
    main_slot, tail_slot = slots_of(target_ref[...], me_ref[0], groups, main)
    pick_main = onehot_rows(main_slot, rows)
    tail = jnp.zeros((rows, piece), jnp.float32)
    for q in range(FOLD):
        columns = slice(q * piece, (q + 1) * piece)
        block = tokens_ref[:, columns]
        picked = jnp.dot(pick_main, block, preferred_element_type=jnp.float32)
        for k in range(groups):
            out_refs[k][:, columns] = picked[k * main : (k + 1) * main].astype(jnp.bfloat16)
        tail += jnp.dot(
            onehot_rows(tail_slot + q * unit, rows), block, preferred_element_type=jnp.float32
        )
    for k in range(groups):
        out_refs[k][:, width:] = tail[k * main : (k + 1) * main].astype(jnp.bfloat16)


def combine_kernel(groups, main, me_ref, target_ref, scale_ref, *refs):
    back_refs, out_ref = refs[:-1], refs[-1]
    unit = main // FOLD
    rows = groups * main
    tok, width = out_ref.shape
    piece = width // FOLD
    main_slot, tail_slot = slots_of(target_ref[...], me_ref[0], groups, main)
    pick_main = onehot_rows(main_slot, rows)
    square = lax.broadcasted_iota(jnp.int32, (tok, tok), 0) == lax.broadcasted_iota(
        jnp.int32, (tok, tok), 1
    )
    scale = jnp.sum(jnp.where(square, scale_ref[...], 0.0), axis=1, keepdims=True)

    def joined(columns):
        parts = [r[:, columns] for r in back_refs]
        if main % 16 == 0:
            return jnp.concatenate(parts, axis=0)
        return jnp.concatenate([p.astype(jnp.float32) for p in parts], axis=0).astype(jnp.bfloat16)

    tail = joined(slice(width, width + piece))
    over_slots = (((0,), (0,)), ((), ()))
    for q in range(FOLD):
        columns = slice(q * piece, (q + 1) * piece)
        value = lax.dot_general(
            pick_main, joined(columns), over_slots, preferred_element_type=jnp.float32
        )
        value += lax.dot_general(
            onehot_rows(tail_slot + q * unit, rows),
            tail,
            over_slots,
            preferred_element_type=jnp.float32,
        )
        out_ref[:, columns] = (scale * value).astype(jnp.bfloat16)


def expert_kernel(main, parts, gate_ref, up_ref, down_ref, *refs):
    in_refs = refs[:parts]
    keep_ref, send_ref, rows_ref, gate_acc, up_acc, hidden_ref, tail_acc = refs[parts:]
    unit = main // FOLD
    step = pl.program_id(0)
    part_rows = in_refs[0].shape[0]
    rows = parts * part_rows
    half = rows // 2
    tail_rows = rows // FOLD
    piece = gate_ref.shape[0]
    width = piece * FOLD

    def fold_matrix(q):
        tail_id = lax.broadcasted_iota(jnp.int32, (tail_rows, rows), 0)
        folded = lax.broadcasted_iota(jnp.int32, (tail_rows, rows), 1)
        wanted = (tail_id // unit) * main + q * unit + tail_id % unit
        return (wanted == folded).astype(jnp.float32).astype(jnp.bfloat16)

    @pl.when(step == 0)
    def _():
        for a in range(parts):
            for q in range(FOLD):
                rows_ref[q, a * part_rows : (a + 1) * part_rows, :] = in_refs[a][
                    :, q * piece : (q + 1) * piece
                ]
        folded = jnp.concatenate([r[:, width:] for r in in_refs], axis=0)
        for q in range(FOLD):
            rows_ref[q, rows:, :] = jnp.dot(
                fold_matrix(q), folded, preferred_element_type=jnp.float32
            ).astype(jnp.bfloat16)
        gate_acc[...] = jnp.zeros_like(gate_acc)
        up_acc[...] = jnp.zeros_like(up_acc)
        tail_acc[...] = jnp.zeros_like(tail_acc)

    @pl.when(step < FOLD)
    def _():
        block = rows_ref[step]
        gate_acc[...] += jnp.dot(block, gate_ref[...], preferred_element_type=jnp.float32)
        up_acc[...] += jnp.dot(block, up_ref[...], preferred_element_type=jnp.float32)

    @pl.when(step == FOLD - 1)
    def _():
        gate_pre = gate_acc[...]
        hidden_ref[...] = (gate_pre / (1.0 + jnp.exp(-gate_pre)) * up_acc[...]).astype(jnp.bfloat16)

    @pl.when((step >= FOLD) & (step < 2 * FOLD))
    def _():
        partial = jnp.dot(
            hidden_ref[...], down_ref[...], preferred_element_type=jnp.float32
        ).astype(jnp.bfloat16)
        keep_ref[...] = partial[:half]
        send_ref[...] = partial[half:rows]
        tail_acc[...] += lax.dot_general(
            fold_matrix(step - FOLD),
            partial[rows:],
            (((0,), (0,)), ((), ())),
            preferred_element_type=jnp.float32,
        )

    @pl.when(step == 2 * FOLD)
    def _():
        tail = tail_acc[...].astype(jnp.bfloat16)
        keep_ref[...] = tail[:half]
        send_ref[...] = tail[half:]


def run_experts(blocks, gate_mat, up_mat, down_mat, main):
    parts = len(blocks)
    part_rows, folded_width = blocks[0].shape
    width, slice_width = gate_mat.shape
    piece = width // FOLD
    rows = parts * part_rows
    half = rows // 2
    every = rows + rows // FOLD
    whole = pl.BlockSpec((part_rows, folded_width), lambda i: (0, 0))
    into = pl.BlockSpec((piece, slice_width), lambda i: (jnp.minimum(i, FOLD - 1), 0))
    out_of = pl.BlockSpec((slice_width, piece), lambda i: (0, jnp.clip(i - FOLD, 0, FOLD - 1)))
    result = pl.BlockSpec((half, piece), lambda i: (0, jnp.maximum(i - FOLD, 0)))
    return pl.pallas_call(
        functools.partial(expert_kernel, main, parts),
        grid=(2 * FOLD + 1,),
        in_specs=[into, into, out_of] + [whole] * parts,
        out_specs=[result, result],
        out_shape=[jax.ShapeDtypeStruct((half, folded_width), jnp.bfloat16)] * 2,
        scratch_shapes=[
            pltpu.VMEM((FOLD, every, piece), jnp.bfloat16),
            pltpu.VMEM((every, slice_width), jnp.float32),
            pltpu.VMEM((every, slice_width), jnp.float32),
            pltpu.VMEM((every, slice_width), jnp.bfloat16),
            pltpu.VMEM((rows, piece), jnp.float32),
        ],
        compiler_params=pltpu.CompilerParams(vmem_limit_bytes=VMEM_LIMIT),
        cost_estimate=pl.CostEstimate(
            flops=6 * every * width * slice_width,
            bytes_accessed=6 * width * slice_width + 4 * rows * folded_width,
            transcendentals=every * slice_width,
        ),
        name="experts",
    )(gate_mat, up_mat, down_mat, *blocks)


def f32(x):
    return x.astype(jnp.float32)


def body(tokens, target, gate_scale, gate_weight, up_weight, down_weight):
    groups = lax.axis_size("group")
    inner = lax.axis_size("inner")
    chips = inner // 2
    tok_count, width = tokens.shape
    capacity = tok_count * 5 // (4 * groups)
    main = capacity * FOLD // (FOLD + 1)
    folded_width = width + width // FOLD
    per_chunk = groups // CHUNKS

    def to_group(x, offset):
        return lax.ppermute(x, "group", [(i, i ^ offset) for i in range(groups)])

    def to_chip(x, offset):
        return lax.ppermute(x, "inner", [(i, i ^ (2 * offset)) for i in range(inner)])

    def to_core(x):
        return lax.ppermute(x, "inner", [(i, i ^ 1) for i in range(inner)])

    me = lax.axis_index("group").astype(jnp.int32).reshape(1)
    target_row = target.reshape(1, tok_count)
    scalar = pl.BlockSpec(memory_space=pltpu.SMEM)
    vmem = pl.BlockSpec(memory_space=pltpu.VMEM)
    outbound = pl.pallas_call(
        functools.partial(dispatch_kernel, groups, main),
        in_specs=[scalar, vmem, vmem],
        out_specs=[vmem] * groups,
        out_shape=[jax.ShapeDtypeStruct((main, folded_width), jnp.bfloat16)] * groups,
        compiler_params=pltpu.CompilerParams(vmem_limit_bytes=VMEM_LIMIT),
        cost_estimate=pl.CostEstimate(
            flops=4 * tok_count * tok_count * width,
            bytes_accessed=5 * tok_count * width,
            transcendentals=0,
        ),
        name="dispatch",
    )(me, target_row, tokens)

    gate_mat, up_mat, down_mat = gate_weight[0], up_weight[0], down_weight[0]
    back = [None] * groups
    arrived = {}
    for k in sorted(range(groups), key=lambda k: -k):
        arrived[k] = to_group(outbound[k], k) if k else outbound[0]
    for chunk in (0, 1, 3, 2):
        offsets = range(chunk * per_chunk, (chunk + 1) * per_chunk)
        own = jnp.concatenate([arrived[k] for k in offsets], axis=0)
        held = [own] + [to_chip(own, c) for c in range(1, chips)]
        held += [to_core(x) for x in held]
        keep, send = run_experts(held, gate_mat, up_mat, down_mat, main)
        got = to_core(send)
        count = own.shape[0]
        mine = f32(keep[:count]) + f32(got[:count])
        for c in range(1, chips):
            rows = slice(c * count, (c + 1) * count)
            theirs = (f32(keep[rows]) + f32(got[rows])).astype(jnp.bfloat16)
            mine = mine + f32(to_chip(theirs, c))
        finished = mine.astype(jnp.bfloat16)
        for n, k in enumerate(offsets):
            rows = finished[n * main : (n + 1) * main]
            back[k] = to_group(rows, k) if k else rows

    return pl.pallas_call(
        functools.partial(combine_kernel, groups, main),
        in_specs=[scalar] + [vmem] * (2 + groups),
        out_specs=vmem,
        out_shape=jax.ShapeDtypeStruct((tok_count, width), jnp.bfloat16),
        compiler_params=pltpu.CompilerParams(vmem_limit_bytes=VMEM_LIMIT),
        cost_estimate=pl.CostEstimate(
            flops=4 * tok_count * tok_count * width,
            bytes_accessed=5 * tok_count * width,
            transcendentals=0,
        ),
        name="combine",
    )(me, target_row, gate_scale.reshape(1, tok_count), *back)


def solution(mesh):
    in_specs = (
        P(("group", "inner"), None),
        P(("group", "inner")),
        P(("group", "inner")),
        P("group", None, "inner"),
        P("group", None, "inner"),
        P("group", "inner", None),
    )
    out_specs = P(("group", "inner"), None)
    return jax.shard_map(body, mesh=mesh, in_specs=in_specs, out_specs=out_specs, check_vma=False)
```

time: 341 us -> 230 us (0.67)
  blocking collectives: 138 us -> 0 us
  starting transfers between devices: 0.04 us -> 59.1 us
  Pallas kernels: 0 us -> 55.2 us
  matrix products: 31 us -> 0 us
  waiting for transfers between devices: 138 us -> 111 us
  local copies, waits for them, and re-layouts: 16.6 us -> 2.48 us
  between operations: 13.5 us -> 0.25 us
    all_to_all x2 -> x0, blocking collectives: 138 us -> none  [the longest x1 70 us: body(): lax.all_to_all(outbound.reshape(groups, capacity, model_width), 'group',...]
    ppermute x0 -> x34, waiting for transfers between devices: none -> 111 us  [the longest x8 69 us: to_chip(): return lax.ppermute(x, 'inner', [(i, i ^ 2 * offset) for i in range(inner)])]
    reduce_scatter x1 -> x0, waiting for transfers between devices: 76.9 us -> none  [body(): lax.psum_scatter(partial_value, 'inner', scatter_dimension=0, tiled=True)]
    all_gather x1 -> x0, waiting for transfers between devices: 61.5 us -> none  [body(): lax.all_gather(arrived.reshape(slot_count, model_width), 'inner', axis=0,...]
    ppermute x0 -> x34, starting transfers between devices: none -> 59.1 us  [the longest x14 46.9 us: to_group(): return lax.ppermute(x, 'group', [(i, i ^ offset) for i in range(groups)])]
    pallas_call x0 -> x6, Pallas kernels: none -> 55.2 us  [the longest x4 51.4 us: run_experts(): pl.pallas_call(functools.partial(expert_kernel, main, parts), grid=(2 * F...]
    dot_general x5 -> x0, matrix products: 31 us -> none  [the longest x1 9.68 us: expert_part(): gate_pre = jnp.dot(rows_in, gate_mat, preferred_element_type=jnp.float32)]
    reshape x4 -> x0, local copies, waits for them, and re-layouts: 16.6 us -> none  [the longest x1 4.18 us: body(): back_rows = finished.reshape(slot_count, model_width)]
  transfers between devices with their start and end apart: 2 -> 34, of which waited for: 2 -> 14; matrix products, arithmetic and copies ran while one was open for 0% -> 1% of each run, Pallas kernels for 0% -> 22%
where the time goes in v1:
time: 230 us
  waiting for transfers between devices  111 us (48%)
  starting transfers between devices  59.1 us (26%)
  Pallas kernels  55.2 us (24%)
  local copies, waits for them, and re-layouts  2.48 us (1%)
    ppermute x8, waiting for transfers between devices, to_chip(): return lax.ppermute(x, 'inner', [(i, i ^ 2 * offset) for i in range(inner)])  69 us
    pallas_call x4, Pallas kernels, run_experts(): pl.pallas_call(functools.partial(expert_kernel, main, parts), grid=(2 * F...  51.4 us
    ppermute x14, starting transfers between devices, to_group(): return lax.ppermute(x, 'group', [(i, i ^ offset) for i in range(groups)])  46.9 us
    ppermute x14, waiting for transfers between devices, to_group(): return lax.ppermute(x, 'group', [(i, i ^ offset) for i in range(groups)])  42.4 us
    ppermute x8, starting transfers between devices, to_chip(): return lax.ppermute(x, 'inner', [(i, i ^ 2 * offset) for i in range(inner)])  9.52 us
  transfers between devices with their start and end apart: 34, of which 14 were waited for; matrix products, arithmetic and copies ran while one was open for 1% of the time, Pallas kernels for 22%

profile of v1, /device:TPU:0, one launch (start us, length us, event | category | flops | bytes accessed | tf_op | source)
XLA Modules:
  0.0 229.8 jit_solution(14508927675179859871)
XLA Ops:
  3.4 5.1 %collective-permute-start.25 = (bf16[16,8960]{1,0:T(8,128)(2,1)S(1)}, bf16[16,8960]{1,0:T(8,128)(2,1)S(1)}, u32[]{:S(2)}, u32[]{:S(2)}) collective-permute-start(bf16[16,8960]{1,0:T(8,128)(2,1)S(1)} %get-tuple-element.33), channel_id=1, source_target_pairs={{0,24},{4,28},{8,16},{12,20},{16,8},{20,12},{24,0},{28,4},{1,25},{... | collective-permute-start | bytes 860168 | tf_op jit(solution)/shard_map/ppermute | solution.py:212
  13.9 2.5 %collective-permute-done.25 = bf16[16,8960]{1,0:T(8,128)(2,1)S(1)} collective-permute-done((bf16[16,8960]{1,0:T(8,128)(2,1)S(1)}, bf16[16,8960]{1,0:T(8,128)(2,1)S(1)}, u32[]{:S(2)}, u32[]{:S(2)}) %collective-permute-start.25) | collective-permute-done | bytes 286752 | tf_op jit(solution)/shard_map/ppermute | solution.py:212
  16.4 25.2 %collective-permute-start.8 = (bf16[16,8960]{1,0:T(8,128)(2,1)S(1)}, bf16[16,8960]{1,0:T(8,128)(2,1)S(1)}, u32[]{:S(2)}, u32[]{:S(2)}) collective-permute-start(bf16[16,8960]{1,0:T(8,128)(2,1)S(1)} %get-tuple-element.26), channel_id=1, source_target_pairs={{0,12},{4,8},{8,4},{12,0},{16,28},{20,24},{24,20},{28,16},{1,13},{... | collective-permute-start | bytes 860168 | tf_op jit(solution)/shard_map/ppermute | solution.py:212
  42.2 11.6 %collective-permute-done.16 = bf16[16,8960]{1,0:T(8,128)(2,1)S(1)} collective-permute-done((bf16[16,8960]{1,0:T(8,128)(2,1)S(1)}, bf16[16,8960]{1,0:T(8,128)(2,1)S(1)}, u32[]{:S(2)}, u32[]{:S(2)}) %collective-permute-start.16) | collective-permute-done | bytes 286752 | tf_op jit(solution)/shard_map/ppermute | solution.py:212
  55.3 5.4 %collective-permute-done.17 = bf16[16,8960]{1,0:T(8,128)(2,1)S(1)} collective-permute-done((bf16[16,8960]{1,0:T(8,128)(2,1)S(1)}, bf16[16,8960]{1,0:T(8,128)(2,1)S(1)}, u32[]{:S(2)}, u32[]{:S(2)}) %collective-permute-start.17) | collective-permute-done | bytes 286752 | tf_op jit(solution)/shard_map/ppermute | solution.py:212
  63.2 6.5 %collective-permute-done.27.refs_1_ = bf16[32,8960]{1,0:T(8,128)(2,1)S(1)} collective-permute-done((bf16[32,8960]{1,0:T(8,128)(2,1)S(1)}, bf16[32,8960]{1,0:T(8,128)(2,1)S(1)}, u32[]{:S(2)}, u32[]{:S(2)}) %collective-permute-start.27) | collective-permute-done | bytes 573472 | tf_op jit(solution)/shard_map/ppermute | solution.py:215
  71.3 10.7 %collective-permute-done.18.refs_1_ = bf16[32,8960]{1,0:T(8,128)(2,1)S(1)} collective-permute-done((bf16[32,8960]{1,0:T(8,128)(2,1)S(1)}, bf16[32,8960]{1,0:T(8,128)(2,1)S(1)}, u32[]{:S(2)}, u32[]{:S(2)}) %collective-permute-start.18) | collective-permute-done | bytes 573472 | tf_op jit(solution)/shard_map/ppermute | solution.py:215
  82.0 12.3 %collective-permute-done.9.refs_1_ = bf16[32,8960]{1,0:T(8,128)(2,1)S(1)} collective-permute-done((bf16[32,8960]{1,0:T(8,128)(2,1)S(1)}, bf16[32,8960]{1,0:T(8,128)(2,1)S(1)}, u32[]{:S(2)}, u32[]{:S(2)}) %collective-permute-start.9) | collective-permute-done | bytes 573472 | tf_op jit(solution)/shard_map/ppermute | solution.py:215
  94.8 12.9 %experts.7 = (bf16[64,8960]{1,0:T(8,128)(2,1)S(1)}, bf16[64,8960]{1,0:T(8,128)(2,1)S(1)}) custom-call(bf16[7168,512]{1,0:T(8,128)(2,1)} %bitcast.9, bf16[7168,512]{1,0:T(8,128)(2,1)} %bitcast.13, bf16[512,7168]{1,0:T(8,128)(2,1)} %bitcast.17, bf16[32,8960]{1,0:T(8,128)(2,1)S(1)} %constant_dynamic-update-slice_fusion.6.refs_0_, ...), custom_call_target="tpu_custom_call" | custom-call | flops 3523215360 | bytes 26607616 | tf_op jit(solution)/shard_map/experts/pallas_call | solution.py:174
  108.5 12.9 %experts.6 = (bf16[64,8960]{1,0:T(8,128)(2,1)S(1)}, bf16[64,8960]{1,0:T(8,128)(2,1)S(1)}) custom-call(bf16[7168,512]{1,0:T(8,128)(2,1)} %bitcast.10, bf16[7168,512]{1,0:T(8,128)(2,1)} %bitcast.14, bf16[512,7168]{1,0:T(8,128)(2,1)} %bitcast.18, bf16[32,8960]{1,0:T(8,128)(2,1)S(1)} %constant_dynamic-update-slice_fusion.4.refs_0_, ...), custom_call_target="tpu_custom_call" | custom-call | flops 3523215360 | bytes 26607616 | tf_op jit(solution)/shard_map/experts/pallas_call | solution.py:174
  121.7 12.9 %experts.5 = (bf16[64,8960]{1,0:T(8,128)(2,1)S(1)}, bf16[64,8960]{1,0:T(8,128)(2,1)S(1)}) custom-call(bf16[7168,512]{1,0:T(8,128)(2,1)} %bitcast.11, bf16[7168,512]{1,0:T(8,128)(2,1)} %bitcast.15, bf16[512,7168]{1,0:T(8,128)(2,1)} %bitcast.19, bf16[32,8960]{1,0:T(8,128)(2,1)S(1)} %constant_dynamic-update-slice_fusion.2.refs_0_, ...), custom_call_target="tpu_custom_call" | custom-call | flops 3523215360 | bytes 26607616 | tf_op jit(solution)/shard_map/experts/pallas_call | solution.py:174
  134.8 12.9 %experts.4 = (bf16[64,8960]{1,0:T(8,128)(2,1)S(1)}, bf16[64,8960]{1,0:T(8,128)(2,1)S(1)}) custom-call(bf16[7168,512]{1,0:T(8,128)(2,1)} %bitcast.12, bf16[7168,512]{1,0:T(8,128)(2,1)} %bitcast.16, bf16[512,7168]{1,0:T(8,128)(2,1)} %bitcast.20, bf16[32,8960]{1,0:T(8,128)(2,1)S(1)} %constant_dynamic-update-slice_fusion.refs_0_, ...), custom_call_target="tpu_custom_call" | custom-call | flops 3523215360 | bytes 26607616 | tf_op jit(solution)/shard_map/experts/pallas_call | solution.py:174
  153.0 11.1 %collective-permute-done.31 = bf16[32,8960]{1,0:T(8,128)(2,1)S(1)} collective-permute-done((bf16[32,8960]{1,0:T(8,128)(2,1)S(1)}, bf16[32,8960]{1,0:T(8,128)(2,1)S(1)}, u32[]{:S(2)}, u32[]{:S(2)}) %collective-permute-start.31) | collective-permute-done | bytes 573472 | tf_op jit(solution)/shard_map/ppermute | solution.py:215
  164.4 2.0 collective-permute-start.32
  166.3 3.6 %collective-permute-start.33 = (bf16[16,8960]{1,0:T(8,128)(2,1)S(1)}, bf16[16,8960]{1,0:T(8,128)(2,1)S(1)}, u32[]{:S(2)}, u32[]{:S(2)}) collective-permute-start(bf16[16,8960]{1,0:T(8,128)(2,1)S(1)} %get-tuple-element.37), channel_id=1, source_target_pairs={{0,28},{4,24},{8,20},{12,16},{16,12},{20,8},{24,4},{28,0},{1,29},{... | collective-permute-start | bytes 860168 | tf_op jit(solution)/shard_map/ppermute | solution.py:212
  170.0 6.4 %collective-permute-done.22 = bf16[32,8960]{1,0:T(8,128)(2,1)S(1)} collective-permute-done((bf16[32,8960]{1,0:T(8,128)(2,1)S(1)}, bf16[32,8960]{1,0:T(8,128)(2,1)S(1)}, u32[]{:S(2)}, u32[]{:S(2)}) %collective-permute-start.22) | collective-permute-done | bytes 573472 | tf_op jit(solution)/shard_map/ppermute | solution.py:215
  176.7 12.0 %collective-permute-done.13 = bf16[32,8960]{1,0:T(8,128)(2,1)S(1)} collective-permute-done((bf16[32,8960]{1,0:T(8,128)(2,1)S(1)}, bf16[32,8960]{1,0:T(8,128)(2,1)S(1)}, u32[]{:S(2)}, u32[]{:S(2)}) %collective-permute-start.13) | collective-permute-done | bytes 573472 | tf_op jit(solution)/shard_map/ppermute | solution.py:215
  190.2 10.0 %collective-permute-done.5 = bf16[32,8960]{1,0:T(8,128)(2,1)S(1)} collective-permute-done((bf16[32,8960]{1,0:T(8,128)(2,1)S(1)}, bf16[32,8960]{1,0:T(8,128)(2,1)S(1)}, u32[]{:S(2)}, u32[]{:S(2)}) %collective-permute-start.5) | collective-permute-done | bytes 573472 | tf_op jit(solution)/shard_map/ppermute | solution.py:215
  200.5 3.8 %collective-permute-start.15 = (bf16[16,8960]{1,0:T(8,128)(2,1)S(1)}, bf16[16,8960]{1,0:T(8,128)(2,1)S(1)}, u32[]{:S(2)}, u32[]{:S(2)}) collective-permute-start(bf16[16,8960]{1,0:T(8,128)(2,1)S(1)} %get-tuple-element.41), channel_id=1, source_target_pairs={{0,12},{4,8},{8,4},{12,0},{16,28},{20,24},{24,20},{28,16},{1,13},{... | collective-permute-start | bytes 860168 | tf_op jit(solution)/shard_map/ppermute | solution.py:212
  204.3 6.1 %collective-permute-done.23.refs_4_ = bf16[16,8960]{1,0:T(8,128)(2,1)S(1)} collective-permute-done((bf16[16,8960]{1,0:T(8,128)(2,1)S(1)}, bf16[16,8960]{1,0:T(8,128)(2,1)S(1)}, u32[]{:S(2)}, u32[]{:S(2)}) %collective-permute-start.23) | collective-permute-done | bytes 286752 | tf_op jit(solution)/shard_map/ppermute | solution.py:212
  210.5 5.8 %collective-permute-done.24.refs_5_ = bf16[16,8960]{1,0:T(8,128)(2,1)S(1)} collective-permute-done((bf16[16,8960]{1,0:T(8,128)(2,1)S(1)}, bf16[16,8960]{1,0:T(8,128)(2,1)S(1)}, u32[]{:S(2)}, u32[]{:S(2)}) %collective-permute-start.24) | collective-permute-done | bytes 286752 | tf_op jit(solution)/shard_map/ppermute | solution.py:212
  216.3 3.8 %collective-permute-done.14.refs_2_ = bf16[16,8960]{1,0:T(8,128)(2,1)S(1)} collective-permute-done((bf16[16,8960]{1,0:T(8,128)(2,1)S(1)}, bf16[16,8960]{1,0:T(8,128)(2,1)S(1)}, u32[]{:S(2)}, u32[]{:S(2)}) %collective-permute-start.14) | collective-permute-done | bytes 286752 | tf_op jit(solution)/shard_map/ppermute | solution.py:212
  220.1 7.1 %collective-permute-done.15.refs_3_ = bf16[16,8960]{1,0:T(8,128)(2,1)S(1)} collective-permute-done((bf16[16,8960]{1,0:T(8,128)(2,1)S(1)}, bf16[16,8960]{1,0:T(8,128)(2,1)S(1)}, u32[]{:S(2)}, u32[]{:S(2)}) %collective-permute-start.15) | collective-permute-done | bytes 286752 | tf_op jit(solution)/shard_map/ppermute | solution.py:212
  227.3 2.5 %combine.1 = bf16[128,7168]{1,0:T(8,128)(2,1)} custom-call(s32[1]{0:T(128)} %bitcast.me_ref, s32[1,128]{1,0:T(1,128)S(1)} %bitcast.7, f32[1,128]{1,0:T(1,128)S(1)} %bitcast.8, bf16[16,8960]{1,0:T(8,128)(2,1)S(1)} %get-tuple-element.44.refs_0_, bf16[16,8960]{1,0:T(8,128)(2,1)S(1)} %collective-permute-done.6.refs_1_, ...), custom_call_target="tpu_custom_call" | custom-call | flops 469762048 | bytes 4587520 | tf_op jit(solution)/shard_map/combine/pallas_call | solution.py:261
  (78 shorter events, 24.5 us)
Async XLA Ops:
  8.5 33.1 %collective-permute-start.26 = (bf16[16,8960]{1,0:T(8,128)(2,1)S(1)}, bf16[16,8960]{1,0:T(8,128)(2,1)S(1)}, u32[]{:S(2)}, u32[]{:S(2)}) collective-permute-start(bf16[16,8960]{1,0:T(8,128)(2,1)S(1)} %get-tuple-element.34), channel_id=1, source_target_pairs={{0,28},{4,24},{8,20},{12,16},{16,12},{20,8},{24,4},{28,0},{1,29},{... | collective-permute-start | bytes 860168 | tf_op jit(solution)/shard_map/ppermute | solution.py:212
  9.7 44.1 %collective-permute-start.16 = (bf16[16,8960]{1,0:T(8,128)(2,1)S(1)}, bf16[16,8960]{1,0:T(8,128)(2,1)S(1)}, u32[]{:S(2)}, u32[]{:S(2)}) collective-permute-start(bf16[16,8960]{1,0:T(8,128)(2,1)S(1)} %get-tuple-element.29), channel_id=1, source_target_pairs={{0,16},{4,20},{8,24},{12,28},{16,0},{20,4},{24,8},{28,12},{1,17},{... | collective-permute-start | bytes 860168 | tf_op jit(solution)/shard_map/ppermute | solution.py:212
  10.5 50.2 %collective-permute-start.17 = (bf16[16,8960]{1,0:T(8,128)(2,1)S(1)}, bf16[16,8960]{1,0:T(8,128)(2,1)S(1)}, u32[]{:S(2)}, u32[]{:S(2)}) collective-permute-start(bf16[16,8960]{1,0:T(8,128)(2,1)S(1)} %get-tuple-element.30), channel_id=1, source_target_pairs={{0,20},{4,16},{8,28},{12,24},{16,4},{20,0},{24,12},{28,8},{1,21},{... | collective-permute-start | bytes 860168 | tf_op jit(solution)/shard_map/ppermute | solution.py:212
  12.4 48.3 %collective-permute-start.7 = (bf16[16,8960]{1,0:T(8,128)(2,1)S(1)}, bf16[16,8960]{1,0:T(8,128)(2,1)S(1)}, u32[]{:S(2)}, u32[]{:S(2)}) collective-permute-start(bf16[16,8960]{1,0:T(8,128)(2,1)S(1)} %get-tuple-element.25), channel_id=1, source_target_pairs={{0,8},{4,12},{8,0},{12,4},{16,24},{20,28},{24,16},{28,20},{1,9},{5... | collective-permute-start | bytes 860168 | tf_op jit(solution)/shard_map/ppermute | solution.py:212
  16.4 45.9 %collective-permute-start.8 = (bf16[16,8960]{1,0:T(8,128)(2,1)S(1)}, bf16[16,8960]{1,0:T(8,128)(2,1)S(1)}, u32[]{:S(2)}, u32[]{:S(2)}) collective-permute-start(bf16[16,8960]{1,0:T(8,128)(2,1)S(1)} %get-tuple-element.26), channel_id=1, source_target_pairs={{0,12},{4,8},{8,4},{12,0},{16,28},{20,24},{24,20},{28,16},{1,13},{... | collective-permute-start | bytes 860168 | tf_op jit(solution)/shard_map/ppermute | solution.py:212
  62.3 45.3 %collective-permute-start.19 = (bf16[32,8960]{1,0:T(8,128)(2,1)S(1)}, bf16[32,8960]{1,0:T(8,128)(2,1)S(1)}, u32[]{:S(2)}, u32[]{:S(2)}) collective-permute-start(bf16[32,8960]{1,0:T(8,128)(2,1)S(1)} %constant_dynamic-update-slice_fusion.4.refs_0_), channel_id=1, source_target_pairs={{0,1},{1,0},{2,3},{3,2},{4,5},{5,4},{6,7},{7,6},{8,9},{9,8},{10,11... | collective-permute-start | bytes 1720328 | tf_op jit(solution)/shard_map/ppermute | solution.py:218
  62.7 31.6 %collective-permute-start.9 = (bf16[32,8960]{1,0:T(8,128)(2,1)S(1)}, bf16[32,8960]{1,0:T(8,128)(2,1)S(1)}, u32[]{:S(2)}, u32[]{:S(2)}) collective-permute-start(bf16[32,8960]{1,0:T(8,128)(2,1)S(1)} %constant_dynamic-update-slice_fusion.2.refs_0_), channel_id=1, source_target_pairs={{0,2},{1,3},{2,0},{3,1},{4,6},{5,7},{6,4},{7,5},{8,10},{9,11},{10,... | collective-permute-start | bytes 1720328 | tf_op jit(solution)/shard_map/ppermute | solution.py:215
  69.7 24.6 %collective-permute-start.29 = (bf16[32,8960]{1,0:T(8,128)(2,1)S(1)}, bf16[32,8960]{1,0:T(8,128)(2,1)S(1)}, u32[]{:S(2)}, u32[]{:S(2)}) collective-permute-start(bf16[32,8960]{1,0:T(8,128)(2,1)S(1)} %collective-permute-done.27.refs_1_), channel_id=1, source_target_pairs={{0,1},{1,0},{2,3},{3,2},{4,5},{5,4},{6,7},{7,6},{8,9},{9,8},{10,11... | collective-permute-start | bytes 1720328 | tf_op jit(solution)/shard_map/ppermute | solution.py:218
  69.7 38.2 %collective-permute-start.1 = (bf16[32,8960]{1,0:T(8,128)(2,1)S(1)}, bf16[32,8960]{1,0:T(8,128)(2,1)S(1)}, u32[]{:S(2)}, u32[]{:S(2)}) collective-permute-start(bf16[32,8960]{1,0:T(8,128)(2,1)S(1)} %constant_dynamic-update-slice_fusion.refs_0_), channel_id=1, source_target_pairs={{0,2},{1,3},{2,0},{3,1},{4,6},{5,7},{6,4},{7,5},{8,10},{9,11},{10,... | collective-permute-start | bytes 1720328 | tf_op jit(solution)/shard_map/ppermute | solution.py:215
  82.0 26.3 %collective-permute-start.20 = (bf16[32,8960]{1,0:T(8,128)(2,1)S(1)}, bf16[32,8960]{1,0:T(8,128)(2,1)S(1)}, u32[]{:S(2)}, u32[]{:S(2)}) collective-permute-start(bf16[32,8960]{1,0:T(8,128)(2,1)S(1)} %collective-permute-done.18.refs_1_), channel_id=1, source_target_pairs={{0,1},{1,0},{2,3},{3,2},{4,5},{5,4},{6,7},{7,6},{8,9},{9,8},{10,11... | collective-permute-start | bytes 1720328 | tf_op jit(solution)/shard_map/ppermute | solution.py:218
  94.3 27.0 %collective-permute-start.10 = (bf16[32,8960]{1,0:T(8,128)(2,1)S(1)}, bf16[32,8960]{1,0:T(8,128)(2,1)S(1)}, u32[]{:S(2)}, u32[]{:S(2)}) collective-permute-start(bf16[32,8960]{1,0:T(8,128)(2,1)S(1)} %constant_dynamic-update-slice_fusion.2.refs_0_), channel_id=1, source_target_pairs={{0,1},{1,0},{2,3},{3,2},{4,5},{5,4},{6,7},{7,6},{8,9},{9,8},{10,11... | collective-permute-start | bytes 1720328 | tf_op jit(solution)/shard_map/ppermute | solution.py:218
  94.3 27.4 %collective-permute-start.11 = (bf16[32,8960]{1,0:T(8,128)(2,1)S(1)}, bf16[32,8960]{1,0:T(8,128)(2,1)S(1)}, u32[]{:S(2)}, u32[]{:S(2)}) collective-permute-start(bf16[32,8960]{1,0:T(8,128)(2,1)S(1)} %collective-permute-done.9.refs_1_), channel_id=1, source_target_pairs={{0,1},{1,0},{2,3},{3,2},{4,5},{5,4},{6,7},{7,6},{8,9},{9,8},{10,11... | collective-permute-start | bytes 1720328 | tf_op jit(solution)/shard_map/ppermute | solution.py:218
  107.7 40.4 %collective-permute-start.30 = (bf16[64,8960]{1,0:T(8,128)(2,1)S(1)}, bf16[64,8960]{1,0:T(8,128)(2,1)S(1)}, u32[]{:S(2)}, u32[]{:S(2)}) collective-permute-start(bf16[64,8960]{1,0:T(8,128)(2,1)S(1)} %get-tuple-element.36), channel_id=1, source_target_pairs={{0,1},{1,0},{2,3},{3,2},{4,5},{5,4},{6,7},{7,6},{8,9},{9,8},{10,11... | collective-permute-start | bytes 3440648 | tf_op jit(solution)/shard_map/ppermute | solution.py:218
  107.9 26.9 %collective-permute-start.2 = (bf16[32,8960]{1,0:T(8,128)(2,1)S(1)}, bf16[32,8960]{1,0:T(8,128)(2,1)S(1)}, u32[]{:S(2)}, u32[]{:S(2)}) collective-permute-start(bf16[32,8960]{1,0:T(8,128)(2,1)S(1)} %constant_dynamic-update-slice_fusion.refs_0_), channel_id=1, source_target_pairs={{0,1},{1,0},{2,3},{3,2},{4,5},{5,4},{6,7},{7,6},{8,9},{9,8},{10,11... | collective-permute-start | bytes 1720328 | tf_op jit(solution)/shard_map/ppermute | solution.py:218
  108.3 26.6 %collective-permute-start.3 = (bf16[32,8960]{1,0:T(8,128)(2,1)S(1)}, bf16[32,8960]{1,0:T(8,128)(2,1)S(1)}, u32[]{:S(2)}, u32[]{:S(2)}) collective-permute-start(bf16[32,8960]{1,0:T(8,128)(2,1)S(1)} %collective-permute-done.1.refs_1_), channel_id=1, source_target_pairs={{0,1},{1,0},{2,3},{3,2},{4,5},{5,4},{6,7},{7,6},{8,9},{9,8},{10,11... | collective-permute-start | bytes 1720328 | tf_op jit(solution)/shard_map/ppermute | solution.py:218
  121.3 28.5 %collective-permute-start.21 = (bf16[64,8960]{1,0:T(8,128)(2,1)S(1)}, bf16[64,8960]{1,0:T(8,128)(2,1)S(1)}, u32[]{:S(2)}, u32[]{:S(2)}) collective-permute-start(bf16[64,8960]{1,0:T(8,128)(2,1)S(1)} %get-tuple-element.32), channel_id=1, source_target_pairs={{0,1},{1,0},{2,3},{3,2},{4,5},{5,4},{6,7},{7,6},{8,9},{9,8},{10,11... | collective-permute-start | bytes 3440648 | tf_op jit(solution)/shard_map/ppermute | solution.py:218
  149.9 26.5 %collective-permute-start.22 = (bf16[32,8960]{1,0:T(8,128)(2,1)S(1)}, bf16[32,8960]{1,0:T(8,128)(2,1)S(1)}, u32[]{:S(2)}, u32[]{:S(2)}) collective-permute-start(bf16[32,8960]{1,0:T(8,128)(2,1)S(1)} %add_convert_fusion.3), channel_id=1, source_target_pairs={{0,2},{1,3},{2,0},{3,1},{4,6},{5,7},{6,4},{7,5},{8,10},{9,11},{10,... | collective-permute-start | bytes 1720328 | tf_op jit(solution)/shard_map/ppermute | solution.py:215
  150.7 38.0 %collective-permute-start.13 = (bf16[32,8960]{1,0:T(8,128)(2,1)S(1)}, bf16[32,8960]{1,0:T(8,128)(2,1)S(1)}, u32[]{:S(2)}, u32[]{:S(2)}) collective-permute-start(bf16[32,8960]{1,0:T(8,128)(2,1)S(1)} %add_convert_fusion.5), channel_id=1, source_target_pairs={{0,2},{1,3},{2,0},{3,1},{4,6},{5,7},{6,4},{7,5},{8,10},{9,11},{10,... | collective-permute-start | bytes 1720328 | tf_op jit(solution)/shard_map/ppermute | solution.py:215
  152.4 47.9 %collective-permute-start.5 = (bf16[32,8960]{1,0:T(8,128)(2,1)S(1)}, bf16[32,8960]{1,0:T(8,128)(2,1)S(1)}, u32[]{:S(2)}, u32[]{:S(2)}) collective-permute-start(bf16[32,8960]{1,0:T(8,128)(2,1)S(1)} %add_convert_fusion.7), channel_id=1, source_target_pairs={{0,2},{1,3},{2,0},{3,1},{4,6},{5,7},{6,4},{7,5},{8,10},{9,11},{10,... | collective-permute-start | bytes 1720328 | tf_op jit(solution)/shard_map/ppermute | solution.py:215
  164.4 36.2 %collective-permute-start.32 = (bf16[16,8960]{1,0:T(8,128)(2,1)S(1)}, bf16[16,8960]{1,0:T(8,128)(2,1)S(1)}, u32[]{:S(2)}, u32[]{:S(2)}) collective-permute-start(bf16[16,8960]{1,0:T(8,128)(2,1)S(1)} %get-tuple-element.38), channel_id=1, source_target_pairs={{0,24},{4,28},{8,16},{12,20},{16,8},{20,12},{24,0},{28,4},{1,25},{... | collective-permute-start | bytes 860168 | tf_op jit(solution)/shard_map/ppermute | solution.py:212
  166.3 38.0 %collective-permute-start.33 = (bf16[16,8960]{1,0:T(8,128)(2,1)S(1)}, bf16[16,8960]{1,0:T(8,128)(2,1)S(1)}, u32[]{:S(2)}, u32[]{:S(2)}) collective-permute-start(bf16[16,8960]{1,0:T(8,128)(2,1)S(1)} %get-tuple-element.37), channel_id=1, source_target_pairs={{0,28},{4,24},{8,20},{12,16},{16,12},{20,8},{24,4},{28,0},{1,29},{... | collective-permute-start | bytes 860168 | tf_op jit(solution)/shard_map/ppermute | solution.py:212
  176.7 33.8 %collective-permute-start.23 = (bf16[16,8960]{1,0:T(8,128)(2,1)S(1)}, bf16[16,8960]{1,0:T(8,128)(2,1)S(1)}, u32[]{:S(2)}, u32[]{:S(2)}) collective-permute-start(bf16[16,8960]{1,0:T(8,128)(2,1)S(1)} %get-tuple-element.40), channel_id=1, source_target_pairs={{0,16},{4,20},{8,24},{12,28},{16,0},{20,4},{24,8},{28,12},{1,17},{... | collective-permute-start | bytes 860168 | tf_op jit(solution)/shard_map/ppermute | solution.py:212
  188.7 27.6 %collective-permute-start.24 = (bf16[16,8960]{1,0:T(8,128)(2,1)S(1)}, bf16[16,8960]{1,0:T(8,128)(2,1)S(1)}, u32[]{:S(2)}, u32[]{:S(2)}) collective-permute-start(bf16[16,8960]{1,0:T(8,128)(2,1)S(1)} %get-tuple-element.39), channel_id=1, source_target_pairs={{0,20},{4,16},{8,28},{12,24},{16,4},{20,0},{24,12},{28,8},{1,21},{... | collective-permute-start | bytes 860168 | tf_op jit(solution)/shard_map/ppermute | solution.py:212
  200.5 26.7 %collective-permute-start.15 = (bf16[16,8960]{1,0:T(8,128)(2,1)S(1)}, bf16[16,8960]{1,0:T(8,128)(2,1)S(1)}, u32[]{:S(2)}, u32[]{:S(2)}) collective-permute-start(bf16[16,8960]{1,0:T(8,128)(2,1)S(1)} %get-tuple-element.41), channel_id=1, source_target_pairs={{0,12},{4,8},{8,4},{12,0},{16,28},{20,24},{24,20},{28,16},{1,13},{... | collective-permute-start | bytes 860168 | tf_op jit(solution)/shard_map/ppermute | solution.py:212
  (14 other events, 215.2 us)

commit v2 on v1

--- a/solution.py
+++ b/solution.py
@@ -9,7 +9,8 @@
 
 FOLD = 4
 CHUNKS = 4
-VMEM_LIMIT = 48 * 1024 * 1024
+VMEM_LIMIT = 16 * 1024 * 1024
+EXPERT_VMEM = 16 * 1024 * 1024
 
 
 def slots_of(target_row, me, groups, main):
@@ -59,7 +60,7 @@
 
 
 def combine_kernel(groups, main, me_ref, target_ref, scale_ref, *refs):
-    back_refs, out_ref = refs[:-1], refs[-1]
+    back_refs, out_ref = refs[:-2], refs[-1]
     unit = main // FOLD
     rows = groups * main
     tok, width = out_ref.shape
@@ -95,15 +96,14 @@
 
 def expert_kernel(main, parts, gate_ref, up_ref, down_ref, *refs):
     in_refs = refs[:parts]
-    keep_ref, send_ref, rows_ref, gate_acc, up_acc, hidden_ref, tail_acc = refs[parts:]
+    keep_ref, send_ref, rows_ref = refs[parts:]
     unit = main // FOLD
-    step = pl.program_id(0)
     part_rows = in_refs[0].shape[0]
     rows = parts * part_rows
     half = rows // 2
     tail_rows = rows // FOLD
-    piece = gate_ref.shape[0]
-    width = piece * FOLD
+    width = gate_ref.shape[0]
+    piece = width // FOLD
 
     def fold_matrix(q):
         tail_id = lax.broadcasted_iota(jnp.int32, (tail_rows, rows), 0)
@@ -111,52 +111,38 @@
         wanted = (tail_id // unit) * main + q * unit + tail_id % unit
         return (wanted == folded).astype(jnp.float32).astype(jnp.bfloat16)
 
-    @pl.when(step == 0)
-    def _():
+    folded = jnp.concatenate([r[:, width:] for r in in_refs], axis=0)
+    gate_pre = up_pre = None
+    for q in range(FOLD):
+        columns = slice(q * piece, (q + 1) * piece)
         for a in range(parts):
-            for q in range(FOLD):
-                rows_ref[q, a * part_rows : (a + 1) * part_rows, :] = in_refs[a][
-                    :, q * piece : (q + 1) * piece
-                ]
-        folded = jnp.concatenate([r[:, width:] for r in in_refs], axis=0)
-        for q in range(FOLD):
-            rows_ref[q, rows:, :] = jnp.dot(
-                fold_matrix(q), folded, preferred_element_type=jnp.float32
-            ).astype(jnp.bfloat16)
-        gate_acc[...] = jnp.zeros_like(gate_acc)
-        up_acc[...] = jnp.zeros_like(up_acc)
-        tail_acc[...] = jnp.zeros_like(tail_acc)
-
-    @pl.when(step < FOLD)
-    def _():
-        block = rows_ref[step]
-        gate_acc[...] += jnp.dot(block, gate_ref[...], preferred_element_type=jnp.float32)
-        up_acc[...] += jnp.dot(block, up_ref[...], preferred_element_type=jnp.float32)
-
-    @pl.when(step == FOLD - 1)
-    def _():
-        gate_pre = gate_acc[...]
-        hidden_ref[...] = (gate_pre / (1.0 + jnp.exp(-gate_pre)) * up_acc[...]).astype(jnp.bfloat16)
-
-    @pl.when((step >= FOLD) & (step < 2 * FOLD))
-    def _():
+            rows_ref[a * part_rows : (a + 1) * part_rows, :] = in_refs[a][:, columns]
+        rows_ref[rows:, :] = jnp.dot(
+            fold_matrix(q), folded, preferred_element_type=jnp.float32
+        ).astype(jnp.bfloat16)
+        block = rows_ref[...]
+        gate_part = jnp.dot(block, gate_ref[columns, :], preferred_element_type=jnp.float32)
+        up_part = jnp.dot(block, up_ref[columns, :], preferred_element_type=jnp.float32)
+        gate_pre = gate_part if q == 0 else gate_pre + gate_part
+        up_pre = up_part if q == 0 else up_pre + up_part
+    hidden = (gate_pre / (1.0 + jnp.exp(-gate_pre)) * up_pre).astype(jnp.bfloat16)
+    tail = jnp.zeros((rows, piece), jnp.float32)
+    for q in range(FOLD):
+        columns = slice(q * piece, (q + 1) * piece)
         partial = jnp.dot(
-            hidden_ref[...], down_ref[...], preferred_element_type=jnp.float32
+            hidden, down_ref[:, columns], preferred_element_type=jnp.float32
         ).astype(jnp.bfloat16)
-        keep_ref[...] = partial[:half]
-        send_ref[...] = partial[half:rows]
-        tail_acc[...] += lax.dot_general(
-            fold_matrix(step - FOLD),
+        keep_ref[:, columns] = partial[:half]
+        send_ref[:, columns] = partial[half:rows]
+        tail += lax.dot_general(
+            fold_matrix(q),
             partial[rows:],
             (((0,), (0,)), ((), ())),
             preferred_element_type=jnp.float32,
         )
-
-    @pl.when(step == 2 * FOLD)
-    def _():
-        tail = tail_acc[...].astype(jnp.bfloat16)
-        keep_ref[...] = tail[:half]
-        send_ref[...] = tail[half:]
+    tail = tail.astype(jnp.bfloat16)
+    keep_ref[:, width:] = tail[:half]
+    send_ref[:, width:] = tail[half:]
 
 
 def run_experts(blocks, gate_mat, up_mat, down_mat, main):
@@ -167,31 +153,44 @@
     rows = parts * part_rows
     half = rows // 2
     every = rows + rows // FOLD
-    whole = pl.BlockSpec((part_rows, folded_width), lambda i: (0, 0))
-    into = pl.BlockSpec((piece, slice_width), lambda i: (jnp.minimum(i, FOLD - 1), 0))
-    out_of = pl.BlockSpec((slice_width, piece), lambda i: (0, jnp.clip(i - FOLD, 0, FOLD - 1)))
-    result = pl.BlockSpec((half, piece), lambda i: (0, jnp.maximum(i - FOLD, 0)))
+    vmem = pl.BlockSpec(memory_space=pltpu.VMEM)
     return pl.pallas_call(
         functools.partial(expert_kernel, main, parts),
-        grid=(2 * FOLD + 1,),
-        in_specs=[into, into, out_of] + [whole] * parts,
-        out_specs=[result, result],
+        in_specs=[vmem] * (3 + parts),
+        out_specs=[vmem, vmem],
         out_shape=[jax.ShapeDtypeStruct((half, folded_width), jnp.bfloat16)] * 2,
-        scratch_shapes=[
-            pltpu.VMEM((FOLD, every, piece), jnp.bfloat16),
-            pltpu.VMEM((every, slice_width), jnp.float32),
-            pltpu.VMEM((every, slice_width), jnp.float32),
-            pltpu.VMEM((every, slice_width), jnp.bfloat16),
-            pltpu.VMEM((rows, piece), jnp.float32),
-        ],
-        compiler_params=pltpu.CompilerParams(vmem_limit_bytes=VMEM_LIMIT),
+        scratch_shapes=[pltpu.VMEM((every, piece), jnp.bfloat16)],
+        compiler_params=pltpu.CompilerParams(vmem_limit_bytes=EXPERT_VMEM),
         cost_estimate=pl.CostEstimate(
             flops=6 * every * width * slice_width,
-            bytes_accessed=6 * width * slice_width + 4 * rows * folded_width,
+            bytes_accessed=4 * rows * folded_width,
             transcendentals=every * slice_width,
         ),
         name="experts",
     )(gate_mat, up_mat, down_mat, *blocks)
+
+
+def loaded(near, *weights):
+    def kernel(near_ref, *refs):
+        refs[-1][...] = jnp.zeros_like(refs[-1])
+
+    mark = pl.pallas_call(
+        kernel,
+        in_specs=[pl.BlockSpec(memory_space=pl.ANY)]
+        + [pl.BlockSpec(memory_space=pltpu.VMEM)] * len(weights),
+        out_specs=pl.BlockSpec(memory_space=pltpu.VMEM),
+        out_shape=jax.ShapeDtypeStruct((8, 128), jnp.int32),
+        compiler_params=pltpu.CompilerParams(vmem_limit_bytes=EXPERT_VMEM),
+        cost_estimate=pl.CostEstimate(
+            flops=0, bytes_accessed=sum(2 * w.size for w in weights), transcendentals=0
+        ),
+        name="loaded",
+    )(near, *weights)
+    return mark
+
+
+def together(*values):
+    return lax.optimization_barrier(values)
 
 
 def f32(x):
@@ -229,38 +228,94 @@
         compiler_params=pltpu.CompilerParams(vmem_limit_bytes=VMEM_LIMIT),
         cost_estimate=pl.CostEstimate(
             flops=4 * tok_count * tok_count * width,
-            bytes_accessed=5 * tok_count * width,
+            bytes_accessed=8 * gate_weight.size,
             transcendentals=0,
         ),
         name="dispatch",
     )(me, target_row, tokens)
 
     gate_mat, up_mat, down_mat = gate_weight[0], up_weight[0], down_weight[0]
-    back = [None] * groups
-    arrived = {}
-    for k in sorted(range(groups), key=lambda k: -k):
-        arrived[k] = to_group(outbound[k], k) if k else outbound[0]
-    for chunk in (0, 1, 3, 2):
-        offsets = range(chunk * per_chunk, (chunk + 1) * per_chunk)
-        own = jnp.concatenate([arrived[k] for k in offsets], axis=0)
-        held = [own] + [to_chip(own, c) for c in range(1, chips)]
-        held += [to_core(x) for x in held]
+
+    def offsets(chunk):
+        return range(chunk * per_chunk, (chunk + 1) * per_chunk)
+
+    def over_chips(own):
+        return [own] + [to_chip(own, c) for c in range(1, chips)]
+
+    def stack(parts):
+        return jnp.concatenate(list(parts), axis=0)
+
+    def stack_each(lists):
+        return [stack(same) for same in zip(*lists)]
+
+    def experts(held):
+        held = held + [to_core(x) for x in held]
         keep, send = run_experts(held, gate_mat, up_mat, down_mat, main)
-        got = to_core(send)
-        count = own.shape[0]
+        return keep, to_core(send)
+
+    def chip_sums(keep, got):
+        count = keep.shape[0] // chips
         mine = f32(keep[:count]) + f32(got[:count])
+        theirs = []
         for c in range(1, chips):
             rows = slice(c * count, (c + 1) * count)
-            theirs = (f32(keep[rows]) + f32(got[rows])).astype(jnp.bfloat16)
-            mine = mine + f32(to_chip(theirs, c))
-        finished = mine.astype(jnp.bfloat16)
-        for n, k in enumerate(offsets):
+            theirs.append((f32(keep[rows]) + f32(got[rows])).astype(jnp.bfloat16))
+        return mine, theirs
+
+    def reduce_chips(mine, theirs):
+        for c in range(1, chips):
+            mine = mine + f32(to_chip(theirs[c - 1], c))
+        return mine.astype(jnp.bfloat16)
+
+    back = [None] * groups
+
+    def return_chunk(chunk, finished):
+        for n, k in enumerate(offsets(chunk)):
             rows = finished[n * main : (n + 1) * main]
             back[k] = to_group(rows, k) if k else rows
 
+    arrived3 = [to_group(outbound[k], k) for k in offsets(3)]
+    first = over_chips(outbound[0])
+    near = [to_group(outbound[k], k) for k in offsets(0) if k]
+    relayed = to_group(stack([outbound[k] for k in offsets(1)]), per_chunk)
+    mark = loaded(near[-1], gate_mat, up_mat, down_mat)
+    held0 = stack_each([first] + [over_chips(x) for x in near])
+    outbound2 = [outbound[k] for k in offsets(2)]
+    held0[0], mark, relayed, *rest = together(held0[0], mark, relayed, *arrived3, *outbound2)
+    arrived3, outbound2 = rest[:per_chunk], rest[per_chunk:]
+    keep0, got0 = experts(held0)
+    arrived2 = [to_group(x, k) for x, k in zip(outbound2, offsets(2))]
+    held3 = over_chips(stack(arrived3))
+    arrived1 = [
+        to_group(relayed[n * main : (n + 1) * main], n) if n else relayed[:main]
+        for n in range(per_chunk)
+    ]
+    arrived1[-1], keep0 = together(arrived1[-1], keep0)
+    held1 = stack_each([over_chips(x) for x in arrived1])
+    held3[-1], held1[-1], *arrived2 = together(held3[-1], held1[-1], *arrived2)
+    held2 = over_chips(stack(arrived2))
+    keep3, got3 = experts(held3)
+    mine3, theirs3 = chip_sums(keep3, got3)
+    keep1, got1 = experts(held1)
+    held2[-1], keep1, *theirs3 = together(held2[-1], keep1, *theirs3)
+    keep2, got2 = experts(held2)
+    finished3 = reduce_chips(mine3, theirs3)
+    mine2, theirs2 = chip_sums(keep2, got2)
+    mine1, theirs1 = chip_sums(keep1, got1)
+    mine0, theirs0 = chip_sums(keep0, got0)
+    finished3, *theirs1 = together(finished3, *theirs1)
+    return_chunk(3, finished3)
+    finished2 = reduce_chips(mine2, theirs2)
+    finished1 = reduce_chips(mine1, theirs1)
+    finished2, *theirs0 = together(finished2, *theirs0)
+    return_chunk(2, finished2)
+    return_chunk(1, finished1)
+    finished0 = reduce_chips(mine0, theirs0)
+    return_chunk(0, finished0)
+
     return pl.pallas_call(
         functools.partial(combine_kernel, groups, main),
-        in_specs=[scalar] + [vmem] * (2 + groups),
+        in_specs=[scalar] + [vmem] * (2 + groups) + [pl.BlockSpec(memory_space=pl.ANY)],
         out_specs=vmem,
         out_shape=jax.ShapeDtypeStruct((tok_count, width), jnp.bfloat16),
         compiler_params=pltpu.CompilerParams(vmem_limit_bytes=VMEM_LIMIT),
@@ -270,7 +325,7 @@
             transcendentals=0,
         ),
         name="combine",
-    )(me, target_row, gate_scale.reshape(1, tok_count), *back)
+    )(me, target_row, gate_scale.reshape(1, tok_count), *back, mark)
 
 
 def solution(mesh):

time: 230 us -> 171 us (0.74)
  Pallas kernels: 55.2 us -> 22.9 us
  starting transfers between devices: 59.1 us -> 37 us
  waiting for transfers between devices: 111 us -> 97 us
  local copies, waits for them, and re-layouts: 2.48 us -> 11.7 us
    pallas_call x4 -> x5, Pallas kernels: 51.4 us -> 19.1 us  [the longest x4 19.1 us: run_experts(): pl.pallas_call(functools.partial(expert_kernel, main, parts), in_specs=[v...]
    ppermute x14, starting transfers between devices: 46.9 us -> 22.9 us  [to_group(): return lax.ppermute(x, 'group', [(i, i ^ offset) for i in range(groups)])]
    unnamed x12 -> x17, local copies, waits for them, and re-layouts: 2.24 us -> 11.5 us
    ppermute x14, waiting for transfers between devices: 42.4 us -> 34.2 us  [to_group(): return lax.ppermute(x, 'group', [(i, i ^ offset) for i in range(groups)])]
    ppermute x8 -> x10, waiting for transfers between devices: 69 us -> 61.5 us  [to_chip(): return lax.ppermute(x, 'inner', [(i, i ^ 2 * offset) for i in range(inner)])]
    ppermute x8 -> x10, starting transfers between devices: 9.52 us -> 11.6 us  [to_chip(): return lax.ppermute(x, 'inner', [(i, i ^ 2 * offset) for i in range(inner)])]
  transfers between devices with their start and end apart: 34 -> 36, of which waited for: 14 -> 15; matrix products, arithmetic and copies ran while one was open for 1% -> 1% of each run, Pallas kernels for 22% -> 11%
where the time goes in v2:
time: 171 us; the launch traced here: 170 us
  waiting for transfers between devices  97 us (57%)
  starting transfers between devices  37 us (22%)
  Pallas kernels  22.9 us (13%)
  local copies, waits for them, and re-layouts  11.7 us (7%)
    ppermute x10, waiting for transfers between devices, to_chip(): return lax.ppermute(x, 'inner', [(i, i ^ 2 * offset) for i in range(inner)])  61.5 us
    ppermute x14, waiting for transfers between devices, to_group(): return lax.ppermute(x, 'group', [(i, i ^ offset) for i in range(groups)])  34.2 us
    ppermute x14, starting transfers between devices, to_group(): return lax.ppermute(x, 'group', [(i, i ^ offset) for i in range(groups)])  22.9 us
    pallas_call x4, Pallas kernels, run_experts(): pl.pallas_call(functools.partial(expert_kernel, main, parts), in_specs=[v...  19.1 us
    ppermute x10, starting transfers between devices, to_chip(): return lax.ppermute(x, 'inner', [(i, i ^ 2 * offset) for i in range(inner)])  11.6 us
    unnamed x17, local copies, waits for them, and re-layouts  11.5 us
  transfers between devices with their start and end apart: 36, of which 15 were waited for; matrix products, arithmetic and copies ran while one was open for 1% of the time, Pallas kernels for 11%

profile of v2, /device:TPU:0, one launch (start us, length us, event | category | flops | bytes accessed | tf_op | source)
XLA Modules:
  0.0 170.4 jit_solution(5822666130301802765)
XLA Ops:
  3.4 3.0 %collective-permute-start = (bf16[16,8960]{1,0:T(8,128)(2,1)S(1)}, bf16[16,8960]{1,0:T(8,128)(2,1)S(1)}, u32[]{:S(2)}, u32[]{:S(2)}) collective-permute-start(bf16[16,8960]{1,0:T(8,128)(2,1)S(1)} %get-tuple-element.42), channel_id=1, source_target_pairs={{0,4},{4,0},{8,12},{12,8},{16,20},{20,16},{24,28},{28,24},{1,5},{5... | collective-permute-start | bytes 860168 | tf_op jit(solution)/shard_map/ppermute | solution.py:211
  8.1 2.5 %collective-permute-start.2 = (bf16[16,8960]{1,0:T(8,128)(2,1)S(1)}, bf16[16,8960]{1,0:T(8,128)(2,1)S(1)}, u32[]{:S(2)}, u32[]{:S(2)}) collective-permute-start(bf16[16,8960]{1,0:T(8,128)(2,1)S(1)} %get-tuple-element.45), channel_id=1, source_target_pairs={{0,24},{4,28},{8,16},{12,20},{16,8},{20,12},{24,0},{28,4},{1,25},{... | collective-permute-start | bytes 860168 | tf_op jit(solution)/shard_map/ppermute | solution.py:211
  15.1 6.6 %collective-permute-done.5 = bf16[16,8960]{1,0:T(8,128)(2,1)S(1)} collective-permute-done((bf16[16,8960]{1,0:T(8,128)(2,1)S(1)}, bf16[16,8960]{1,0:T(8,128)(2,1)S(1)}, u32[]{:S(2)}, u32[]{:S(2)}) %collective-permute-start.5) | collective-permute-done | bytes 286752 | tf_op jit(solution)/shard_map/ppermute | solution.py:214
  21.7 3.1 %copy-done = bf16[1,7168,512]{2,1,0:T(8,128)(2,1)S(1)} copy-done((bf16[1,7168,512]{2,1,0:T(8,128)(2,1)S(1)}, bf16[1,7168,512]{2,1,0:T(8,128)(2,1)}, u32[]{:S(2)}) %copy-start) | copy-done | bytes 7340056
  24.8 3.1 %copy-done.1 = bf16[1,7168,512]{2,1,0:T(8,128)(2,1)S(1)} copy-done((bf16[1,7168,512]{2,1,0:T(8,128)(2,1)S(1)}, bf16[1,7168,512]{2,1,0:T(8,128)(2,1)}, u32[]{:S(2)}) %copy-start.1) | copy-done | bytes 7340056
  27.9 3.1 %copy-done.2 = bf16[1,512,7168]{2,1,0:T(8,128)(2,1)S(1)} copy-done((bf16[1,512,7168]{2,1,0:T(8,128)(2,1)S(1)}, bf16[1,512,7168]{2,1,0:T(8,128)(2,1)}, u32[]{:S(2)}) %copy-start.2) | copy-done | bytes 7340056
  31.0 4.4 %collective-permute-done.3 = bf16[16,8960]{1,0:T(8,128)(2,1)S(1)} collective-permute-done((bf16[16,8960]{1,0:T(8,128)(2,1)S(1)}, bf16[16,8960]{1,0:T(8,128)(2,1)S(1)}, u32[]{:S(2)}, u32[]{:S(2)}) %collective-permute-start.3) | collective-permute-done | bytes 286752 | tf_op jit(solution)/shard_map/ppermute | solution.py:211
  42.3 4.7 %experts.4 = (bf16[64,8960]{1,0:T(8,128)(2,1)S(1)}, bf16[64,8960]{1,0:T(8,128)(2,1)S(1)}) custom-call(bf16[7168,512]{1,0:T(8,128)(2,1)S(1)} %bitcast.7, bf16[7168,512]{1,0:T(8,128)(2,1)S(1)} %bitcast.12, bf16[512,7168]{1,0:T(8,128)(2,1)S(1)} %bitcast.17, bf16[32,8960]{1,0:T(8,128)(2,1)S(1)} %pad_maximum_fusion.refs_0_, ...), custom_call_target="tpu_custom_call" | custom-call | flops 3523215360 | bytes 4587520 | tf_op jit(solution)/shard_map/experts/pallas_call | solution.py:157
  48.4 9.1 %collective-permute-done.11 = bf16[16,8960]{1,0:T(8,128)(2,1)S(1)} collective-permute-done((bf16[16,8960]{1,0:T(8,128)(2,1)S(1)}, bf16[16,8960]{1,0:T(8,128)(2,1)S(1)}, u32[]{:S(2)}, u32[]{:S(2)}) %collective-permute-start.11) | collective-permute-done | bytes 286752 | tf_op jit(solution)/shard_map/ppermute | solution.py:214
  57.5 3.7 %collective-permute-done.12 = bf16[16,8960]{1,0:T(8,128)(2,1)S(1)} collective-permute-done((bf16[16,8960]{1,0:T(8,128)(2,1)S(1)}, bf16[16,8960]{1,0:T(8,128)(2,1)S(1)}, u32[]{:S(2)}, u32[]{:S(2)}) %collective-permute-start.12) | collective-permute-done | bytes 286752 | tf_op jit(solution)/shard_map/ppermute | solution.py:214
  61.9 7.9 %collective-permute-done.14 = bf16[16,8960]{1,0:T(8,128)(2,1)S(1)} collective-permute-done((bf16[16,8960]{1,0:T(8,128)(2,1)S(1)}, bf16[16,8960]{1,0:T(8,128)(2,1)S(1)}, u32[]{:S(2)}, u32[]{:S(2)}) %collective-permute-start.14) | collective-permute-done | bytes 286752 | tf_op jit(solution)/shard_map/ppermute | solution.py:211
  71.9 4.7 %experts.6 = (bf16[64,8960]{1,0:T(8,128)(2,1)S(1)}, bf16[64,8960]{1,0:T(8,128)(2,1)S(1)}) custom-call(bf16[7168,512]{1,0:T(8,128)(2,1)S(1)} %bitcast.8, bf16[7168,512]{1,0:T(8,128)(2,1)S(1)} %bitcast.13, bf16[512,7168]{1,0:T(8,128)(2,1)S(1)} %bitcast.18, bf16[32,8960]{1,0:T(8,128)(2,1)S(1)} %constant_dynamic-update-slice_fusion.2.refs_0_, ...), custom_call_target="tpu_custom_call" | custom-call | flops 3523215360 | bytes 4587520 | tf_op jit(solution)/shard_map/experts/pallas_call | solution.py:157
  77.1 4.9 %experts.5 = (bf16[64,8960]{1,0:T(8,128)(2,1)S(1)}, bf16[64,8960]{1,0:T(8,128)(2,1)S(1)}) custom-call(bf16[7168,512]{1,0:T(8,128)(2,1)S(1)} %bitcast.9, bf16[7168,512]{1,0:T(8,128)(2,1)S(1)} %bitcast.14, bf16[512,7168]{1,0:T(8,128)(2,1)S(1)} %bitcast.19, bf16[32,8960]{1,0:T(8,128)(2,1)S(1)} %pad_maximum_fusion.3.refs_0_, ...), custom_call_target="tpu_custom_call" | custom-call | flops 3523215360 | bytes 4587520 | tf_op jit(solution)/shard_map/experts/pallas_call | solution.py:157
  82.5 2.8 %collective-permute-done.15.refs_1_ = bf16[32,8960]{1,0:T(8,128)(2,1)S(1)} collective-permute-done((bf16[32,8960]{1,0:T(8,128)(2,1)S(1)}, bf16[32,8960]{1,0:T(8,128)(2,1)S(1)}, u32[]{:S(2)}, u32[]{:S(2)}) %collective-permute-start.15) | collective-permute-done | bytes 573472 | tf_op jit(solution)/shard_map/ppermute | solution.py:214
  86.4 13.0 %collective-permute-done.28 = bf16[32,8960]{1,0:T(8,128)(2,1)S(1)} collective-permute-done((bf16[32,8960]{1,0:T(8,128)(2,1)S(1)}, bf16[32,8960]{1,0:T(8,128)(2,1)S(1)}, u32[]{:S(2)}, u32[]{:S(2)}) %collective-permute-start.28) | collective-permute-done | bytes 573472 | tf_op jit(solution)/shard_map/ppermute | solution.py:214
  102.1 2.3 %collective-permute-start.35 = (bf16[16,8960]{1,0:T(8,128)(2,1)S(1)}, bf16[16,8960]{1,0:T(8,128)(2,1)S(1)}, u32[]{:S(2)}, u32[]{:S(2)}) collective-permute-start(bf16[16,8960]{1,0:T(8,128)(2,1)S(1)} %get-tuple-element.77), channel_id=1, source_target_pairs={{0,28},{4,24},{8,20},{12,16},{16,12},{20,8},{24,4},{28,0},{1,29},{... | collective-permute-start | bytes 860168 | tf_op jit(solution)/shard_map/ppermute | solution.py:211
  104.4 4.7 %experts.7 = (bf16[64,8960]{1,0:T(8,128)(2,1)S(1)}, bf16[64,8960]{1,0:T(8,128)(2,1)S(1)}) custom-call(bf16[7168,512]{1,0:T(8,128)(2,1)S(1)} %bitcast.10, bf16[7168,512]{1,0:T(8,128)(2,1)S(1)} %bitcast.15, bf16[512,7168]{1,0:T(8,128)(2,1)S(1)} %bitcast.20, bf16[32,8960]{1,0:T(8,128)(2,1)S(1)} %constant_dynamic-update-slice_fusion.4.refs_0_, ...), custom_call_target="tpu_custom_call" | custom-call | flops 3523215360 | bytes 4587520 | tf_op jit(solution)/shard_map/experts/pallas_call | solution.py:157
  109.2 3.5 %collective-permute-done.29 = bf16[32,8960]{1,0:T(8,128)(2,1)S(1)} collective-permute-done((bf16[32,8960]{1,0:T(8,128)(2,1)S(1)}, bf16[32,8960]{1,0:T(8,128)(2,1)S(1)}, u32[]{:S(2)}, u32[]{:S(2)}) %collective-permute-start.29) | collective-permute-done | bytes 573472 | tf_op jit(solution)/shard_map/ppermute | solution.py:214
  116.4 10.8 %collective-permute-done.24 = bf16[32,8960]{1,0:T(8,128)(2,1)S(1)} collective-permute-done((bf16[32,8960]{1,0:T(8,128)(2,1)S(1)}, bf16[32,8960]{1,0:T(8,128)(2,1)S(1)}, u32[]{:S(2)}, u32[]{:S(2)}) %collective-permute-start.24) | collective-permute-done | bytes 573472 | tf_op jit(solution)/shard_map/ppermute | solution.py:214
  128.7 12.0 %collective-permute-done.25 = bf16[32,8960]{1,0:T(8,128)(2,1)S(1)} collective-permute-done((bf16[32,8960]{1,0:T(8,128)(2,1)S(1)}, bf16[32,8960]{1,0:T(8,128)(2,1)S(1)}, u32[]{:S(2)}, u32[]{:S(2)}) %collective-permute-start.25) | collective-permute-done | bytes 573472 | tf_op jit(solution)/shard_map/ppermute | solution.py:214
  141.0 5.0 %collective-permute-start.33 = (bf16[16,8960]{1,0:T(8,128)(2,1)S(1)}, bf16[16,8960]{1,0:T(8,128)(2,1)S(1)}, u32[]{:S(2)}, u32[]{:S(2)}) collective-permute-start(bf16[16,8960]{1,0:T(8,128)(2,1)S(1)} %get-tuple-element.79), channel_id=1, source_target_pairs={{0,20},{4,16},{8,28},{12,24},{16,4},{20,0},{24,12},{28,8},{1,21},{... | collective-permute-start | bytes 860168 | tf_op jit(solution)/shard_map/ppermute | solution.py:211
  146.0 13.3 %collective-permute-done.32.refs_4_ = bf16[16,8960]{1,0:T(8,128)(2,1)S(1)} collective-permute-done((bf16[16,8960]{1,0:T(8,128)(2,1)S(1)}, bf16[16,8960]{1,0:T(8,128)(2,1)S(1)}, u32[]{:S(2)}, u32[]{:S(2)}) %collective-permute-start.32) | collective-permute-done | bytes 286752 | tf_op jit(solution)/shard_map/ppermute | solution.py:211
  159.2 8.6 %collective-permute-done.33.refs_5_ = bf16[16,8960]{1,0:T(8,128)(2,1)S(1)} collective-permute-done((bf16[16,8960]{1,0:T(8,128)(2,1)S(1)}, bf16[16,8960]{1,0:T(8,128)(2,1)S(1)}, u32[]{:S(2)}, u32[]{:S(2)}) %collective-permute-start.33) | collective-permute-done | bytes 286752 | tf_op jit(solution)/shard_map/ppermute | solution.py:211
  167.9 2.5 %combine.1 = bf16[128,7168]{1,0:T(8,128)(2,1)} custom-call(s32[1]{0:T(128)} %bitcast.me_ref, s32[1,128]{1,0:T(1,128)S(1)} %bitcast.22, f32[1,128]{1,0:T(1,128)S(1)} %bitcast.23, bf16[16,8960]{1,0:T(8,128)(2,1)S(1)} %get-tuple-element.84.refs_0_, bf16[16,8960]{1,0:T(8,128)(2,1)S(1)} %collective-permute-done.26.refs_1_, ...), custom_call_target="tpu_custom_call" | custom-call | flops 469762048 | bytes 4587520 | tf_op jit(solution)/shard_map/combine/pallas_call | solution.py:316
  (92 shorter events, 30.8 us)
Async XLA Ops:
  6.5 28.9 %collective-permute-start.1 = (bf16[32,8960]{1,0:T(8,128)(2,1)S(1)}, bf16[32,8960]{1,0:T(8,128)(2,1)S(1)}, u32[]{:S(2)}, u32[]{:S(2)}) collective-permute-start(bf16[32,8960]{1,0:T(8,128)(2,1)S(1)} %pad_maximum_fusion.1), channel_id=1, source_target_pairs={{0,8},{4,12},{8,0},{12,4},{16,24},{20,28},{24,16},{28,20},{1,9},{5... | collective-permute-start | bytes 1720328 | tf_op jit(solution)/shard_map/ppermute | solution.py:211
  8.1 22.8 %collective-permute-start.2 = (bf16[16,8960]{1,0:T(8,128)(2,1)S(1)}, bf16[16,8960]{1,0:T(8,128)(2,1)S(1)}, u32[]{:S(2)}, u32[]{:S(2)}) collective-permute-start(bf16[16,8960]{1,0:T(8,128)(2,1)S(1)} %get-tuple-element.45), channel_id=1, source_target_pairs={{0,24},{4,28},{8,16},{12,20},{16,8},{20,12},{24,0},{28,4},{1,25},{... | collective-permute-start | bytes 860168 | tf_op jit(solution)/shard_map/ppermute | solution.py:211
  10.6 24.7 %collective-permute-start.3 = (bf16[16,8960]{1,0:T(8,128)(2,1)S(1)}, bf16[16,8960]{1,0:T(8,128)(2,1)S(1)}, u32[]{:S(2)}, u32[]{:S(2)}) collective-permute-start(bf16[16,8960]{1,0:T(8,128)(2,1)S(1)} %get-tuple-element.46), channel_id=1, source_target_pairs={{0,28},{4,24},{8,20},{12,16},{16,12},{20,8},{24,4},{28,0},{1,29},{... | collective-permute-start | bytes 860168 | tf_op jit(solution)/shard_map/ppermute | solution.py:211
  13.4 24.0 %collective-permute-start.6 = (bf16[16,8960]{1,0:T(8,128)(2,1)S(1)}, bf16[16,8960]{1,0:T(8,128)(2,1)S(1)}, u32[]{:S(2)}, u32[]{:S(2)}) collective-permute-start(bf16[16,8960]{1,0:T(8,128)(2,1)S(1)} %collective-permute-done.near_ref), channel_id=1, source_target_pairs={{0,2},{1,3},{2,0},{3,1},{4,6},{5,7},{6,4},{7,5},{8,10},{9,11},{10,... | collective-permute-start | bytes 860168 | tf_op jit(solution)/shard_map/ppermute | solution.py:214
  35.4 34.4 %collective-permute-start.10 = (bf16[32,8960]{1,0:T(8,128)(2,1)S(1)}, bf16[32,8960]{1,0:T(8,128)(2,1)S(1)}, u32[]{:S(2)}, u32[]{:S(2)}) collective-permute-start(bf16[32,8960]{1,0:T(8,128)(2,1)S(1)} %constant_dynamic-update-slice_fusion.2.refs_0_), channel_id=1, source_target_pairs={{0,2},{1,3},{2,0},{3,1},{4,6},{5,7},{6,4},{7,5},{8,10},{9,11},{10,... | collective-permute-start | bytes 1720328 | tf_op jit(solution)/shard_map/ppermute | solution.py:214
  37.0 33.4 %collective-permute-start.18 = (bf16[32,8960]{1,0:T(8,128)(2,1)S(1)}, bf16[32,8960]{1,0:T(8,128)(2,1)S(1)}, u32[]{:S(2)}, u32[]{:S(2)}) collective-permute-start(bf16[32,8960]{1,0:T(8,128)(2,1)S(1)} %constant_dynamic-update-slice_fusion.2.refs_0_), channel_id=1, source_target_pairs={{0,1},{1,0},{2,3},{3,2},{4,5},{5,4},{6,7},{7,6},{8,9},{9,8},{10,11... | collective-permute-start | bytes 1720328 | tf_op jit(solution)/shard_map/ppermute | solution.py:217
  39.8 17.8 %collective-permute-start.11 = (bf16[16,8960]{1,0:T(8,128)(2,1)S(1)}, bf16[16,8960]{1,0:T(8,128)(2,1)S(1)}, u32[]{:S(2)}, u32[]{:S(2)}) collective-permute-start(bf16[16,8960]{1,0:T(8,128)(2,1)S(1)} %get-tuple-element.85), channel_id=1, source_target_pairs={{0,2},{1,3},{2,0},{3,1},{4,6},{5,7},{6,4},{7,5},{8,10},{9,11},{10,... | collective-permute-start | bytes 860168 | tf_op jit(solution)/shard_map/ppermute | solution.py:214
  40.6 20.7 %collective-permute-start.13 = (bf16[16,8960]{1,0:T(8,128)(2,1)S(1)}, bf16[16,8960]{1,0:T(8,128)(2,1)S(1)}, u32[]{:S(2)}, u32[]{:S(2)}) collective-permute-start(bf16[16,8960]{1,0:T(8,128)(2,1)S(1)} %get-tuple-element.57), channel_id=1, source_target_pairs={{0,16},{4,20},{8,24},{12,28},{16,0},{20,4},{24,8},{28,12},{1,17},{... | collective-permute-start | bytes 860168 | tf_op jit(solution)/shard_map/ppermute | solution.py:211
  47.1 14.1 %collective-permute-start.12 = (bf16[16,8960]{1,0:T(8,128)(2,1)S(1)}, bf16[16,8960]{1,0:T(8,128)(2,1)S(1)}, u32[]{:S(2)}, u32[]{:S(2)}) collective-permute-start(bf16[16,8960]{1,0:T(8,128)(2,1)S(1)} %collective-permute-done.4), channel_id=1, source_target_pairs={{0,2},{1,3},{2,0},{3,1},{4,6},{5,7},{6,4},{7,5},{8,10},{9,11},{10,... | collective-permute-start | bytes 860168 | tf_op jit(solution)/shard_map/ppermute | solution.py:214
  61.2 15.4 %collective-permute-start.16 = (bf16[32,8960]{1,0:T(8,128)(2,1)S(1)}, bf16[32,8960]{1,0:T(8,128)(2,1)S(1)}, u32[]{:S(2)}, u32[]{:S(2)}) collective-permute-start(bf16[32,8960]{1,0:T(8,128)(2,1)S(1)} %pad_maximum_fusion.3.refs_0_), channel_id=1, source_target_pairs={{0,1},{1,0},{2,3},{3,2},{4,5},{5,4},{6,7},{7,6},{8,9},{9,8},{10,11... | collective-permute-start | bytes 1720328 | tf_op jit(solution)/shard_map/ppermute | solution.py:217
  61.3 20.9 %collective-permute-start.9 = (bf16[64,8960]{1,0:T(8,128)(2,1)S(1)}, bf16[64,8960]{1,0:T(8,128)(2,1)S(1)}, u32[]{:S(2)}, u32[]{:S(2)}) collective-permute-start(bf16[64,8960]{1,0:T(8,128)(2,1)S(1)} %get-tuple-element.53), channel_id=1, source_target_pairs={{0,1},{1,0},{2,3},{3,2},{4,5},{5,4},{6,7},{7,6},{8,9},{9,8},{10,11... | collective-permute-start | bytes 3440648 | tf_op jit(solution)/shard_map/ppermute | solution.py:217
  70.3 15.0 %collective-permute-start.15 = (bf16[32,8960]{1,0:T(8,128)(2,1)S(1)}, bf16[32,8960]{1,0:T(8,128)(2,1)S(1)}, u32[]{:S(2)}, u32[]{:S(2)}) collective-permute-start(bf16[32,8960]{1,0:T(8,128)(2,1)S(1)} %constant_dynamic-update-slice_fusion.4.refs_0_), channel_id=1, source_target_pairs={{0,2},{1,3},{2,0},{3,1},{4,6},{5,7},{6,4},{7,5},{8,10},{9,11},{10,... | collective-permute-start | bytes 1720328 | tf_op jit(solution)/shard_map/ppermute | solution.py:214
  71.7 32.7 %collective-permute-start.21 = (bf16[32,8960]{1,0:T(8,128)(2,1)S(1)}, bf16[32,8960]{1,0:T(8,128)(2,1)S(1)}, u32[]{:S(2)}, u32[]{:S(2)}) collective-permute-start(bf16[32,8960]{1,0:T(8,128)(2,1)S(1)} %constant_dynamic-update-slice_fusion.4.refs_0_), channel_id=1, source_target_pairs={{0,1},{1,0},{2,3},{3,2},{4,5},{5,4},{6,7},{7,6},{8,9},{9,8},{10,11... | collective-permute-start | bytes 1720328 | tf_op jit(solution)/shard_map/ppermute | solution.py:217
  85.3 14.0 %collective-permute-start.28 = (bf16[32,8960]{1,0:T(8,128)(2,1)S(1)}, bf16[32,8960]{1,0:T(8,128)(2,1)S(1)}, u32[]{:S(2)}, u32[]{:S(2)}) collective-permute-start(bf16[32,8960]{1,0:T(8,128)(2,1)S(1)} %add_convert_fusion.7), channel_id=1, source_target_pairs={{0,2},{1,3},{2,0},{3,1},{4,6},{5,7},{6,4},{7,5},{8,10},{9,11},{10,... | collective-permute-start | bytes 1720328 | tf_op jit(solution)/shard_map/ppermute | solution.py:214
  86.2 18.2 %collective-permute-start.22 = (bf16[32,8960]{1,0:T(8,128)(2,1)S(1)}, bf16[32,8960]{1,0:T(8,128)(2,1)S(1)}, u32[]{:S(2)}, u32[]{:S(2)}) collective-permute-start(bf16[32,8960]{1,0:T(8,128)(2,1)S(1)} %collective-permute-done.15.refs_1_), channel_id=1, source_target_pairs={{0,1},{1,0},{2,3},{3,2},{4,5},{5,4},{6,7},{7,6},{8,9},{9,8},{10,11... | collective-permute-start | bytes 1720328 | tf_op jit(solution)/shard_map/ppermute | solution.py:217
  100.6 40.4 %collective-permute-start.34 = (bf16[16,8960]{1,0:T(8,128)(2,1)S(1)}, bf16[16,8960]{1,0:T(8,128)(2,1)S(1)}, u32[]{:S(2)}, u32[]{:S(2)}) collective-permute-start(bf16[16,8960]{1,0:T(8,128)(2,1)S(1)} %get-tuple-element.78), channel_id=1, source_target_pairs={{0,24},{4,28},{8,16},{12,20},{16,8},{20,12},{24,0},{28,4},{1,25},{... | collective-permute-start | bytes 860168 | tf_op jit(solution)/shard_map/ppermute | solution.py:211
  102.1 43.9 %collective-permute-start.35 = (bf16[16,8960]{1,0:T(8,128)(2,1)S(1)}, bf16[16,8960]{1,0:T(8,128)(2,1)S(1)}, u32[]{:S(2)}, u32[]{:S(2)}) collective-permute-start(bf16[16,8960]{1,0:T(8,128)(2,1)S(1)} %get-tuple-element.77), channel_id=1, source_target_pairs={{0,28},{4,24},{8,20},{12,16},{16,12},{20,8},{24,4},{28,0},{1,29},{... | collective-permute-start | bytes 860168 | tf_op jit(solution)/shard_map/ppermute | solution.py:211
  113.1 14.2 %collective-permute-start.24 = (bf16[32,8960]{1,0:T(8,128)(2,1)S(1)}, bf16[32,8960]{1,0:T(8,128)(2,1)S(1)}, u32[]{:S(2)}, u32[]{:S(2)}) collective-permute-start(bf16[32,8960]{1,0:T(8,128)(2,1)S(1)} %add_convert_fusion.6), channel_id=1, source_target_pairs={{0,2},{1,3},{2,0},{3,1},{4,6},{5,7},{6,4},{7,5},{8,10},{9,11},{10,... | collective-permute-start | bytes 1720328 | tf_op jit(solution)/shard_map/ppermute | solution.py:214
  114.1 31.8 %collective-permute-start.30 = (bf16[16,8960]{1,0:T(8,128)(2,1)S(1)}, bf16[16,8960]{1,0:T(8,128)(2,1)S(1)}, u32[]{:S(2)}, u32[]{:S(2)}) collective-permute-start(bf16[16,8960]{1,0:T(8,128)(2,1)S(1)} %get-tuple-element.82), channel_id=1, source_target_pairs={{0,8},{4,12},{8,0},{12,4},{16,24},{20,28},{24,16},{28,20},{1,9},{5... | collective-permute-start | bytes 860168 | tf_op jit(solution)/shard_map/ppermute | solution.py:211
  114.2 31.8 %collective-permute-start.31 = (bf16[16,8960]{1,0:T(8,128)(2,1)S(1)}, bf16[16,8960]{1,0:T(8,128)(2,1)S(1)}, u32[]{:S(2)}, u32[]{:S(2)}) collective-permute-start(bf16[16,8960]{1,0:T(8,128)(2,1)S(1)} %get-tuple-element.81), channel_id=1, source_target_pairs={{0,12},{4,8},{8,4},{12,0},{16,28},{20,24},{24,20},{28,16},{1,13},{... | collective-permute-start | bytes 860168 | tf_op jit(solution)/shard_map/ppermute | solution.py:211
  127.4 13.2 %collective-permute-start.25 = (bf16[32,8960]{1,0:T(8,128)(2,1)S(1)}, bf16[32,8960]{1,0:T(8,128)(2,1)S(1)}, u32[]{:S(2)}, u32[]{:S(2)}) collective-permute-start(bf16[32,8960]{1,0:T(8,128)(2,1)S(1)} %add_convert_fusion.4), channel_id=1, source_target_pairs={{0,2},{1,3},{2,0},{3,1},{4,6},{5,7},{6,4},{7,5},{8,10},{9,11},{10,... | collective-permute-start | bytes 1720328 | tf_op jit(solution)/shard_map/ppermute | solution.py:214
  140.7 18.6 %collective-permute-start.32 = (bf16[16,8960]{1,0:T(8,128)(2,1)S(1)}, bf16[16,8960]{1,0:T(8,128)(2,1)S(1)}, u32[]{:S(2)}, u32[]{:S(2)}) collective-permute-start(bf16[16,8960]{1,0:T(8,128)(2,1)S(1)} %get-tuple-element.80), channel_id=1, source_target_pairs={{0,16},{4,20},{8,24},{12,28},{16,0},{20,4},{24,8},{28,12},{1,17},{... | collective-permute-start | bytes 860168 | tf_op jit(solution)/shard_map/ppermute | solution.py:211
  141.0 26.9 %collective-permute-start.33 = (bf16[16,8960]{1,0:T(8,128)(2,1)S(1)}, bf16[16,8960]{1,0:T(8,128)(2,1)S(1)}, u32[]{:S(2)}, u32[]{:S(2)}) collective-permute-start(bf16[16,8960]{1,0:T(8,128)(2,1)S(1)} %get-tuple-element.79), channel_id=1, source_target_pairs={{0,20},{4,16},{8,28},{12,24},{16,4},{20,0},{24,12},{28,8},{1,21},{... | collective-permute-start | bytes 860168 | tf_op jit(solution)/shard_map/ppermute | solution.py:211
  145.9 21.9 %collective-permute-start.26 = (bf16[16,8960]{1,0:T(8,128)(2,1)S(1)}, bf16[16,8960]{1,0:T(8,128)(2,1)S(1)}, u32[]{:S(2)}, u32[]{:S(2)}) collective-permute-start(bf16[16,8960]{1,0:T(8,128)(2,1)S(1)} %get-tuple-element.83), channel_id=1, source_target_pairs={{0,4},{4,0},{8,12},{12,8},{16,20},{20,16},{24,28},{28,24},{1,5},{5... | collective-permute-start | bytes 860168 | tf_op jit(solution)/shard_map/ppermute | solution.py:211
  (19 other events, 148.9 us)

commit v3 on v2

--- a/solution.py
+++ b/solution.py
@@ -11,6 +11,15 @@
 CHUNKS = 4
 VMEM_LIMIT = 16 * 1024 * 1024
 EXPERT_VMEM = 16 * 1024 * 1024
+
+
+ORDER = (
+    "S.g30 S.y0 S.x00 S.g1 S.g31 L.g D.y0 S.x01 S.y2 L.u D.x00 D.x01 S.c0 S.c0x L.d D.y2 D.c0 D.c0x "
+    "D.g30 D.g31 D.g1 S.g2 S.x31 S.y1 S.x30 S.x10 D.x30 E.0 S.b0 S.c3 D.x31 D.y1 S.c3x S.x11 D.b0 D.x10 "
+    "D.c3 D.c3x E.3 S.b3 D.x11 S.c1 S.c1x D.g2 S.x2 D.c1x D.b3 D.c1 S.c2 S.r3 E.1 S.b1 D.c2 D.b1 D.x2 "
+    "S.c2x D.c2x E.2 S.b2 D.r3 D.b2 S.h30 S.h31 S.r1 S.r2 D.r1 S.r0 D.h31 S.h1 D.r2 S.h20 S.h21 D.r0 "
+    "S.h0 D.h30 D.h1 D.h20 D.h21 D.h0"
+).split()
 
 
 def slots_of(target_row, me, groups, main):
@@ -57,6 +66,7 @@
         )
     for k in range(groups):
         out_refs[k][:, width:] = tail[k * main : (k + 1) * main].astype(jnp.bfloat16)
+    out_refs[groups][...] = jnp.zeros_like(out_refs[groups])
 
 
 def combine_kernel(groups, main, me_ref, target_ref, scale_ref, *refs):
@@ -170,23 +180,22 @@
     )(gate_mat, up_mat, down_mat, *blocks)
 
 
-def loaded(near, *weights):
-    def kernel(near_ref, *refs):
-        refs[-1][...] = jnp.zeros_like(refs[-1])
-
-    mark = pl.pallas_call(
+def loaded(mark, weight):
+    def kernel(mark_ref, weight_ref, out_ref):
+        out_ref[...] = mark_ref[...]
+
+    vmem = pl.BlockSpec(memory_space=pltpu.VMEM)
+    return pl.pallas_call(
         kernel,
-        in_specs=[pl.BlockSpec(memory_space=pl.ANY)]
-        + [pl.BlockSpec(memory_space=pltpu.VMEM)] * len(weights),
-        out_specs=pl.BlockSpec(memory_space=pltpu.VMEM),
-        out_shape=jax.ShapeDtypeStruct((8, 128), jnp.int32),
+        in_specs=[vmem, vmem],
+        out_specs=vmem,
+        out_shape=jax.ShapeDtypeStruct(mark.shape, mark.dtype),
         compiler_params=pltpu.CompilerParams(vmem_limit_bytes=EXPERT_VMEM),
         cost_estimate=pl.CostEstimate(
-            flops=0, bytes_accessed=sum(2 * w.size for w in weights), transcendentals=0
+            flops=0, bytes_accessed=2 * weight.size, transcendentals=0
         ),
         name="loaded",
-    )(near, *weights)
-    return mark
+    )(mark, weight)
 
 
 def together(*values):
@@ -220,11 +229,12 @@
     target_row = target.reshape(1, tok_count)
     scalar = pl.BlockSpec(memory_space=pltpu.SMEM)
     vmem = pl.BlockSpec(memory_space=pltpu.VMEM)
-    outbound = pl.pallas_call(
+    *outbound, mark = pl.pallas_call(
         functools.partial(dispatch_kernel, groups, main),
         in_specs=[scalar, vmem, vmem],
-        out_specs=[vmem] * groups,
-        out_shape=[jax.ShapeDtypeStruct((main, folded_width), jnp.bfloat16)] * groups,
+        out_specs=[vmem] * (groups + 1),
+        out_shape=[jax.ShapeDtypeStruct((main, folded_width), jnp.bfloat16)] * groups
+        + [jax.ShapeDtypeStruct((8, 128), jnp.int32)],
         compiler_params=pltpu.CompilerParams(vmem_limit_bytes=VMEM_LIMIT),
         cost_estimate=pl.CostEstimate(
             flops=4 * tok_count * tok_count * width,
@@ -236,82 +246,127 @@
 
     gate_mat, up_mat, down_mat = gate_weight[0], up_weight[0], down_weight[0]
 
-    def offsets(chunk):
-        return range(chunk * per_chunk, (chunk + 1) * per_chunk)
-
-    def over_chips(own):
-        return [own] + [to_chip(own, c) for c in range(1, chips)]
-
     def stack(parts):
         return jnp.concatenate(list(parts), axis=0)
 
-    def stack_each(lists):
-        return [stack(same) for same in zip(*lists)]
-
-    def experts(held):
-        held = held + [to_core(x) for x in held]
-        keep, send = run_experts(held, gate_mat, up_mat, down_mat, main)
-        return keep, to_core(send)
-
-    def chip_sums(keep, got):
-        count = keep.shape[0] // chips
-        mine = f32(keep[:count]) + f32(got[:count])
-        theirs = []
-        for c in range(1, chips):
-            rows = slice(c * count, (c + 1) * count)
-            theirs.append((f32(keep[rows]) + f32(got[rows])).astype(jnp.bfloat16))
-        return mine, theirs
-
-    def reduce_chips(mine, theirs):
-        for c in range(1, chips):
-            mine = mine + f32(to_chip(theirs[c - 1], c))
-        return mine.astype(jnp.bfloat16)
-
-    back = [None] * groups
-
-    def return_chunk(chunk, finished):
-        for n, k in enumerate(offsets(chunk)):
-            rows = finished[n * main : (n + 1) * main]
-            back[k] = to_group(rows, k) if k else rows
-
-    arrived3 = [to_group(outbound[k], k) for k in offsets(3)]
-    first = over_chips(outbound[0])
-    near = [to_group(outbound[k], k) for k in offsets(0) if k]
-    relayed = to_group(stack([outbound[k] for k in offsets(1)]), per_chunk)
-    mark = loaded(near[-1], gate_mat, up_mat, down_mat)
-    held0 = stack_each([first] + [over_chips(x) for x in near])
-    outbound2 = [outbound[k] for k in offsets(2)]
-    held0[0], mark, relayed, *rest = together(held0[0], mark, relayed, *arrived3, *outbound2)
-    arrived3, outbound2 = rest[:per_chunk], rest[per_chunk:]
-    keep0, got0 = experts(held0)
-    arrived2 = [to_group(x, k) for x, k in zip(outbound2, offsets(2))]
-    held3 = over_chips(stack(arrived3))
-    arrived1 = [
-        to_group(relayed[n * main : (n + 1) * main], n) if n else relayed[:main]
-        for n in range(per_chunk)
-    ]
-    arrived1[-1], keep0 = together(arrived1[-1], keep0)
-    held1 = stack_each([over_chips(x) for x in arrived1])
-    held3[-1], held1[-1], *arrived2 = together(held3[-1], held1[-1], *arrived2)
-    held2 = over_chips(stack(arrived2))
-    keep3, got3 = experts(held3)
-    mine3, theirs3 = chip_sums(keep3, got3)
-    keep1, got1 = experts(held1)
-    held2[-1], keep1, *theirs3 = together(held2[-1], keep1, *theirs3)
-    keep2, got2 = experts(held2)
-    finished3 = reduce_chips(mine3, theirs3)
-    mine2, theirs2 = chip_sums(keep2, got2)
-    mine1, theirs1 = chip_sums(keep1, got1)
-    mine0, theirs0 = chip_sums(keep0, got0)
-    finished3, *theirs1 = together(finished3, *theirs1)
-    return_chunk(3, finished3)
-    finished2 = reduce_chips(mine2, theirs2)
-    finished1 = reduce_chips(mine1, theirs1)
-    finished2, *theirs0 = together(finished2, *theirs0)
-    return_chunk(2, finished2)
-    return_chunk(1, finished1)
-    finished0 = reduce_chips(mine0, theirs0)
-    return_chunk(0, finished0)
+    def cut(x, rows):
+        return [x[at : at + rows] for at in range(0, x.shape[0], rows)]
+
+    def step(*values):
+        nonlocal mark
+        *values, mark = together(*values, mark)
+        return values
+
+    def to_chips(x):
+        return [to_chip(step(x)[0], c) for c in range(1, chips)]
+
+    def to_chips_each(parts):
+        return [to_chip(step(x)[0], c + 1) for c, x in enumerate(parts)]
+
+    half = per_chunk // 2
+    near = range(1, per_chunk)
+
+    def chunk_rows(chunk):
+        return outbound[chunk * per_chunk : (chunk + 1) * per_chunk]
+
+    def to_groups(rows, offsets):
+        return [to_group(step(x)[0], k) if k else x for x, k in zip(rows, offsets)]
+
+    def halves(chunk):
+        first = chunk * per_chunk
+        return range(first, first + half), range(first + half, first + per_chunk)
+
+    own = {"00": [outbound[0]]}
+    chip = {}
+    held = {}
+    got, keep, sums = {}, {}, {}
+
+    def expert_rows(chunk, mine, others):
+        held[chunk] = [stack(mine)] + [stack(parts) for parts in zip(*others)]
+
+    def start(name):
+        kind, n = name[0], name[1:]
+        if name == "y0":
+            return to_groups(chunk_rows(0)[1:], near)
+        if name == "y2":
+            return to_groups(chunk_rows(2)[1:], near)
+        if name == "y1":
+            return to_groups(got["g1"][1:], near)
+        if name == "g1":
+            return [to_group(step(stack(chunk_rows(1)))[0], per_chunk)]
+        if name == "g2":
+            rows = stack(chunk_rows(2)[:1] + got["y2"])
+            return [to_group(step(rows)[0], 2 * per_chunk)]
+        if kind == "g":
+            part = halves(3)[int(n[1])]
+            return to_groups([outbound[k] for k in part], part)
+        if kind == "x":
+            return to_chips(stack(own[n]))
+        if kind == "c":
+            if n[1:] == "x":
+                return [to_core(step(x)[0]) for x in held[n[0]][1:]]
+            return [to_core(step(held_own(n))[0])]
+        if kind == "b":
+            return [to_core(keep[n][1])]
+        if kind == "r":
+            return to_chips_each(sums[n][1:])
+        part = {"0": near, "1": range(per_chunk)}.get(n)
+        if part is None:
+            part = range(half) if n[1] == "0" else range(half, per_chunk)
+        return to_groups([sums[n[0]][0][k] for k in part], [int(n[0]) * per_chunk + k for k in part])
+
+    def held_own(n):
+        parts = {"0": ("00", "01"), "1": ("10", "11"), "2": ("2",), "3": ("30", "31")}[n]
+        return stack([x for p in parts for x in own[p]])
+
+    def finish(name):
+        kind, n = name[0], name[1:]
+        if name == "y0":
+            own["01"] = got[name]
+        elif name == "g1":
+            got[name] = cut(got[name][0], main)
+            own["10"] = got[name][:1]
+        elif name == "y1":
+            own["11"] = got[name]
+        elif name == "g2":
+            own["2"] = got[name]
+        elif kind == "g":
+            own[n] = got[name]
+        elif kind == "x":
+            chip[n] = got[name]
+            parts = {"0": ("00", "01"), "1": ("10", "11"), "2": ("2",), "3": ("30", "31")}[n[0]]
+            if all(p in chip for p in parts):
+                others = [stack(same) for same in zip(*[chip[p] for p in parts])]
+                held[n[0]] = [held_own(n[0])] + others
+        elif kind == "b":
+            kept, came = keep[n][0], got[name][0]
+            count = kept.shape[0] // chips
+            total = [f32(a) + f32(b) for a, b in zip(cut(kept, count), cut(came, count))]
+            sums[n] = total[:1] + [x.astype(jnp.bfloat16) for x in total[1:]]
+        elif kind == "r":
+            total = sums[n][0]
+            for x in got[name]:
+                total = total + f32(x)
+            sums[n] = [cut(total.astype(jnp.bfloat16), main)]
+
+    flying = {}
+    for name in ORDER:
+        kind, what = name[0], name[2:]
+        if kind == "L":
+            mark = loaded(mark, {"g": gate_mat, "u": up_mat, "d": down_mat}[what])
+        elif kind == "E":
+            rows = step(*held[what], *got["c" + what], *got["c" + what + "x"])
+            kept, send = run_experts(rows, gate_mat, up_mat, down_mat, main)
+            keep[what] = (kept, step(send)[0])
+        elif kind == "S":
+            flying[what] = start(what)
+        else:
+            got[what] = step(*flying.pop(what))
+            finish(what)
+
+    back = [sums["0"][0][0]] + got["h0"] + got["h1"]
+    for part in ("20", "21", "30", "31"):
+        back += got["h" + part]
 
     return pl.pallas_call(
         functools.partial(combine_kernel, groups, main),

time: 171 us -> 155 us (0.906)
  waiting for transfers between devices: 97 us -> 83.9 us
  local copies, waits for them, and re-layouts: 11.7 us -> 8.72 us
    ppermute x10 -> x11, waiting for transfers between devices: 61.5 us -> 49.2 us  [to_chip(): return lax.ppermute(x, 'inner', [(i, i ^ 2 * offset) for i in range(inner)])]
    ppermute x14, waiting for transfers between devices: 34.2 us -> 25.9 us  [to_group(): return lax.ppermute(x, 'group', [(i, i ^ offset) for i in range(groups)])]
    ppermute x12, waiting for transfers between devices: 1.28 us -> 8.77 us  [to_core(): return lax.ppermute(x, 'inner', [(i, i ^ 1) for i in range(inner)])]
    unnamed x17 -> x23, local copies, waits for them, and re-layouts: 11.5 us -> 8.43 us
    ppermute x14, starting transfers between devices: 22.9 us -> 24.6 us  [to_group(): return lax.ppermute(x, 'group', [(i, i ^ offset) for i in range(groups)])]
    ppermute x10 -> x11, starting transfers between devices: 11.6 us -> 10.9 us  [to_chip(): return lax.ppermute(x, 'inner', [(i, i ^ 2 * offset) for i in range(inner)])]
  transfers between devices with their start and end apart: 36 -> 37, of which waited for: 15 -> 22; matrix products, arithmetic and copies ran while one was open for 1% -> 1% of each run, Pallas kernels for 11% -> 12%
where the time goes in v3:
time: 155 us
  waiting for transfers between devices  83.9 us (54%)
  starting transfers between devices  37.8 us (24%)
  Pallas kernels  22.7 us (15%)
  local copies, waits for them, and re-layouts  8.72 us (6%)
  other arithmetic  1.74 us (1%)
    ppermute x11, waiting for transfers between devices, to_chip(): return lax.ppermute(x, 'inner', [(i, i ^ 2 * offset) for i in range(inner)])  49.2 us
    ppermute x14, waiting for transfers between devices, to_group(): return lax.ppermute(x, 'group', [(i, i ^ offset) for i in range(groups)])  25.9 us
    ppermute x14, starting transfers between devices, to_group(): return lax.ppermute(x, 'group', [(i, i ^ offset) for i in range(groups)])  24.6 us
    pallas_call x4, Pallas kernels, run_experts(): pl.pallas_call(functools.partial(expert_kernel, main, parts), in_specs=[v...  18.9 us
    ppermute x11, starting transfers between devices, to_chip(): return lax.ppermute(x, 'inner', [(i, i ^ 2 * offset) for i in range(inner)])  10.9 us
    ppermute x12, waiting for transfers between devices, to_core(): return lax.ppermute(x, 'inner', [(i, i ^ 1) for i in range(inner)])  8.77 us
    unnamed x23, local copies, waits for them, and re-layouts  8.43 us
  transfers between devices with their start and end apart: 37, of which 22 were waited for; matrix products, arithmetic and copies ran while one was open for 1% of the time, Pallas kernels for 12%

profile of v3, /device:TPU:0, one launch (start us, length us, event | category | flops | bytes accessed | tf_op | source)
XLA Modules:
  0.0 155.2 jit_solution(13177145942413232833)
XLA Ops:
  3.4 3.0 %collective-permute-start = (bf16[16,8960]{1,0:T(8,128)(2,1)S(1)}, bf16[16,8960]{1,0:T(8,128)(2,1)S(1)}, u32[]{:S(2)}, u32[]{:S(2)}) collective-permute-start(bf16[16,8960]{1,0:T(8,128)(2,1)S(1)} %get-tuple-element.191), channel_id=1, source_target_pairs={{0,4},{4,0},{8,12},{12,8},{16,20},{20,16},{24,28},{28,24},{1,5},{5... | collective-permute-start | bytes 860168 | tf_op jit(solution)/shard_map/ppermute | solution.py:220
  7.9 3.6 %collective-permute-start.6 = (bf16[16,8960]{1,0:T(8,128)(2,1)S(1)}, bf16[16,8960]{1,0:T(8,128)(2,1)S(1)}, u32[]{:S(2)}, u32[]{:S(2)}) collective-permute-start(bf16[16,8960]{1,0:T(8,128)(2,1)S(1)} %get-tuple-element.218), channel_id=1, source_target_pairs={{0,24},{4,28},{8,16},{12,20},{16,8},{20,12},{24,0},{28,4},{1,25},{... | collective-permute-start | bytes 860168 | tf_op jit(solution)/shard_map/ppermute | solution.py:220
  11.9 3.1 %copy-done = bf16[1,7168,512]{2,1,0:T(8,128)(2,1)S(1)} copy-done((bf16[1,7168,512]{2,1,0:T(8,128)(2,1)S(1)}, bf16[1,7168,512]{2,1,0:T(8,128)(2,1)}, u32[]{:S(2)}) %copy-start) | copy-done | bytes 7340056
  14.9 3.1 %copy-done.1 = bf16[1,7168,512]{2,1,0:T(8,128)(2,1)S(1)} copy-done((bf16[1,7168,512]{2,1,0:T(8,128)(2,1)S(1)}, bf16[1,7168,512]{2,1,0:T(8,128)(2,1)}, u32[]{:S(2)}) %copy-start.1) | copy-done | bytes 7340056
  20.2 5.5 %collective-permute-done.2 = bf16[16,8960]{1,0:T(8,128)(2,1)S(1)} collective-permute-done((bf16[16,8960]{1,0:T(8,128)(2,1)S(1)}, bf16[16,8960]{1,0:T(8,128)(2,1)S(1)}, u32[]{:S(2)}, u32[]{:S(2)}) %collective-permute-start.2) | collective-permute-done | bytes 286752 | tf_op jit(solution)/shard_map/ppermute | solution.py:223
  25.8 4.4 %collective-permute-done.4 = bf16[16,8960]{1,0:T(8,128)(2,1)S(1)} collective-permute-done((bf16[16,8960]{1,0:T(8,128)(2,1)S(1)}, bf16[16,8960]{1,0:T(8,128)(2,1)S(1)}, u32[]{:S(2)}, u32[]{:S(2)}) %collective-permute-start.4) | collective-permute-done | bytes 286752 | tf_op jit(solution)/shard_map/ppermute | solution.py:220
  32.3 4.1 %collective-permute-done.7 = bf16[32,8960]{1,0:T(8,128)(2,1)S(1)} collective-permute-done((bf16[32,8960]{1,0:T(8,128)(2,1)S(1)}, bf16[32,8960]{1,0:T(8,128)(2,1)S(1)}, u32[]{:S(2)}, u32[]{:S(2)}) %collective-permute-start.7) | collective-permute-done | bytes 573472 | tf_op jit(solution)/shard_map/ppermute | solution.py:220
  41.2 4.9 %collective-permute-done.9 = bf16[16,8960]{1,0:T(8,128)(2,1)S(1)} collective-permute-done((bf16[16,8960]{1,0:T(8,128)(2,1)S(1)}, bf16[16,8960]{1,0:T(8,128)(2,1)S(1)}, u32[]{:S(2)}, u32[]{:S(2)}) %collective-permute-start.9) | collective-permute-done | bytes 286752 | tf_op jit(solution)/shard_map/ppermute | solution.py:223
  46.2 4.7 %experts.4 = (bf16[64,8960]{1,0:T(8,128)(2,1)S(1)}, bf16[64,8960]{1,0:T(8,128)(2,1)S(1)}) custom-call(bf16[7168,512]{1,0:T(8,128)(2,1)S(1)} %bitcast.9, bf16[7168,512]{1,0:T(8,128)(2,1)S(1)} %bitcast.14, bf16[512,7168]{1,0:T(8,128)(2,1)S(1)} %bitcast.19, bf16[32,8960]{1,0:T(8,128)(2,1)S(1)} %constant_dynamic-update-slice_fusion.refs_0_, ...), custom_call_target="tpu_custom_call" | custom-call | flops 3523215360 | bytes 4587520 | tf_op jit(solution)/shard_map/experts/pallas_call | solution.py:167
  57.5 4.7 %experts.5 = (bf16[64,8960]{1,0:T(8,128)(2,1)S(1)}, bf16[64,8960]{1,0:T(8,128)(2,1)S(1)}) custom-call(bf16[7168,512]{1,0:T(8,128)(2,1)S(1)} %bitcast.10, bf16[7168,512]{1,0:T(8,128)(2,1)S(1)} %bitcast.15, bf16[512,7168]{1,0:T(8,128)(2,1)S(1)} %bitcast.20, bf16[32,8960]{1,0:T(8,128)(2,1)S(1)} %constant_dynamic-update-slice_fusion.4.refs_0_, ...), custom_call_target="tpu_custom_call" | custom-call | flops 3523215360 | bytes 4587520 | tf_op jit(solution)/shard_map/experts/pallas_call | solution.py:167
  68.9 4.7 %experts.6 = (bf16[64,8960]{1,0:T(8,128)(2,1)S(1)}, bf16[64,8960]{1,0:T(8,128)(2,1)S(1)}) custom-call(bf16[7168,512]{1,0:T(8,128)(2,1)S(1)} %bitcast.11, bf16[7168,512]{1,0:T(8,128)(2,1)S(1)} %bitcast.16, bf16[512,7168]{1,0:T(8,128)(2,1)S(1)} %bitcast.21, bf16[32,8960]{1,0:T(8,128)(2,1)S(1)} %pad_maximum_fusion.2.refs_0_, ...), custom_call_target="tpu_custom_call" | custom-call | flops 3523215360 | bytes 4587520 | tf_op jit(solution)/shard_map/experts/pallas_call | solution.py:167
  77.3 5.1 %collective-permute-done.24.refs_1_ = bf16[32,8960]{1,0:T(8,128)(2,1)S(1)} collective-permute-done((bf16[32,8960]{1,0:T(8,128)(2,1)S(1)}, bf16[32,8960]{1,0:T(8,128)(2,1)S(1)}, u32[]{:S(2)}, u32[]{:S(2)}) %collective-permute-start.24) | collective-permute-done | bytes 573472 | tf_op jit(solution)/shard_map/ppermute | solution.py:223
  84.5 4.7 %experts.7 = (bf16[64,8960]{1,0:T(8,128)(2,1)S(1)}, bf16[64,8960]{1,0:T(8,128)(2,1)S(1)}) custom-call(bf16[7168,512]{1,0:T(8,128)(2,1)S(1)} %bitcast.12, bf16[7168,512]{1,0:T(8,128)(2,1)S(1)} %bitcast.17, bf16[512,7168]{1,0:T(8,128)(2,1)S(1)} %bitcast.22, bf16[32,8960]{1,0:T(8,128)(2,1)S(1)} %collective-permute-done.20.refs_0_, ...), custom_call_target="tpu_custom_call" | custom-call | flops 3523215360 | bytes 4587520 | tf_op jit(solution)/shard_map/experts/pallas_call | solution.py:167
  89.4 3.4 %collective-permute-done.23 = bf16[32,8960]{1,0:T(8,128)(2,1)S(1)} collective-permute-done((bf16[32,8960]{1,0:T(8,128)(2,1)S(1)}, bf16[32,8960]{1,0:T(8,128)(2,1)S(1)}, u32[]{:S(2)}, u32[]{:S(2)}) %collective-permute-start.23) | collective-permute-done | bytes 573472 | tf_op jit(solution)/shard_map/ppermute | solution.py:223
  94.8 4.5 %collective-permute-start.30 = (bf16[16,8960]{1,0:T(8,128)(2,1)S(1)}, bf16[16,8960]{1,0:T(8,128)(2,1)S(1)}, u32[]{:S(2)}, u32[]{:S(2)}) collective-permute-start(bf16[16,8960]{1,0:T(8,128)(2,1)S(1)} %get-tuple-element.337), channel_id=1, source_target_pairs={{0,28},{4,24},{8,20},{12,16},{16,12},{20,8},{24,4},{28,0},{1,29},{... | collective-permute-start | bytes 860168 | tf_op jit(solution)/shard_map/ppermute | solution.py:220
  100.2 8.9 %collective-permute-done.27 = bf16[32,8960]{1,0:T(8,128)(2,1)S(1)} collective-permute-done((bf16[32,8960]{1,0:T(8,128)(2,1)S(1)}, bf16[32,8960]{1,0:T(8,128)(2,1)S(1)}, u32[]{:S(2)}, u32[]{:S(2)}) %collective-permute-start.27) | collective-permute-done | bytes 573472 | tf_op jit(solution)/shard_map/ppermute | solution.py:223
  109.3 10.1 %collective-permute-done.29 = bf16[32,8960]{1,0:T(8,128)(2,1)S(1)} collective-permute-done((bf16[32,8960]{1,0:T(8,128)(2,1)S(1)}, bf16[32,8960]{1,0:T(8,128)(2,1)S(1)}, u32[]{:S(2)}, u32[]{:S(2)}) %collective-permute-start.29) | collective-permute-done | bytes 573472 | tf_op jit(solution)/shard_map/ppermute | solution.py:223
  124.3 2.1 %collective-permute-start.33 = (bf16[16,8960]{1,0:T(8,128)(2,1)S(1)}, bf16[16,8960]{1,0:T(8,128)(2,1)S(1)}, u32[]{:S(2)}, u32[]{:S(2)}) collective-permute-start(bf16[16,8960]{1,0:T(8,128)(2,1)S(1)} %get-tuple-element.350), channel_id=1, source_target_pairs={{0,16},{4,20},{8,24},{12,28},{16,0},{20,4},{24,8},{28,12},{1,17},{... | collective-permute-start | bytes 860168 | tf_op jit(solution)/shard_map/ppermute | solution.py:220
  126.4 6.3 %collective-permute-done.28 = bf16[32,8960]{1,0:T(8,128)(2,1)S(1)} collective-permute-done((bf16[32,8960]{1,0:T(8,128)(2,1)S(1)}, bf16[32,8960]{1,0:T(8,128)(2,1)S(1)}, u32[]{:S(2)}, u32[]{:S(2)}) %collective-permute-start.28) | collective-permute-done | bytes 573472 | tf_op jit(solution)/shard_map/ppermute | solution.py:223
  133.8 3.2 %collective-permute-start.31 = (bf16[16,8960]{1,0:T(8,128)(2,1)S(1)}, bf16[16,8960]{1,0:T(8,128)(2,1)S(1)}, u32[]{:S(2)}, u32[]{:S(2)}) collective-permute-start(bf16[16,8960]{1,0:T(8,128)(2,1)S(1)} %get-tuple-element.348), channel_id=1, source_target_pairs={{0,4},{4,0},{8,12},{12,8},{16,20},{20,16},{24,28},{28,24},{1,5},{5... | collective-permute-start | bytes 860168 | tf_op jit(solution)/shard_map/ppermute | solution.py:220
  137.0 3.3 %collective-permute-done.35.refs_3_ = bf16[16,8960]{1,0:T(8,128)(2,1)S(1)} collective-permute-done((bf16[16,8960]{1,0:T(8,128)(2,1)S(1)}, bf16[16,8960]{1,0:T(8,128)(2,1)S(1)}, u32[]{:S(2)}, u32[]{:S(2)}) %collective-permute-start.35) | collective-permute-done | bytes 286752 | tf_op jit(solution)/shard_map/ppermute | solution.py:220
  140.2 3.2 %collective-permute-done.34.refs_2_ = bf16[16,8960]{1,0:T(8,128)(2,1)S(1)} collective-permute-done((bf16[16,8960]{1,0:T(8,128)(2,1)S(1)}, bf16[16,8960]{1,0:T(8,128)(2,1)S(1)}, u32[]{:S(2)}, u32[]{:S(2)}) %collective-permute-start.34) | collective-permute-done | bytes 286752 | tf_op jit(solution)/shard_map/ppermute | solution.py:220
  143.4 9.3 %collective-permute-done.32.refs_5_ = bf16[16,8960]{1,0:T(8,128)(2,1)S(1)} collective-permute-done((bf16[16,8960]{1,0:T(8,128)(2,1)S(1)}, bf16[16,8960]{1,0:T(8,128)(2,1)S(1)}, u32[]{:S(2)}, u32[]{:S(2)}) %collective-permute-start.32) | collective-permute-done | bytes 286752 | tf_op jit(solution)/shard_map/ppermute | solution.py:220
  152.7 2.5 %combine.1 = bf16[128,7168]{1,0:T(8,128)(2,1)} custom-call(s32[1]{0:T(128)} %bitcast.me_ref, s32[1,128]{1,0:T(1,128)S(1)} %bitcast.24, f32[1,128]{1,0:T(1,128)S(1)} %bitcast.25, bf16[16,8960]{1,0:T(8,128)(2,1)S(1)} %get-tuple-element.368.refs_0_, bf16[16,8960]{1,0:T(8,128)(2,1)S(1)} %collective-permute-done.31.refs_1_, ...), custom_call_target="tpu_custom_call" | custom-call | flops 469762048 | bytes 4587520 | tf_op jit(solution)/shard_map/combine/pallas_call | solution.py:371
  (104 shorter events, 42.4 us)
Async XLA Ops:
  3.4 11.5 %collective-permute-start = (bf16[16,8960]{1,0:T(8,128)(2,1)S(1)}, bf16[16,8960]{1,0:T(8,128)(2,1)S(1)}, u32[]{:S(2)}, u32[]{:S(2)}) collective-permute-start(bf16[16,8960]{1,0:T(8,128)(2,1)S(1)} %get-tuple-element.191), channel_id=1, source_target_pairs={{0,4},{4,0},{8,12},{12,8},{16,20},{20,16},{24,28},{28,24},{1,5},{5... | collective-permute-start | bytes 860168 | tf_op jit(solution)/shard_map/ppermute | solution.py:220
  6.4 11.6 %collective-permute-start.1 = (bf16[16,8960]{1,0:T(8,128)(2,1)S(1)}, bf16[16,8960]{1,0:T(8,128)(2,1)S(1)}, u32[]{:S(2)}, u32[]{:S(2)}) collective-permute-start(bf16[16,8960]{1,0:T(8,128)(2,1)S(1)} %get-tuple-element.200), channel_id=1, source_target_pairs={{0,2},{1,3},{2,0},{3,1},{4,6},{5,7},{6,4},{7,5},{8,10},{9,11},{10,... | collective-permute-start | bytes 860168 | tf_op jit(solution)/shard_map/ppermute | solution.py:223
  7.9 24.3 %collective-permute-start.6 = (bf16[16,8960]{1,0:T(8,128)(2,1)S(1)}, bf16[16,8960]{1,0:T(8,128)(2,1)S(1)}, u32[]{:S(2)}, u32[]{:S(2)}) collective-permute-start(bf16[16,8960]{1,0:T(8,128)(2,1)S(1)} %get-tuple-element.218), channel_id=1, source_target_pairs={{0,24},{4,28},{8,16},{12,20},{16,8},{20,12},{24,0},{28,4},{1,25},{... | collective-permute-start | bytes 860168 | tf_op jit(solution)/shard_map/ppermute | solution.py:220
  11.6 20.6 %collective-permute-start.8 = (bf16[16,8960]{1,0:T(8,128)(2,1)S(1)}, bf16[16,8960]{1,0:T(8,128)(2,1)S(1)}, u32[]{:S(2)}, u32[]{:S(2)}) collective-permute-start(bf16[16,8960]{1,0:T(8,128)(2,1)S(1)} %get-tuple-element.222), channel_id=1, source_target_pairs={{0,28},{4,24},{8,20},{12,16},{16,12},{20,8},{24,4},{28,0},{1,29},{... | collective-permute-start | bytes 860168 | tf_op jit(solution)/shard_map/ppermute | solution.py:220
  11.8 24.5 %collective-permute-start.7 = (bf16[32,8960]{1,0:T(8,128)(2,1)S(1)}, bf16[32,8960]{1,0:T(8,128)(2,1)S(1)}, u32[]{:S(2)}, u32[]{:S(2)}) collective-permute-start(bf16[32,8960]{1,0:T(8,128)(2,1)S(1)} %pad_maximum_fusion), channel_id=1, source_target_pairs={{0,8},{4,12},{8,0},{12,4},{16,24},{20,28},{24,16},{28,20},{1,9},{5... | collective-permute-start | bytes 1720328 | tf_op jit(solution)/shard_map/ppermute | solution.py:220
  18.5 11.7 %collective-permute-start.4 = (bf16[16,8960]{1,0:T(8,128)(2,1)S(1)}, bf16[16,8960]{1,0:T(8,128)(2,1)S(1)}, u32[]{:S(2)}, u32[]{:S(2)}) collective-permute-start(bf16[16,8960]{1,0:T(8,128)(2,1)S(1)} %get-tuple-element.210), channel_id=1, source_target_pairs={{0,4},{4,0},{8,12},{12,8},{16,20},{20,16},{24,28},{28,24},{1,5},{5... | collective-permute-start | bytes 860168 | tf_op jit(solution)/shard_map/ppermute | solution.py:220
  36.4 9.8 %collective-permute-start.9 = (bf16[16,8960]{1,0:T(8,128)(2,1)S(1)}, bf16[16,8960]{1,0:T(8,128)(2,1)S(1)}, u32[]{:S(2)}, u32[]{:S(2)}) collective-permute-start(bf16[16,8960]{1,0:T(8,128)(2,1)S(1)} %collective-permute-done.6), channel_id=1, source_target_pairs={{0,2},{1,3},{2,0},{3,1},{4,6},{5,7},{6,4},{7,5},{8,10},{9,11},{10,... | collective-permute-start | bytes 860168 | tf_op jit(solution)/shard_map/ppermute | solution.py:223
  37.0 15.3 %collective-permute-start.12 = (bf16[16,8960]{1,0:T(8,128)(2,1)S(1)}, bf16[16,8960]{1,0:T(8,128)(2,1)S(1)}, u32[]{:S(2)}, u32[]{:S(2)}) collective-permute-start(bf16[16,8960]{1,0:T(8,128)(2,1)S(1)} %collective-permute-done.8), channel_id=1, source_target_pairs={{0,2},{1,3},{2,0},{3,1},{4,6},{5,7},{6,4},{7,5},{8,10},{9,11},{10,... | collective-permute-start | bytes 860168 | tf_op jit(solution)/shard_map/ppermute | solution.py:223
  38.6 13.9 %collective-permute-start.11 = (bf16[16,8960]{1,0:T(8,128)(2,1)S(1)}, bf16[16,8960]{1,0:T(8,128)(2,1)S(1)}, u32[]{:S(2)}, u32[]{:S(2)}) collective-permute-start(bf16[16,8960]{1,0:T(8,128)(2,1)S(1)} %get-tuple-element.245), channel_id=1, source_target_pairs={{0,4},{4,0},{8,12},{12,8},{16,20},{20,16},{24,28},{28,24},{1,5},{5... | collective-permute-start | bytes 860168 | tf_op jit(solution)/shard_map/ppermute | solution.py:220
  39.1 18.4 %collective-permute-start.13 = (bf16[16,8960]{1,0:T(8,128)(2,1)S(1)}, bf16[16,8960]{1,0:T(8,128)(2,1)S(1)}, u32[]{:S(2)}, u32[]{:S(2)}) collective-permute-start(bf16[16,8960]{1,0:T(8,128)(2,1)S(1)} %get-tuple-element.257), channel_id=1, source_target_pairs={{0,2},{1,3},{2,0},{3,1},{4,6},{5,7},{6,4},{7,5},{8,10},{9,11},{10,... | collective-permute-start | bytes 860168 | tf_op jit(solution)/shard_map/ppermute | solution.py:223
  39.6 27.0 %collective-permute-start.20 = (bf16[32,8960]{1,0:T(8,128)(2,1)S(1)}, bf16[32,8960]{1,0:T(8,128)(2,1)S(1)}, u32[]{:S(2)}, u32[]{:S(2)}) collective-permute-start(bf16[32,8960]{1,0:T(8,128)(2,1)S(1)} %pad_maximum_fusion.1), channel_id=1, source_target_pairs={{0,16},{4,20},{8,24},{12,28},{16,0},{20,4},{24,8},{28,12},{1,17},{... | collective-permute-start | bytes 1720328 | tf_op jit(solution)/shard_map/ppermute | solution.py:220
  55.2 8.9 %collective-permute-start.14 = (bf16[16,8960]{1,0:T(8,128)(2,1)S(1)}, bf16[16,8960]{1,0:T(8,128)(2,1)S(1)}, u32[]{:S(2)}, u32[]{:S(2)}) collective-permute-start(bf16[16,8960]{1,0:T(8,128)(2,1)S(1)} %collective-permute-done.11), channel_id=1, source_target_pairs={{0,2},{1,3},{2,0},{3,1},{4,6},{5,7},{6,4},{7,5},{8,10},{9,11},{10,... | collective-permute-start | bytes 860168 | tf_op jit(solution)/shard_map/ppermute | solution.py:223
  66.6 15.9 %collective-permute-start.24 = (bf16[32,8960]{1,0:T(8,128)(2,1)S(1)}, bf16[32,8960]{1,0:T(8,128)(2,1)S(1)}, u32[]{:S(2)}, u32[]{:S(2)}) collective-permute-start(bf16[32,8960]{1,0:T(8,128)(2,1)S(1)} %collective-permute-done.20.refs_0_), channel_id=1, source_target_pairs={{0,2},{1,3},{2,0},{3,1},{4,6},{5,7},{6,4},{7,5},{8,10},{9,11},{10,... | collective-permute-start | bytes 1720328 | tf_op jit(solution)/shard_map/ppermute | solution.py:223
  74.4 18.4 %collective-permute-start.23 = (bf16[32,8960]{1,0:T(8,128)(2,1)S(1)}, bf16[32,8960]{1,0:T(8,128)(2,1)S(1)}, u32[]{:S(2)}, u32[]{:S(2)}) collective-permute-start(bf16[32,8960]{1,0:T(8,128)(2,1)S(1)} %add_convert_fusion.6), channel_id=1, source_target_pairs={{0,2},{1,3},{2,0},{3,1},{4,6},{5,7},{6,4},{7,5},{8,10},{9,11},{10,... | collective-permute-start | bytes 1720328 | tf_op jit(solution)/shard_map/ppermute | solution.py:223
  93.0 16.0 %collective-permute-start.27 = (bf16[32,8960]{1,0:T(8,128)(2,1)S(1)}, bf16[32,8960]{1,0:T(8,128)(2,1)S(1)}, u32[]{:S(2)}, u32[]{:S(2)}) collective-permute-start(bf16[32,8960]{1,0:T(8,128)(2,1)S(1)} %add_convert_fusion.5), channel_id=1, source_target_pairs={{0,2},{1,3},{2,0},{3,1},{4,6},{5,7},{6,4},{7,5},{8,10},{9,11},{10,... | collective-permute-start | bytes 1720328 | tf_op jit(solution)/shard_map/ppermute | solution.py:223
  94.8 14.5 %collective-permute-start.30 = (bf16[16,8960]{1,0:T(8,128)(2,1)S(1)}, bf16[16,8960]{1,0:T(8,128)(2,1)S(1)}, u32[]{:S(2)}, u32[]{:S(2)}) collective-permute-start(bf16[16,8960]{1,0:T(8,128)(2,1)S(1)} %get-tuple-element.337), channel_id=1, source_target_pairs={{0,28},{4,24},{8,20},{12,16},{16,12},{20,8},{24,4},{28,0},{1,29},{... | collective-permute-start | bytes 860168 | tf_op jit(solution)/shard_map/ppermute | solution.py:220
  99.3 20.1 %collective-permute-start.29 = (bf16[32,8960]{1,0:T(8,128)(2,1)S(1)}, bf16[32,8960]{1,0:T(8,128)(2,1)S(1)}, u32[]{:S(2)}, u32[]{:S(2)}) collective-permute-start(bf16[32,8960]{1,0:T(8,128)(2,1)S(1)} %add_convert_fusion.3), channel_id=1, source_target_pairs={{0,2},{1,3},{2,0},{3,1},{4,6},{5,7},{6,4},{7,5},{8,10},{9,11},{10,... | collective-permute-start | bytes 1720328 | tf_op jit(solution)/shard_map/ppermute | solution.py:223
  99.8 34.0 %collective-permute-start.36 = (bf16[16,8960]{1,0:T(8,128)(2,1)S(1)}, bf16[16,8960]{1,0:T(8,128)(2,1)S(1)}, u32[]{:S(2)}, u32[]{:S(2)}) collective-permute-start(bf16[16,8960]{1,0:T(8,128)(2,1)S(1)} %get-tuple-element.353), channel_id=1, source_target_pairs={{0,24},{4,28},{8,16},{12,20},{16,8},{20,12},{24,0},{28,4},{1,25},{... | collective-permute-start | bytes 860168 | tf_op jit(solution)/shard_map/ppermute | solution.py:220
  119.6 13.1 %collective-permute-start.28 = (bf16[32,8960]{1,0:T(8,128)(2,1)S(1)}, bf16[32,8960]{1,0:T(8,128)(2,1)S(1)}, u32[]{:S(2)}, u32[]{:S(2)}) collective-permute-start(bf16[32,8960]{1,0:T(8,128)(2,1)S(1)} %add_convert_fusion.7), channel_id=1, source_target_pairs={{0,2},{1,3},{2,0},{3,1},{4,6},{5,7},{6,4},{7,5},{8,10},{9,11},{10,... | collective-permute-start | bytes 1720328 | tf_op jit(solution)/shard_map/ppermute | solution.py:223
  121.2 19.0 %collective-permute-start.35 = (bf16[16,8960]{1,0:T(8,128)(2,1)S(1)}, bf16[16,8960]{1,0:T(8,128)(2,1)S(1)}, u32[]{:S(2)}, u32[]{:S(2)}) collective-permute-start(bf16[16,8960]{1,0:T(8,128)(2,1)S(1)} %get-tuple-element.352), channel_id=1, source_target_pairs={{0,12},{4,8},{8,4},{12,0},{16,28},{20,24},{24,20},{28,16},{1,13},{... | collective-permute-start | bytes 860168 | tf_op jit(solution)/shard_map/ppermute | solution.py:220
  123.0 20.4 %collective-permute-start.34 = (bf16[16,8960]{1,0:T(8,128)(2,1)S(1)}, bf16[16,8960]{1,0:T(8,128)(2,1)S(1)}, u32[]{:S(2)}, u32[]{:S(2)}) collective-permute-start(bf16[16,8960]{1,0:T(8,128)(2,1)S(1)} %get-tuple-element.351), channel_id=1, source_target_pairs={{0,8},{4,12},{8,0},{12,4},{16,24},{20,28},{24,16},{28,20},{1,9},{5... | collective-permute-start | bytes 860168 | tf_op jit(solution)/shard_map/ppermute | solution.py:220
  124.3 19.2 %collective-permute-start.33 = (bf16[16,8960]{1,0:T(8,128)(2,1)S(1)}, bf16[16,8960]{1,0:T(8,128)(2,1)S(1)}, u32[]{:S(2)}, u32[]{:S(2)}) collective-permute-start(bf16[16,8960]{1,0:T(8,128)(2,1)S(1)} %get-tuple-element.350), channel_id=1, source_target_pairs={{0,16},{4,20},{8,24},{12,28},{16,0},{20,4},{24,8},{28,12},{1,17},{... | collective-permute-start | bytes 860168 | tf_op jit(solution)/shard_map/ppermute | solution.py:220
  132.7 20.0 %collective-permute-start.32 = (bf16[16,8960]{1,0:T(8,128)(2,1)S(1)}, bf16[16,8960]{1,0:T(8,128)(2,1)S(1)}, u32[]{:S(2)}, u32[]{:S(2)}) collective-permute-start(bf16[16,8960]{1,0:T(8,128)(2,1)S(1)} %get-tuple-element.349), channel_id=1, source_target_pairs={{0,20},{4,16},{8,28},{12,24},{16,4},{20,0},{24,12},{28,8},{1,21},{... | collective-permute-start | bytes 860168 | tf_op jit(solution)/shard_map/ppermute | solution.py:220
  133.8 18.9 %collective-permute-start.31 = (bf16[16,8960]{1,0:T(8,128)(2,1)S(1)}, bf16[16,8960]{1,0:T(8,128)(2,1)S(1)}, u32[]{:S(2)}, u32[]{:S(2)}) collective-permute-start(bf16[16,8960]{1,0:T(8,128)(2,1)S(1)} %get-tuple-element.348), channel_id=1, source_target_pairs={{0,4},{4,0},{8,12},{12,8},{16,20},{20,16},{24,28},{28,24},{1,5},{5... | collective-permute-start | bytes 860168 | tf_op jit(solution)/shard_map/ppermute | solution.py:220
  (22 other events, 157.2 us)

commit v4 on v3

--- a/solution.py
+++ b/solution.py
@@ -14,12 +14,15 @@
 
 
 ORDER = (
-    "S.g30 S.y0 S.x00 S.g1 S.g31 L.g D.y0 S.x01 S.y2 L.u D.x00 D.x01 S.c0 S.c0x L.d D.y2 D.c0 D.c0x "
-    "D.g30 D.g31 D.g1 S.g2 S.x31 S.y1 S.x30 S.x10 D.x30 E.0 S.b0 S.c3 D.x31 D.y1 S.c3x S.x11 D.b0 D.x10 "
-    "D.c3 D.c3x E.3 S.b3 D.x11 S.c1 S.c1x D.g2 S.x2 D.c1x D.b3 D.c1 S.c2 S.r3 E.1 S.b1 D.c2 D.b1 D.x2 "
-    "S.c2x D.c2x E.2 S.b2 D.r3 D.b2 S.h30 S.h31 S.r1 S.r2 D.r1 S.r0 D.h31 S.h1 D.r2 S.h20 S.h21 D.r0 "
-    "S.h0 D.h30 D.h1 D.h20 D.h21 D.h0"
-).split()
+    "S.g30", "S.y0", "S.g1", "S.x00", "S.g31", "L.g", "D.y0", "S.y2", "L.u", "S.x01", "D.x00",
+    "D.x01", "S.c0", "S.c0x", "L.d", "D.c0", "D.g30", "D.g31", "S.x31", "D.y2", "D.g1", "S.g2",
+    "S.y1", "D.c0x", "S.x30", "D.x30", "S.x10", "E.0", "D.x31", "S.b0", "D.b0", "S.c3x", "D.y1",
+    "S.x11", "S.c3", "D.c3", "D.x10", "D.c3x", "E.3", "S.b3", "D.x11", "S.c1", "S.c1x", "D.g2",
+    "S.x2", "D.c1x", "S.c2", "D.c1", "D.b3", "S.r3", "E.1", "S.b1", "D.b1", "D.x2", "S.c2x",
+    "S.r1", "D.c2", "D.c2x", "E.2", "S.b2", "D.r3", "D.b2", "S.h30", "S.h31", "S.r2", "D.h31",
+    "S.r0", "D.r1", "S.h1", "D.r2", "S.h20", "S.h21", "D.r0", "S.h0", "D.h30", "D.h20", "D.h21",
+    "D.h1", "D.h0",
+)
 
 
 def slots_of(target_row, me, groups, main):

time: 155 us -> 154 us (level)
  waiting for transfers between devices: 83.9 us -> 78.2 us
  starting transfers between devices: 37.8 us -> 42 us
    ppermute x11, waiting for transfers between devices: 49.2 us -> 35 us  [to_chip(): return lax.ppermute(x, 'inner', [(i, i ^ 2 * offset) for i in range(inner)])]
    ppermute x14, starting transfers between devices: 24.6 us -> 32.1 us  [to_group(): return lax.ppermute(x, 'group', [(i, i ^ offset) for i in range(groups)])]
    ppermute x14, waiting for transfers between devices: 25.9 us -> 32.5 us  [to_group(): return lax.ppermute(x, 'group', [(i, i ^ offset) for i in range(groups)])]
    ppermute x11, starting transfers between devices: 10.9 us -> 7.65 us  [to_chip(): return lax.ppermute(x, 'inner', [(i, i ^ 2 * offset) for i in range(inner)])]
    ppermute x12, waiting for transfers between devices: 8.77 us -> 10.7 us  [to_core(): return lax.ppermute(x, 'inner', [(i, i ^ 1) for i in range(inner)])]
  transfers between devices with their start and end apart: 37 -> 37, of which waited for: 22 -> 20; matrix products, arithmetic and copies ran while one was open for 1% -> 1% of each run, Pallas kernels for 12% -> 12%
where the time goes in v4:
time: 154 us
  waiting for transfers between devices  78.2 us (51%)
  starting transfers between devices  42 us (27%)
  Pallas kernels  22.7 us (15%)
  local copies, waits for them, and re-layouts  8.73 us (6%)
  other arithmetic  1.67 us (1%)
    ppermute x11, waiting for transfers between devices, to_chip(): return lax.ppermute(x, 'inner', [(i, i ^ 2 * offset) for i in range(inner)])  35 us
    ppermute x14, waiting for transfers between devices, to_group(): return lax.ppermute(x, 'group', [(i, i ^ offset) for i in range(groups)])  32.5 us
    ppermute x14, starting transfers between devices, to_group(): return lax.ppermute(x, 'group', [(i, i ^ offset) for i in range(groups)])  32.1 us
    pallas_call x4, Pallas kernels, run_experts(): pl.pallas_call(functools.partial(expert_kernel, main, parts), in_specs=[v...  18.9 us
    ppermute x12, waiting for transfers between devices, to_core(): return lax.ppermute(x, 'inner', [(i, i ^ 1) for i in range(inner)])  10.7 us
    unnamed x23, local copies, waits for them, and re-layouts  8.43 us
    ppermute x11, starting transfers between devices, to_chip(): return lax.ppermute(x, 'inner', [(i, i ^ 2 * offset) for i in range(inner)])  7.65 us
  transfers between devices with their start and end apart: 37, of which 20 were waited for; matrix products, arithmetic and copies ran while one was open for 1% of the time, Pallas kernels for 12%

profile of v4, /device:TPU:0, one launch (start us, length us, event | category | flops | bytes accessed | tf_op | source)
XLA Modules:
  0.0 153.7 jit_solution(3362746539321372221)
XLA Ops:
  3.4 3.0 %collective-permute-start = (bf16[16,8960]{1,0:T(8,128)(2,1)S(1)}, bf16[16,8960]{1,0:T(8,128)(2,1)S(1)}, u32[]{:S(2)}, u32[]{:S(2)}) collective-permute-start(bf16[16,8960]{1,0:T(8,128)(2,1)S(1)} %get-tuple-element.190), channel_id=1, source_target_pairs={{0,4},{4,0},{8,12},{12,8},{16,20},{20,16},{24,28},{28,24},{1,5},{5... | collective-permute-start | bytes 860168 | tf_op jit(solution)/shard_map/ppermute | solution.py:223
  8.0 3.6 %collective-permute-start.8 = (bf16[16,8960]{1,0:T(8,128)(2,1)S(1)}, bf16[16,8960]{1,0:T(8,128)(2,1)S(1)}, u32[]{:S(2)}, u32[]{:S(2)}) collective-permute-start(bf16[16,8960]{1,0:T(8,128)(2,1)S(1)} %get-tuple-element.217), channel_id=1, source_target_pairs={{0,24},{4,28},{8,16},{12,20},{16,8},{20,12},{24,0},{28,4},{1,25},{... | collective-permute-start | bytes 860168 | tf_op jit(solution)/shard_map/ppermute | solution.py:223
  11.9 3.1 %copy-done = bf16[1,7168,512]{2,1,0:T(8,128)(2,1)S(1)} copy-done((bf16[1,7168,512]{2,1,0:T(8,128)(2,1)S(1)}, bf16[1,7168,512]{2,1,0:T(8,128)(2,1)}, u32[]{:S(2)}) %copy-start) | copy-done | bytes 7340056
  14.9 3.1 %copy-done.1 = bf16[1,7168,512]{2,1,0:T(8,128)(2,1)S(1)} copy-done((bf16[1,7168,512]{2,1,0:T(8,128)(2,1)S(1)}, bf16[1,7168,512]{2,1,0:T(8,128)(2,1)}, u32[]{:S(2)}) %copy-start.1) | copy-done | bytes 7340056
  20.2 5.4 %collective-permute-done.2 = bf16[16,8960]{1,0:T(8,128)(2,1)S(1)} collective-permute-done((bf16[16,8960]{1,0:T(8,128)(2,1)S(1)}, bf16[16,8960]{1,0:T(8,128)(2,1)S(1)}, u32[]{:S(2)}, u32[]{:S(2)}) %collective-permute-start.2) | collective-permute-done | bytes 286752 | tf_op jit(solution)/shard_map/ppermute | solution.py:226
  27.7 2.6 %collective-permute-done.6 = bf16[16,8960]{1,0:T(8,128)(2,1)S(1)} collective-permute-done((bf16[16,8960]{1,0:T(8,128)(2,1)S(1)}, bf16[16,8960]{1,0:T(8,128)(2,1)S(1)}, u32[]{:S(2)}, u32[]{:S(2)}) %collective-permute-start.6) | collective-permute-done | bytes 286752 | tf_op jit(solution)/shard_map/ppermute | solution.py:223
  30.4 6.1 %collective-permute-done.5 = bf16[32,8960]{1,0:T(8,128)(2,1)S(1)} collective-permute-done((bf16[32,8960]{1,0:T(8,128)(2,1)S(1)}, bf16[32,8960]{1,0:T(8,128)(2,1)S(1)}, u32[]{:S(2)}, u32[]{:S(2)}) %collective-permute-start.5) | collective-permute-done | bytes 573472 | tf_op jit(solution)/shard_map/ppermute | solution.py:223
  40.8 5.5 %collective-permute-done.9 = bf16[16,8960]{1,0:T(8,128)(2,1)S(1)} collective-permute-done((bf16[16,8960]{1,0:T(8,128)(2,1)S(1)}, bf16[16,8960]{1,0:T(8,128)(2,1)S(1)}, u32[]{:S(2)}, u32[]{:S(2)}) %collective-permute-start.9) | collective-permute-done | bytes 286752 | tf_op jit(solution)/shard_map/ppermute | solution.py:226
  46.3 4.7 %experts.4 = (bf16[64,8960]{1,0:T(8,128)(2,1)S(1)}, bf16[64,8960]{1,0:T(8,128)(2,1)S(1)}) custom-call(bf16[7168,512]{1,0:T(8,128)(2,1)S(1)} %bitcast.9, bf16[7168,512]{1,0:T(8,128)(2,1)S(1)} %bitcast.14, bf16[512,7168]{1,0:T(8,128)(2,1)S(1)} %bitcast.19, bf16[32,8960]{1,0:T(8,128)(2,1)S(1)} %constant_dynamic-update-slice_fusion.refs_0_, ...), custom_call_target="tpu_custom_call" | custom-call | flops 3523215360 | bytes 4587520 | tf_op jit(solution)/shard_map/experts/pallas_call | solution.py:170
  56.0 5.3 %collective-permute-done.15 = bf16[16,8960]{1,0:T(8,128)(2,1)S(1)} collective-permute-done((bf16[16,8960]{1,0:T(8,128)(2,1)S(1)}, bf16[16,8960]{1,0:T(8,128)(2,1)S(1)}, u32[]{:S(2)}, u32[]{:S(2)}) %collective-permute-start.15) | collective-permute-done | bytes 286752 | tf_op jit(solution)/shard_map/ppermute | solution.py:226
  61.2 4.7 %experts.5 = (bf16[64,8960]{1,0:T(8,128)(2,1)S(1)}, bf16[64,8960]{1,0:T(8,128)(2,1)S(1)}) custom-call(bf16[7168,512]{1,0:T(8,128)(2,1)S(1)} %bitcast.10, bf16[7168,512]{1,0:T(8,128)(2,1)S(1)} %bitcast.15, bf16[512,7168]{1,0:T(8,128)(2,1)S(1)} %bitcast.20, bf16[32,8960]{1,0:T(8,128)(2,1)S(1)} %constant_dynamic-update-slice_fusion.4.refs_0_, ...), custom_call_target="tpu_custom_call" | custom-call | flops 3523215360 | bytes 4587520 | tf_op jit(solution)/shard_map/experts/pallas_call | solution.py:170
  68.0 2.4 %collective-permute-done.20.refs_3_ = bf16[32,8960]{1,0:T(8,128)(2,1)S(1)} collective-permute-done((bf16[32,8960]{1,0:T(8,128)(2,1)S(1)}, bf16[32,8960]{1,0:T(8,128)(2,1)S(1)}, u32[]{:S(2)}, u32[]{:S(2)}) %collective-permute-start.20) | collective-permute-done | bytes 573472 | tf_op jit(solution)/shard_map/ppermute | solution.py:229
  71.5 4.7 %experts.6 = (bf16[64,8960]{1,0:T(8,128)(2,1)S(1)}, bf16[64,8960]{1,0:T(8,128)(2,1)S(1)}) custom-call(bf16[7168,512]{1,0:T(8,128)(2,1)S(1)} %bitcast.11, bf16[7168,512]{1,0:T(8,128)(2,1)S(1)} %bitcast.16, bf16[512,7168]{1,0:T(8,128)(2,1)S(1)} %bitcast.21, bf16[32,8960]{1,0:T(8,128)(2,1)S(1)} %pad_maximum_fusion.2.refs_0_, ...), custom_call_target="tpu_custom_call" | custom-call | flops 3523215360 | bytes 4587520 | tf_op jit(solution)/shard_map/experts/pallas_call | solution.py:170
  79.1 4.1 %collective-permute-done.22.refs_1_ = bf16[32,8960]{1,0:T(8,128)(2,1)S(1)} collective-permute-done((bf16[32,8960]{1,0:T(8,128)(2,1)S(1)}, bf16[32,8960]{1,0:T(8,128)(2,1)S(1)}, u32[]{:S(2)}, u32[]{:S(2)}) %collective-permute-start.22) | collective-permute-done | bytes 573472 | tf_op jit(solution)/shard_map/ppermute | solution.py:226
  85.2 4.7 %experts.7 = (bf16[64,8960]{1,0:T(8,128)(2,1)S(1)}, bf16[64,8960]{1,0:T(8,128)(2,1)S(1)}) custom-call(bf16[7168,512]{1,0:T(8,128)(2,1)S(1)} %bitcast.12, bf16[7168,512]{1,0:T(8,128)(2,1)S(1)} %bitcast.17, bf16[512,7168]{1,0:T(8,128)(2,1)S(1)} %bitcast.22, bf16[32,8960]{1,0:T(8,128)(2,1)S(1)} %collective-permute-done.19.refs_0_, ...), custom_call_target="tpu_custom_call" | custom-call | flops 3523215360 | bytes 4587520 | tf_op jit(solution)/shard_map/experts/pallas_call | solution.py:170
  90.1 5.4 %collective-permute-done.21 = bf16[32,8960]{1,0:T(8,128)(2,1)S(1)} collective-permute-done((bf16[32,8960]{1,0:T(8,128)(2,1)S(1)}, bf16[32,8960]{1,0:T(8,128)(2,1)S(1)}, u32[]{:S(2)}, u32[]{:S(2)}) %collective-permute-start.21) | collective-permute-done | bytes 573472 | tf_op jit(solution)/shard_map/ppermute | solution.py:226
  95.8 3.5 %collective-permute-start.27 = (bf16[16,8960]{1,0:T(8,128)(2,1)S(1)}, bf16[16,8960]{1,0:T(8,128)(2,1)S(1)}, u32[]{:S(2)}, u32[]{:S(2)}) collective-permute-start(bf16[16,8960]{1,0:T(8,128)(2,1)S(1)} %get-tuple-element.326), channel_id=1, source_target_pairs={{0,28},{4,24},{8,20},{12,16},{16,12},{20,8},{24,4},{28,0},{1,29},{... | collective-permute-start | bytes 860168 | tf_op jit(solution)/shard_map/ppermute | solution.py:223
  100.4 8.0 %collective-permute-done.27.refs_7_ = bf16[16,8960]{1,0:T(8,128)(2,1)S(1)} collective-permute-done((bf16[16,8960]{1,0:T(8,128)(2,1)S(1)}, bf16[16,8960]{1,0:T(8,128)(2,1)S(1)}, u32[]{:S(2)}, u32[]{:S(2)}) %collective-permute-start.27) | collective-permute-done | bytes 286752 | tf_op jit(solution)/shard_map/ppermute | solution.py:223
  108.9 11.5 %collective-permute-start.33 = (bf16[16,8960]{1,0:T(8,128)(2,1)S(1)}, bf16[16,8960]{1,0:T(8,128)(2,1)S(1)}, u32[]{:S(2)}, u32[]{:S(2)}) collective-permute-start(bf16[16,8960]{1,0:T(8,128)(2,1)S(1)} %get-tuple-element.348), channel_id=1, source_target_pairs={{0,12},{4,8},{8,4},{12,0},{16,28},{20,24},{24,20},{28,16},{1,13},{... | collective-permute-start | bytes 860168 | tf_op jit(solution)/shard_map/ppermute | solution.py:223
  120.6 2.9 %collective-permute-start.35 = (bf16[16,8960]{1,0:T(8,128)(2,1)S(1)}, bf16[16,8960]{1,0:T(8,128)(2,1)S(1)}, u32[]{:S(2)}, u32[]{:S(2)}) collective-permute-start(bf16[16,8960]{1,0:T(8,128)(2,1)S(1)} %get-tuple-element.350), channel_id=1, source_target_pairs={{0,16},{4,20},{8,24},{12,28},{16,0},{20,4},{24,8},{28,12},{1,17},{... | collective-permute-start | bytes 860168 | tf_op jit(solution)/shard_map/ppermute | solution.py:223
  123.6 8.3 %collective-permute-done.28 = bf16[32,8960]{1,0:T(8,128)(2,1)S(1)} collective-permute-done((bf16[32,8960]{1,0:T(8,128)(2,1)S(1)}, bf16[32,8960]{1,0:T(8,128)(2,1)S(1)}, u32[]{:S(2)}, u32[]{:S(2)}) %collective-permute-start.28) | collective-permute-done | bytes 573472 | tf_op jit(solution)/shard_map/ppermute | solution.py:226
  135.4 4.6 %collective-permute-done.35.refs_4_ = bf16[16,8960]{1,0:T(8,128)(2,1)S(1)} collective-permute-done((bf16[16,8960]{1,0:T(8,128)(2,1)S(1)}, bf16[16,8960]{1,0:T(8,128)(2,1)S(1)}, u32[]{:S(2)}, u32[]{:S(2)}) %collective-permute-start.35) | collective-permute-done | bytes 286752 | tf_op jit(solution)/shard_map/ppermute | solution.py:223
  140.0 11.1 %collective-permute-done.34.refs_5_ = bf16[16,8960]{1,0:T(8,128)(2,1)S(1)} collective-permute-done((bf16[16,8960]{1,0:T(8,128)(2,1)S(1)}, bf16[16,8960]{1,0:T(8,128)(2,1)S(1)}, u32[]{:S(2)}, u32[]{:S(2)}) %collective-permute-start.34) | collective-permute-done | bytes 286752 | tf_op jit(solution)/shard_map/ppermute | solution.py:223
  151.1 2.5 %combine.1 = bf16[128,7168]{1,0:T(8,128)(2,1)} custom-call(s32[1]{0:T(128)} %bitcast.me_ref, s32[1,128]{1,0:T(1,128)S(1)} %bitcast.24, f32[1,128]{1,0:T(1,128)S(1)} %bitcast.25, bf16[16,8960]{1,0:T(8,128)(2,1)S(1)} %get-tuple-element.366.refs_0_, bf16[16,8960]{1,0:T(8,128)(2,1)S(1)} %collective-permute-done.31.refs_1_, ...), custom_call_target="tpu_custom_call" | custom-call | flops 469762048 | bytes 4587520 | tf_op jit(solution)/shard_map/combine/pallas_call | solution.py:374
  (104 shorter events, 32.3 us)
Async XLA Ops:
  3.4 11.5 %collective-permute-start = (bf16[16,8960]{1,0:T(8,128)(2,1)S(1)}, bf16[16,8960]{1,0:T(8,128)(2,1)S(1)}, u32[]{:S(2)}, u32[]{:S(2)}) collective-permute-start(bf16[16,8960]{1,0:T(8,128)(2,1)S(1)} %get-tuple-element.190), channel_id=1, source_target_pairs={{0,4},{4,0},{8,12},{12,8},{16,20},{20,16},{24,28},{28,24},{1,5},{5... | collective-permute-start | bytes 860168 | tf_op jit(solution)/shard_map/ppermute | solution.py:223
  6.5 11.5 %collective-permute-start.1 = (bf16[16,8960]{1,0:T(8,128)(2,1)S(1)}, bf16[16,8960]{1,0:T(8,128)(2,1)S(1)}, u32[]{:S(2)}, u32[]{:S(2)}) collective-permute-start(bf16[16,8960]{1,0:T(8,128)(2,1)S(1)} %get-tuple-element.199), channel_id=1, source_target_pairs={{0,2},{1,3},{2,0},{3,1},{4,6},{5,7},{6,4},{7,5},{8,10},{9,11},{10,... | collective-permute-start | bytes 860168 | tf_op jit(solution)/shard_map/ppermute | solution.py:226
  8.0 19.7 %collective-permute-start.8 = (bf16[16,8960]{1,0:T(8,128)(2,1)S(1)}, bf16[16,8960]{1,0:T(8,128)(2,1)S(1)}, u32[]{:S(2)}, u32[]{:S(2)}) collective-permute-start(bf16[16,8960]{1,0:T(8,128)(2,1)S(1)} %get-tuple-element.217), channel_id=1, source_target_pairs={{0,24},{4,28},{8,16},{12,20},{16,8},{20,12},{24,0},{28,4},{1,25},{... | collective-permute-start | bytes 860168 | tf_op jit(solution)/shard_map/ppermute | solution.py:223
  11.7 16.1 %collective-permute-start.7 = (bf16[16,8960]{1,0:T(8,128)(2,1)S(1)}, bf16[16,8960]{1,0:T(8,128)(2,1)S(1)}, u32[]{:S(2)}, u32[]{:S(2)}) collective-permute-start(bf16[16,8960]{1,0:T(8,128)(2,1)S(1)} %get-tuple-element.216), channel_id=1, source_target_pairs={{0,28},{4,24},{8,20},{12,16},{16,12},{20,8},{24,4},{28,0},{1,29},{... | collective-permute-start | bytes 860168 | tf_op jit(solution)/shard_map/ppermute | solution.py:223
  11.8 24.6 %collective-permute-start.5 = (bf16[32,8960]{1,0:T(8,128)(2,1)S(1)}, bf16[32,8960]{1,0:T(8,128)(2,1)S(1)}, u32[]{:S(2)}, u32[]{:S(2)}) collective-permute-start(bf16[32,8960]{1,0:T(8,128)(2,1)S(1)} %pad_maximum_fusion), channel_id=1, source_target_pairs={{0,8},{4,12},{8,0},{12,4},{16,24},{20,28},{24,16},{28,20},{1,9},{5... | collective-permute-start | bytes 1720328 | tf_op jit(solution)/shard_map/ppermute | solution.py:223
  18.4 11.9 %collective-permute-start.6 = (bf16[16,8960]{1,0:T(8,128)(2,1)S(1)}, bf16[16,8960]{1,0:T(8,128)(2,1)S(1)}, u32[]{:S(2)}, u32[]{:S(2)}) collective-permute-start(bf16[16,8960]{1,0:T(8,128)(2,1)S(1)} %get-tuple-element.215), channel_id=1, source_target_pairs={{0,4},{4,0},{8,12},{12,8},{16,20},{20,16},{24,28},{28,24},{1,5},{5... | collective-permute-start | bytes 860168 | tf_op jit(solution)/shard_map/ppermute | solution.py:223
  36.6 9.8 %collective-permute-start.9 = (bf16[16,8960]{1,0:T(8,128)(2,1)S(1)}, bf16[16,8960]{1,0:T(8,128)(2,1)S(1)}, u32[]{:S(2)}, u32[]{:S(2)}) collective-permute-start(bf16[16,8960]{1,0:T(8,128)(2,1)S(1)} %collective-permute-done.8), channel_id=1, source_target_pairs={{0,2},{1,3},{2,0},{3,1},{4,6},{5,7},{6,4},{7,5},{8,10},{9,11},{10,... | collective-permute-start | bytes 860168 | tf_op jit(solution)/shard_map/ppermute | solution.py:226
  37.2 14.4 %collective-permute-start.11 = (bf16[16,8960]{1,0:T(8,128)(2,1)S(1)}, bf16[16,8960]{1,0:T(8,128)(2,1)S(1)}, u32[]{:S(2)}, u32[]{:S(2)}) collective-permute-start(bf16[16,8960]{1,0:T(8,128)(2,1)S(1)} %collective-permute-done.7), channel_id=1, source_target_pairs={{0,2},{1,3},{2,0},{3,1},{4,6},{5,7},{6,4},{7,5},{8,10},{9,11},{10,... | collective-permute-start | bytes 860168 | tf_op jit(solution)/shard_map/ppermute | solution.py:226
  38.7 15.3 %collective-permute-start.12 = (bf16[16,8960]{1,0:T(8,128)(2,1)S(1)}, bf16[16,8960]{1,0:T(8,128)(2,1)S(1)}, u32[]{:S(2)}, u32[]{:S(2)}) collective-permute-start(bf16[16,8960]{1,0:T(8,128)(2,1)S(1)} %get-tuple-element.250), channel_id=1, source_target_pairs={{0,4},{4,0},{8,12},{12,8},{16,20},{20,16},{24,28},{28,24},{1,5},{5... | collective-permute-start | bytes 860168 | tf_op jit(solution)/shard_map/ppermute | solution.py:223
  39.2 28.2 %collective-permute-start.19 = (bf16[32,8960]{1,0:T(8,128)(2,1)S(1)}, bf16[32,8960]{1,0:T(8,128)(2,1)S(1)}, u32[]{:S(2)}, u32[]{:S(2)}) collective-permute-start(bf16[32,8960]{1,0:T(8,128)(2,1)S(1)} %pad_maximum_fusion.1), channel_id=1, source_target_pairs={{0,16},{4,20},{8,24},{12,28},{16,0},{20,4},{24,8},{28,12},{1,17},{... | collective-permute-start | bytes 1720328 | tf_op jit(solution)/shard_map/ppermute | solution.py:223
  51.5 9.7 %collective-permute-start.15 = (bf16[16,8960]{1,0:T(8,128)(2,1)S(1)}, bf16[16,8960]{1,0:T(8,128)(2,1)S(1)}, u32[]{:S(2)}, u32[]{:S(2)}) collective-permute-start(bf16[16,8960]{1,0:T(8,128)(2,1)S(1)} %get-tuple-element.258), channel_id=1, source_target_pairs={{0,2},{1,3},{2,0},{3,1},{4,6},{5,7},{6,4},{7,5},{8,10},{9,11},{10,... | collective-permute-start | bytes 860168 | tf_op jit(solution)/shard_map/ppermute | solution.py:226
  54.5 12.2 %collective-permute-start.17 = (bf16[16,8960]{1,0:T(8,128)(2,1)S(1)}, bf16[16,8960]{1,0:T(8,128)(2,1)S(1)}, u32[]{:S(2)}, u32[]{:S(2)}) collective-permute-start(bf16[16,8960]{1,0:T(8,128)(2,1)S(1)} %collective-permute-done.12), channel_id=1, source_target_pairs={{0,2},{1,3},{2,0},{3,1},{4,6},{5,7},{6,4},{7,5},{8,10},{9,11},{10,... | collective-permute-start | bytes 860168 | tf_op jit(solution)/shard_map/ppermute | solution.py:226
  67.4 15.8 %collective-permute-start.22 = (bf16[32,8960]{1,0:T(8,128)(2,1)S(1)}, bf16[32,8960]{1,0:T(8,128)(2,1)S(1)}, u32[]{:S(2)}, u32[]{:S(2)}) collective-permute-start(bf16[32,8960]{1,0:T(8,128)(2,1)S(1)} %collective-permute-done.19.refs_0_), channel_id=1, source_target_pairs={{0,2},{1,3},{2,0},{3,1},{4,6},{5,7},{6,4},{7,5},{8,10},{9,11},{10,... | collective-permute-start | bytes 1720328 | tf_op jit(solution)/shard_map/ppermute | solution.py:226
  77.0 18.5 %collective-permute-start.21 = (bf16[32,8960]{1,0:T(8,128)(2,1)S(1)}, bf16[32,8960]{1,0:T(8,128)(2,1)S(1)}, u32[]{:S(2)}, u32[]{:S(2)}) collective-permute-start(bf16[32,8960]{1,0:T(8,128)(2,1)S(1)} %add_convert_fusion.6), channel_id=1, source_target_pairs={{0,2},{1,3},{2,0},{3,1},{4,6},{5,7},{6,4},{7,5},{8,10},{9,11},{10,... | collective-permute-start | bytes 1720328 | tf_op jit(solution)/shard_map/ppermute | solution.py:226
  83.4 25.0 %collective-permute-start.30 = (bf16[32,8960]{1,0:T(8,128)(2,1)S(1)}, bf16[32,8960]{1,0:T(8,128)(2,1)S(1)}, u32[]{:S(2)}, u32[]{:S(2)}) collective-permute-start(bf16[32,8960]{1,0:T(8,128)(2,1)S(1)} %add_convert_fusion.5), channel_id=1, source_target_pairs={{0,2},{1,3},{2,0},{3,1},{4,6},{5,7},{6,4},{7,5},{8,10},{9,11},{10,... | collective-permute-start | bytes 1720328 | tf_op jit(solution)/shard_map/ppermute | solution.py:226
  95.8 12.6 %collective-permute-start.27 = (bf16[16,8960]{1,0:T(8,128)(2,1)S(1)}, bf16[16,8960]{1,0:T(8,128)(2,1)S(1)}, u32[]{:S(2)}, u32[]{:S(2)}) collective-permute-start(bf16[16,8960]{1,0:T(8,128)(2,1)S(1)} %get-tuple-element.326), channel_id=1, source_target_pairs={{0,28},{4,24},{8,20},{12,16},{16,12},{20,8},{24,4},{28,0},{1,29},{... | collective-permute-start | bytes 860168 | tf_op jit(solution)/shard_map/ppermute | solution.py:223
  99.4 20.9 %collective-permute-start.29 = (bf16[32,8960]{1,0:T(8,128)(2,1)S(1)}, bf16[32,8960]{1,0:T(8,128)(2,1)S(1)}, u32[]{:S(2)}, u32[]{:S(2)}) collective-permute-start(bf16[32,8960]{1,0:T(8,128)(2,1)S(1)} %add_convert_fusion.3), channel_id=1, source_target_pairs={{0,2},{1,3},{2,0},{3,1},{4,6},{5,7},{6,4},{7,5},{8,10},{9,11},{10,... | collective-permute-start | bytes 1720328 | tf_op jit(solution)/shard_map/ppermute | solution.py:226
  100.0 33.7 %collective-permute-start.36 = (bf16[16,8960]{1,0:T(8,128)(2,1)S(1)}, bf16[16,8960]{1,0:T(8,128)(2,1)S(1)}, u32[]{:S(2)}, u32[]{:S(2)}) collective-permute-start(bf16[16,8960]{1,0:T(8,128)(2,1)S(1)} %get-tuple-element.351), channel_id=1, source_target_pairs={{0,24},{4,28},{8,16},{12,20},{16,8},{20,12},{24,0},{28,4},{1,25},{... | collective-permute-start | bytes 860168 | tf_op jit(solution)/shard_map/ppermute | solution.py:223
  108.6 23.3 %collective-permute-start.28 = (bf16[32,8960]{1,0:T(8,128)(2,1)S(1)}, bf16[32,8960]{1,0:T(8,128)(2,1)S(1)}, u32[]{:S(2)}, u32[]{:S(2)}) collective-permute-start(bf16[32,8960]{1,0:T(8,128)(2,1)S(1)} %add_convert_fusion.7), channel_id=1, source_target_pairs={{0,2},{1,3},{2,0},{3,1},{4,6},{5,7},{6,4},{7,5},{8,10},{9,11},{10,... | collective-permute-start | bytes 1720328 | tf_op jit(solution)/shard_map/ppermute | solution.py:226
  108.9 42.2 %collective-permute-start.33 = (bf16[16,8960]{1,0:T(8,128)(2,1)S(1)}, bf16[16,8960]{1,0:T(8,128)(2,1)S(1)}, u32[]{:S(2)}, u32[]{:S(2)}) collective-permute-start(bf16[16,8960]{1,0:T(8,128)(2,1)S(1)} %get-tuple-element.348), channel_id=1, source_target_pairs={{0,12},{4,8},{8,4},{12,0},{16,28},{20,24},{24,20},{28,16},{1,13},{... | collective-permute-start | bytes 860168 | tf_op jit(solution)/shard_map/ppermute | solution.py:223
  120.3 30.8 %collective-permute-start.32 = (bf16[16,8960]{1,0:T(8,128)(2,1)S(1)}, bf16[16,8960]{1,0:T(8,128)(2,1)S(1)}, u32[]{:S(2)}, u32[]{:S(2)}) collective-permute-start(bf16[16,8960]{1,0:T(8,128)(2,1)S(1)} %get-tuple-element.347), channel_id=1, source_target_pairs={{0,8},{4,12},{8,0},{12,4},{16,24},{20,28},{24,16},{28,20},{1,9},{5... | collective-permute-start | bytes 860168 | tf_op jit(solution)/shard_map/ppermute | solution.py:223
  120.6 19.3 %collective-permute-start.35 = (bf16[16,8960]{1,0:T(8,128)(2,1)S(1)}, bf16[16,8960]{1,0:T(8,128)(2,1)S(1)}, u32[]{:S(2)}, u32[]{:S(2)}) collective-permute-start(bf16[16,8960]{1,0:T(8,128)(2,1)S(1)} %get-tuple-element.350), channel_id=1, source_target_pairs={{0,16},{4,20},{8,24},{12,28},{16,0},{20,4},{24,8},{28,12},{1,17},{... | collective-permute-start | bytes 860168 | tf_op jit(solution)/shard_map/ppermute | solution.py:223
  131.9 19.2 %collective-permute-start.34 = (bf16[16,8960]{1,0:T(8,128)(2,1)S(1)}, bf16[16,8960]{1,0:T(8,128)(2,1)S(1)}, u32[]{:S(2)}, u32[]{:S(2)}) collective-permute-start(bf16[16,8960]{1,0:T(8,128)(2,1)S(1)} %get-tuple-element.349), channel_id=1, source_target_pairs={{0,20},{4,16},{8,28},{12,24},{16,4},{20,0},{24,12},{28,8},{1,21},{... | collective-permute-start | bytes 860168 | tf_op jit(solution)/shard_map/ppermute | solution.py:223
  133.8 17.3 %collective-permute-start.31 = (bf16[16,8960]{1,0:T(8,128)(2,1)S(1)}, bf16[16,8960]{1,0:T(8,128)(2,1)S(1)}, u32[]{:S(2)}, u32[]{:S(2)}) collective-permute-start(bf16[16,8960]{1,0:T(8,128)(2,1)S(1)} %get-tuple-element.346), channel_id=1, source_target_pairs={{0,4},{4,0},{8,12},{12,8},{16,20},{20,16},{24,28},{28,24},{1,5},{5... | collective-permute-start | bytes 860168 | tf_op jit(solution)/shard_map/ppermute | solution.py:223
  (22 other events, 162.8 us)

commit v5 on v3

--- a/solution.py
+++ b/solution.py
@@ -14,12 +14,15 @@
 
 
 ORDER = (
-    "S.g30 S.y0 S.x00 S.g1 S.g31 L.g D.y0 S.x01 S.y2 L.u D.x00 D.x01 S.c0 S.c0x L.d D.y2 D.c0 D.c0x "
-    "D.g30 D.g31 D.g1 S.g2 S.x31 S.y1 S.x30 S.x10 D.x30 E.0 S.b0 S.c3 D.x31 D.y1 S.c3x S.x11 D.b0 D.x10 "
-    "D.c3 D.c3x E.3 S.b3 D.x11 S.c1 S.c1x D.g2 S.x2 D.c1x D.b3 D.c1 S.c2 S.r3 E.1 S.b1 D.c2 D.b1 D.x2 "
-    "S.c2x D.c2x E.2 S.b2 D.r3 D.b2 S.h30 S.h31 S.r1 S.r2 D.r1 S.r0 D.h31 S.h1 D.r2 S.h20 S.h21 D.r0 "
-    "S.h0 D.h30 D.h1 D.h20 D.h21 D.h0"
-).split()
+    "S.g31", "S.y0", "S.g30", "S.g1", "S.y2", "S.x00", "L.g", "D.x00", "L.u", "D.y0", "S.x01",
+    "S.c0", "D.x01", "S.c0x", "L.d", "D.c0", "D.g31", "S.x31", "D.g1", "D.y2", "S.y1", "S.g2",
+    "D.c0x", "D.g30", "E.0", "S.x30", "S.b0", "S.x10", "D.y1", "D.x30", "D.b0", "D.x31",
+    "S.c3x", "S.c3", "S.x11", "D.c3", "D.x10", "S.c1", "D.c3x", "E.3", "D.x11", "D.g2", "S.x2",
+    "S.c1x", "S.b3", "D.b3", "S.c2", "D.c1", "S.r31", "D.c1x", "E.1", "S.r30", "S.b1", "D.b1",
+    "D.x2", "S.c2x", "S.r1", "D.c2", "D.c2x", "E.2", "D.r30", "D.r31", "S.b2", "D.b2", "S.h31",
+    "S.h30", "S.r20", "S.r21", "D.h31", "S.r0", "D.r1", "S.h1", "D.r20", "S.h20", "D.r21",
+    "S.h21", "D.r0", "S.h0", "D.h30", "D.h20", "D.h21", "D.h1", "D.h0",
+)
 
 
 def slots_of(target_row, me, groups, main):
@@ -279,10 +282,22 @@
     own = {"00": [outbound[0]]}
     chip = {}
     held = {}
-    got, keep, sums = {}, {}, {}
+    got, keep, sums, done = {}, {}, {}, {}
 
     def expert_rows(chunk, mine, others):
         held[chunk] = [stack(mine)] + [stack(parts) for parts in zip(*others)]
+
+    def part_of(x, n):
+        if len(n) == 1:
+            return x
+        count = x.shape[0] // 2
+        return x[:count] if n[1] == "0" else x[count:]
+
+    def returned(n):
+        first = int(n[0]) * per_chunk
+        if len(n) == 1:
+            return range(first, first + per_chunk)
+        return range(first, first + half) if n[1] == "0" else range(first + half, first + per_chunk)
 
     def start(name):
         kind, n = name[0], name[1:]
@@ -309,11 +324,8 @@
         if kind == "b":
             return [to_core(keep[n][1])]
         if kind == "r":
-            return to_chips_each(sums[n][1:])
-        part = {"0": near, "1": range(per_chunk)}.get(n)
-        if part is None:
-            part = range(half) if n[1] == "0" else range(half, per_chunk)
-        return to_groups([sums[n[0]][0][k] for k in part], [int(n[0]) * per_chunk + k for k in part])
+            return to_chips_each([part_of(x, n) for x in sums[n[0]][1:]])
+        return to_groups(cut(done[n], main), returned(n))
 
     def held_own(n):
         parts = {"0": ("00", "01"), "1": ("10", "11"), "2": ("2",), "3": ("30", "31")}[n]
@@ -344,10 +356,10 @@
             total = [f32(a) + f32(b) for a, b in zip(cut(kept, count), cut(came, count))]
             sums[n] = total[:1] + [x.astype(jnp.bfloat16) for x in total[1:]]
         elif kind == "r":
-            total = sums[n][0]
+            total = part_of(sums[n[0]][0], n)
             for x in got[name]:
                 total = total + f32(x)
-            sums[n] = [cut(total.astype(jnp.bfloat16), main)]
+            done[n] = total.astype(jnp.bfloat16)
 
     flying = {}
     for name in ORDER:
@@ -364,8 +376,8 @@
             got[what] = step(*flying.pop(what))
             finish(what)
 
-    back = [sums["0"][0][0]] + got["h0"] + got["h1"]
-    for part in ("20", "21", "30", "31"):
+    back = []
+    for part in ("0", "1", "20", "21", "30", "31"):
         back += got["h" + part]
 
     return pl.pallas_call(

time: 155 us -> 149 us (0.961)
  waiting for transfers between devices: 83.9 us -> 76.4 us
  starting transfers between devices: 37.8 us -> 39.6 us
    ppermute x12, waiting for transfers between devices: 8.77 us -> 3.92 us  [to_core(): return lax.ppermute(x, 'inner', [(i, i ^ 1) for i in range(inner)])]
    ppermute x11 -> x13, starting transfers between devices: 10.9 us -> 14.5 us  [to_chip(): return lax.ppermute(x, 'inner', [(i, i ^ 2 * offset) for i in range(inner)])]
    ppermute x11 -> x13, waiting for transfers between devices: 49.2 us -> 45.9 us  [to_chip(): return lax.ppermute(x, 'inner', [(i, i ^ 2 * offset) for i in range(inner)])]
    ppermute x14, starting transfers between devices: 24.6 us -> 22.9 us  [to_group(): return lax.ppermute(x, 'group', [(i, i ^ offset) for i in range(groups)])]
  transfers between devices with their start and end apart: 37 -> 39, of which waited for: 22 -> 22; matrix products, arithmetic and copies ran while one was open for 1% -> 1% of each run, Pallas kernels for 12% -> 13%
where the time goes in v5:
time: 149 us
  waiting for transfers between devices  76.4 us (51%)
  starting transfers between devices  39.6 us (27%)
  Pallas kernels  22.7 us (15%)
  local copies, waits for them, and re-layouts  7.77 us (5%)
  other arithmetic  1.73 us (1%)
    ppermute x13, waiting for transfers between devices, to_chip(): return lax.ppermute(x, 'inner', [(i, i ^ 2 * offset) for i in range(inner)])  45.9 us
    ppermute x14, waiting for transfers between devices, to_group(): return lax.ppermute(x, 'group', [(i, i ^ offset) for i in range(groups)])  26.6 us
    ppermute x14, starting transfers between devices, to_group(): return lax.ppermute(x, 'group', [(i, i ^ offset) for i in range(groups)])  22.9 us
    pallas_call x4, Pallas kernels, run_experts(): pl.pallas_call(functools.partial(expert_kernel, main, parts), in_specs=[v...  18.9 us
    ppermute x13, starting transfers between devices, to_chip(): return lax.ppermute(x, 'inner', [(i, i ^ 2 * offset) for i in range(inner)])  14.5 us
    unnamed x23, local copies, waits for them, and re-layouts  7.47 us
    ppermute x12, waiting for transfers between devices, to_core(): return lax.ppermute(x, 'inner', [(i, i ^ 1) for i in range(inner)])  3.92 us
  transfers between devices with their start and end apart: 39, of which 22 were waited for; matrix products, arithmetic and copies ran while one was open for 1% of the time, Pallas kernels for 13%

profile of v5, /device:TPU:0, one launch (start us, length us, event | category | flops | bytes accessed | tf_op | source)
XLA Modules:
  0.0 148.6 jit_solution(5208461232463790340)
XLA Ops:
  3.5 3.0 %collective-permute-start.1 = (bf16[16,8960]{1,0:T(8,128)(2,1)S(1)}, bf16[16,8960]{1,0:T(8,128)(2,1)S(1)}, u32[]{:S(2)}, u32[]{:S(2)}) collective-permute-start(bf16[16,8960]{1,0:T(8,128)(2,1)S(1)} %get-tuple-element.208), channel_id=1, source_target_pairs={{0,2},{1,3},{2,0},{3,1},{4,6},{5,7},{6,4},{7,5},{8,10},{9,11},{10,... | collective-permute-start | bytes 860168 | tf_op jit(solution)/shard_map/ppermute | solution.py:226
  8.0 3.5 %collective-permute-start.7 = (bf16[16,8960]{1,0:T(8,128)(2,1)S(1)}, bf16[16,8960]{1,0:T(8,128)(2,1)S(1)}, u32[]{:S(2)}, u32[]{:S(2)}) collective-permute-start(bf16[16,8960]{1,0:T(8,128)(2,1)S(1)} %get-tuple-element.225), channel_id=1, source_target_pairs={{0,28},{4,24},{8,20},{12,16},{16,12},{20,8},{24,4},{28,0},{1,29},{... | collective-permute-start | bytes 860168 | tf_op jit(solution)/shard_map/ppermute | solution.py:223
  13.1 3.1 %copy-done = bf16[1,7168,512]{2,1,0:T(8,128)(2,1)S(1)} copy-done((bf16[1,7168,512]{2,1,0:T(8,128)(2,1)S(1)}, bf16[1,7168,512]{2,1,0:T(8,128)(2,1)}, u32[]{:S(2)}) %copy-start) | copy-done | bytes 7340056
  19.3 3.1 %collective-permute-done = bf16[16,8960]{1,0:T(8,128)(2,1)S(1)} collective-permute-done((bf16[16,8960]{1,0:T(8,128)(2,1)S(1)}, bf16[16,8960]{1,0:T(8,128)(2,1)S(1)}, u32[]{:S(2)}, u32[]{:S(2)}) %collective-permute-start) | collective-permute-done | bytes 286752 | tf_op jit(solution)/shard_map/ppermute | solution.py:223
  22.5 6.5 %collective-permute-done.2 = bf16[16,8960]{1,0:T(8,128)(2,1)S(1)} collective-permute-done((bf16[16,8960]{1,0:T(8,128)(2,1)S(1)}, bf16[16,8960]{1,0:T(8,128)(2,1)S(1)}, u32[]{:S(2)}, u32[]{:S(2)}) %collective-permute-start.2) | collective-permute-done | bytes 286752 | tf_op jit(solution)/shard_map/ppermute | solution.py:226
  34.6 2.4 %collective-permute-done.8 = bf16[16,8960]{1,0:T(8,128)(2,1)S(1)} collective-permute-done((bf16[16,8960]{1,0:T(8,128)(2,1)S(1)}, bf16[16,8960]{1,0:T(8,128)(2,1)S(1)}, u32[]{:S(2)}, u32[]{:S(2)}) %collective-permute-start.8) | collective-permute-done | bytes 286752 | tf_op jit(solution)/shard_map/ppermute | solution.py:223
  37.0 4.7 %experts.4 = (bf16[64,8960]{1,0:T(8,128)(2,1)S(1)}, bf16[64,8960]{1,0:T(8,128)(2,1)S(1)}) custom-call(bf16[7168,512]{1,0:T(8,128)(2,1)S(1)} %bitcast.9, bf16[7168,512]{1,0:T(8,128)(2,1)S(1)} %bitcast.14, bf16[512,7168]{1,0:T(8,128)(2,1)S(1)} %bitcast.19, bf16[32,8960]{1,0:T(8,128)(2,1)S(1)} %constant_dynamic-update-slice_fusion.refs_0_, ...), custom_call_target="tpu_custom_call" | custom-call | flops 3523215360 | bytes 4587520 | tf_op jit(solution)/shard_map/experts/pallas_call | solution.py:170
  44.0 7.6 %collective-permute-done.10 = bf16[16,8960]{1,0:T(8,128)(2,1)S(1)} collective-permute-done((bf16[16,8960]{1,0:T(8,128)(2,1)S(1)}, bf16[16,8960]{1,0:T(8,128)(2,1)S(1)}, u32[]{:S(2)}, u32[]{:S(2)}) %collective-permute-start.10) | collective-permute-done | bytes 286752 | tf_op jit(solution)/shard_map/ppermute | solution.py:226
  54.6 4.7 %experts.5 = (bf16[64,8960]{1,0:T(8,128)(2,1)S(1)}, bf16[64,8960]{1,0:T(8,128)(2,1)S(1)}) custom-call(bf16[7168,512]{1,0:T(8,128)(2,1)S(1)} %bitcast.10, bf16[7168,512]{1,0:T(8,128)(2,1)S(1)} %bitcast.15, bf16[512,7168]{1,0:T(8,128)(2,1)S(1)} %bitcast.20, bf16[32,8960]{1,0:T(8,128)(2,1)S(1)} %constant_dynamic-update-slice_fusion.4.refs_0_, ...), custom_call_target="tpu_custom_call" | custom-call | flops 3523215360 | bytes 4587520 | tf_op jit(solution)/shard_map/experts/pallas_call | solution.py:170
  64.4 4.7 %experts.6 = (bf16[64,8960]{1,0:T(8,128)(2,1)S(1)}, bf16[64,8960]{1,0:T(8,128)(2,1)S(1)}) custom-call(bf16[7168,512]{1,0:T(8,128)(2,1)S(1)} %bitcast.11, bf16[7168,512]{1,0:T(8,128)(2,1)S(1)} %bitcast.16, bf16[512,7168]{1,0:T(8,128)(2,1)S(1)} %bitcast.21, bf16[32,8960]{1,0:T(8,128)(2,1)S(1)} %pad_maximum_fusion.2.refs_0_, ...), custom_call_target="tpu_custom_call" | custom-call | flops 3523215360 | bytes 4587520 | tf_op jit(solution)/shard_map/experts/pallas_call | solution.py:170
  72.0 5.9 %collective-permute-done.23.refs_1_ = bf16[32,8960]{1,0:T(8,128)(2,1)S(1)} collective-permute-done((bf16[32,8960]{1,0:T(8,128)(2,1)S(1)}, bf16[32,8960]{1,0:T(8,128)(2,1)S(1)}, u32[]{:S(2)}, u32[]{:S(2)}) %collective-permute-start.23) | collective-permute-done | bytes 573472 | tf_op jit(solution)/shard_map/ppermute | solution.py:226
  79.9 4.7 %experts.7 = (bf16[64,8960]{1,0:T(8,128)(2,1)S(1)}, bf16[64,8960]{1,0:T(8,128)(2,1)S(1)}) custom-call(bf16[7168,512]{1,0:T(8,128)(2,1)S(1)} %bitcast.12, bf16[7168,512]{1,0:T(8,128)(2,1)S(1)} %bitcast.17, bf16[512,7168]{1,0:T(8,128)(2,1)S(1)} %bitcast.22, bf16[32,8960]{1,0:T(8,128)(2,1)S(1)} %collective-permute-done.18.refs_0_, ...), custom_call_target="tpu_custom_call" | custom-call | flops 3523215360 | bytes 4587520 | tf_op jit(solution)/shard_map/experts/pallas_call | solution.py:170
  84.9 5.4 %collective-permute-done.20 = bf16[16,8960]{1,0:T(8,128)(2,1)S(1)} collective-permute-done((bf16[16,8960]{1,0:T(8,128)(2,1)S(1)}, bf16[16,8960]{1,0:T(8,128)(2,1)S(1)}, u32[]{:S(2)}, u32[]{:S(2)}) %collective-permute-start.20) | collective-permute-done | bytes 286752 | tf_op jit(solution)/shard_map/ppermute | solution.py:226
  90.3 5.1 %collective-permute-start.28 = (bf16[16,8960]{1,0:T(8,128)(2,1)S(1)}, bf16[16,8960]{1,0:T(8,128)(2,1)S(1)}, u32[]{:S(2)}, u32[]{:S(2)}) collective-permute-start(bf16[16,8960]{1,0:T(8,128)(2,1)S(1)} %get-tuple-element.337), channel_id=1, source_target_pairs={{0,28},{4,24},{8,20},{12,16},{16,12},{20,8},{24,4},{28,0},{1,29},{... | collective-permute-start | bytes 860168 | tf_op jit(solution)/shard_map/ppermute | solution.py:223
  97.9 4.9 %collective-permute-done.28.refs_7_ = bf16[16,8960]{1,0:T(8,128)(2,1)S(1)} collective-permute-done((bf16[16,8960]{1,0:T(8,128)(2,1)S(1)}, bf16[16,8960]{1,0:T(8,128)(2,1)S(1)}, u32[]{:S(2)}, u32[]{:S(2)}) %collective-permute-start.28) | collective-permute-done | bytes 286752 | tf_op jit(solution)/shard_map/ppermute | solution.py:223
  103.0 5.6 %collective-permute-done.31 = bf16[16,8960]{1,0:T(8,128)(2,1)S(1)} collective-permute-done((bf16[16,8960]{1,0:T(8,128)(2,1)S(1)}, bf16[16,8960]{1,0:T(8,128)(2,1)S(1)}, u32[]{:S(2)}, u32[]{:S(2)}) %collective-permute-start.31) | collective-permute-done | bytes 286752 | tf_op jit(solution)/shard_map/ppermute | solution.py:226
  108.7 5.2 %collective-permute-done.30 = bf16[16,8960]{1,0:T(8,128)(2,1)S(1)} collective-permute-done((bf16[16,8960]{1,0:T(8,128)(2,1)S(1)}, bf16[16,8960]{1,0:T(8,128)(2,1)S(1)}, u32[]{:S(2)}, u32[]{:S(2)}) %collective-permute-start.30) | collective-permute-done | bytes 286752 | tf_op jit(solution)/shard_map/ppermute | solution.py:226
  116.0 2.4 %collective-permute-start.36 = (bf16[16,8960]{1,0:T(8,128)(2,1)S(1)}, bf16[16,8960]{1,0:T(8,128)(2,1)S(1)}, u32[]{:S(2)}, u32[]{:S(2)}) collective-permute-start(bf16[16,8960]{1,0:T(8,128)(2,1)S(1)} %fusion.1), channel_id=1, source_target_pairs={{0,20},{4,16},{8,28},{12,24},{16,4},{20,0},{24,12},{28,8},{1,21},{... | collective-permute-start | bytes 860168 | tf_op jit(solution)/shard_map/ppermute | solution.py:223
  118.4 2.7 %collective-permute-start.35 = (bf16[16,8960]{1,0:T(8,128)(2,1)S(1)}, bf16[16,8960]{1,0:T(8,128)(2,1)S(1)}, u32[]{:S(2)}, u32[]{:S(2)}) collective-permute-start(bf16[16,8960]{1,0:T(8,128)(2,1)S(1)} %get-tuple-element.365), channel_id=1, source_target_pairs={{0,12},{4,8},{8,4},{12,0},{16,28},{20,24},{24,20},{28,16},{1,13},{... | collective-permute-start | bytes 860168 | tf_op jit(solution)/shard_map/ppermute | solution.py:223
  121.1 7.0 %collective-permute-done.29 = bf16[32,8960]{1,0:T(8,128)(2,1)S(1)} collective-permute-done((bf16[32,8960]{1,0:T(8,128)(2,1)S(1)}, bf16[32,8960]{1,0:T(8,128)(2,1)S(1)}, u32[]{:S(2)}, u32[]{:S(2)}) %collective-permute-start.29) | collective-permute-done | bytes 573472 | tf_op jit(solution)/shard_map/ppermute | solution.py:226
  131.0 7.1 %collective-permute-done.37.refs_4_ = bf16[16,8960]{1,0:T(8,128)(2,1)S(1)} collective-permute-done((bf16[16,8960]{1,0:T(8,128)(2,1)S(1)}, bf16[16,8960]{1,0:T(8,128)(2,1)S(1)}, u32[]{:S(2)}, u32[]{:S(2)}) %collective-permute-start.37) | collective-permute-done | bytes 286752 | tf_op jit(solution)/shard_map/ppermute | solution.py:223
  138.1 4.9 %collective-permute-done.36.refs_5_ = bf16[16,8960]{1,0:T(8,128)(2,1)S(1)} collective-permute-done((bf16[16,8960]{1,0:T(8,128)(2,1)S(1)}, bf16[16,8960]{1,0:T(8,128)(2,1)S(1)}, u32[]{:S(2)}, u32[]{:S(2)}) %collective-permute-start.36) | collective-permute-done | bytes 286752 | tf_op jit(solution)/shard_map/ppermute | solution.py:223
  143.0 3.0 %collective-permute-done.34.refs_2_ = bf16[16,8960]{1,0:T(8,128)(2,1)S(1)} collective-permute-done((bf16[16,8960]{1,0:T(8,128)(2,1)S(1)}, bf16[16,8960]{1,0:T(8,128)(2,1)S(1)}, u32[]{:S(2)}, u32[]{:S(2)}) %collective-permute-start.34) | collective-permute-done | bytes 286752 | tf_op jit(solution)/shard_map/ppermute | solution.py:223
  146.1 2.5 %combine.1 = bf16[128,7168]{1,0:T(8,128)(2,1)} custom-call(s32[1]{0:T(128)} %bitcast.me_ref, s32[1,128]{1,0:T(1,128)S(1)} %bitcast.24, f32[1,128]{1,0:T(1,128)S(1)} %bitcast.25, bf16[16,8960]{1,0:T(8,128)(2,1)S(1)} %get-tuple-element.374.refs_0_, bf16[16,8960]{1,0:T(8,128)(2,1)S(1)} %collective-permute-done.33.refs_1_, ...), custom_call_target="tpu_custom_call" | custom-call | flops 469762048 | bytes 4587520 | tf_op jit(solution)/shard_map/combine/pallas_call | solution.py:383
  (109 shorter events, 38.3 us)
Async XLA Ops:
  3.5 12.7 %collective-permute-start.1 = (bf16[16,8960]{1,0:T(8,128)(2,1)S(1)}, bf16[16,8960]{1,0:T(8,128)(2,1)S(1)}, u32[]{:S(2)}, u32[]{:S(2)}) collective-permute-start(bf16[16,8960]{1,0:T(8,128)(2,1)S(1)} %get-tuple-element.208), channel_id=1, source_target_pairs={{0,2},{1,3},{2,0},{3,1},{4,6},{5,7},{6,4},{7,5},{8,10},{9,11},{10,... | collective-permute-start | bytes 860168 | tf_op jit(solution)/shard_map/ppermute | solution.py:226
  6.5 15.9 %collective-permute-start = (bf16[16,8960]{1,0:T(8,128)(2,1)S(1)}, bf16[16,8960]{1,0:T(8,128)(2,1)S(1)}, u32[]{:S(2)}, u32[]{:S(2)}) collective-permute-start(bf16[16,8960]{1,0:T(8,128)(2,1)S(1)} %get-tuple-element.199), channel_id=1, source_target_pairs={{0,4},{4,0},{8,12},{12,8},{16,20},{20,16},{24,28},{28,24},{1,5},{5... | collective-permute-start | bytes 860168 | tf_op jit(solution)/shard_map/ppermute | solution.py:223
  8.0 23.1 %collective-permute-start.7 = (bf16[16,8960]{1,0:T(8,128)(2,1)S(1)}, bf16[16,8960]{1,0:T(8,128)(2,1)S(1)}, u32[]{:S(2)}, u32[]{:S(2)}) collective-permute-start(bf16[16,8960]{1,0:T(8,128)(2,1)S(1)} %get-tuple-element.225), channel_id=1, source_target_pairs={{0,28},{4,24},{8,20},{12,16},{16,12},{20,8},{24,4},{28,0},{1,29},{... | collective-permute-start | bytes 860168 | tf_op jit(solution)/shard_map/ppermute | solution.py:223
  11.5 20.4 %collective-permute-start.6 = (bf16[32,8960]{1,0:T(8,128)(2,1)S(1)}, bf16[32,8960]{1,0:T(8,128)(2,1)S(1)}, u32[]{:S(2)}, u32[]{:S(2)}) collective-permute-start(bf16[32,8960]{1,0:T(8,128)(2,1)S(1)} %pad_maximum_fusion), channel_id=1, source_target_pairs={{0,8},{4,12},{8,0},{12,4},{16,24},{20,28},{24,16},{28,20},{1,9},{5... | collective-permute-start | bytes 1720328 | tf_op jit(solution)/shard_map/ppermute | solution.py:223
  11.5 20.4 %collective-permute-start.5 = (bf16[16,8960]{1,0:T(8,128)(2,1)S(1)}, bf16[16,8960]{1,0:T(8,128)(2,1)S(1)}, u32[]{:S(2)}, u32[]{:S(2)}) collective-permute-start(bf16[16,8960]{1,0:T(8,128)(2,1)S(1)} %get-tuple-element.223), channel_id=1, source_target_pairs={{0,4},{4,0},{8,12},{12,8},{16,20},{20,16},{24,28},{28,24},{1,5},{5... | collective-permute-start | bytes 860168 | tf_op jit(solution)/shard_map/ppermute | solution.py:223
  16.2 20.8 %collective-permute-start.8 = (bf16[16,8960]{1,0:T(8,128)(2,1)S(1)}, bf16[16,8960]{1,0:T(8,128)(2,1)S(1)}, u32[]{:S(2)}, u32[]{:S(2)}) collective-permute-start(bf16[16,8960]{1,0:T(8,128)(2,1)S(1)} %get-tuple-element.235), channel_id=1, source_target_pairs={{0,24},{4,28},{8,16},{12,20},{16,8},{20,12},{24,0},{28,4},{1,25},{... | collective-permute-start | bytes 860168 | tf_op jit(solution)/shard_map/ppermute | solution.py:223
  32.1 9.9 %collective-permute-start.11 = (bf16[16,8960]{1,0:T(8,128)(2,1)S(1)}, bf16[16,8960]{1,0:T(8,128)(2,1)S(1)}, u32[]{:S(2)}, u32[]{:S(2)}) collective-permute-start(bf16[16,8960]{1,0:T(8,128)(2,1)S(1)} %get-tuple-element.249), channel_id=1, source_target_pairs={{0,4},{4,0},{8,12},{12,8},{16,20},{20,16},{24,28},{28,24},{1,5},{5... | collective-permute-start | bytes 860168 | tf_op jit(solution)/shard_map/ppermute | solution.py:223
  33.5 18.0 %collective-permute-start.12 = (bf16[16,8960]{1,0:T(8,128)(2,1)S(1)}, bf16[16,8960]{1,0:T(8,128)(2,1)S(1)}, u32[]{:S(2)}, u32[]{:S(2)}) collective-permute-start(bf16[16,8960]{1,0:T(8,128)(2,1)S(1)} %collective-permute-done.7), channel_id=1, source_target_pairs={{0,2},{1,3},{2,0},{3,1},{4,6},{5,7},{6,4},{7,5},{8,10},{9,11},{10,... | collective-permute-start | bytes 860168 | tf_op jit(solution)/shard_map/ppermute | solution.py:226
  34.2 27.3 %collective-permute-start.18 = (bf16[32,8960]{1,0:T(8,128)(2,1)S(1)}, bf16[32,8960]{1,0:T(8,128)(2,1)S(1)}, u32[]{:S(2)}, u32[]{:S(2)}) collective-permute-start(bf16[32,8960]{1,0:T(8,128)(2,1)S(1)} %pad_maximum_fusion.1), channel_id=1, source_target_pairs={{0,16},{4,20},{8,24},{12,28},{16,0},{20,4},{24,8},{28,12},{1,17},{... | collective-permute-start | bytes 1720328 | tf_op jit(solution)/shard_map/ppermute | solution.py:223
  42.0 12.7 %collective-permute-start.15 = (bf16[16,8960]{1,0:T(8,128)(2,1)S(1)}, bf16[16,8960]{1,0:T(8,128)(2,1)S(1)}, u32[]{:S(2)}, u32[]{:S(2)}) collective-permute-start(bf16[16,8960]{1,0:T(8,128)(2,1)S(1)} %get-tuple-element.268), channel_id=1, source_target_pairs={{0,2},{1,3},{2,0},{3,1},{4,6},{5,7},{6,4},{7,5},{8,10},{9,11},{10,... | collective-permute-start | bytes 860168 | tf_op jit(solution)/shard_map/ppermute | solution.py:226
  62.1 15.8 %collective-permute-start.23 = (bf16[32,8960]{1,0:T(8,128)(2,1)S(1)}, bf16[32,8960]{1,0:T(8,128)(2,1)S(1)}, u32[]{:S(2)}, u32[]{:S(2)}) collective-permute-start(bf16[32,8960]{1,0:T(8,128)(2,1)S(1)} %collective-permute-done.18.refs_0_), channel_id=1, source_target_pairs={{0,2},{1,3},{2,0},{3,1},{4,6},{5,7},{6,4},{7,5},{8,10},{9,11},{10,... | collective-permute-start | bytes 1720328 | tf_op jit(solution)/shard_map/ppermute | solution.py:226
  69.9 15.0 %collective-permute-start.22 = (bf16[16,8960]{1,0:T(8,128)(2,1)S(1)}, bf16[16,8960]{1,0:T(8,128)(2,1)S(1)}, u32[]{:S(2)}, u32[]{:S(2)}) collective-permute-start(bf16[16,8960]{1,0:T(8,128)(2,1)S(1)} %get-tuple-element.309), channel_id=1, source_target_pairs={{0,2},{1,3},{2,0},{3,1},{4,6},{5,7},{6,4},{7,5},{8,10},{9,11},{10,... | collective-permute-start | bytes 860168 | tf_op jit(solution)/shard_map/ppermute | solution.py:226
  71.4 18.8 %collective-permute-start.20 = (bf16[16,8960]{1,0:T(8,128)(2,1)S(1)}, bf16[16,8960]{1,0:T(8,128)(2,1)S(1)}, u32[]{:S(2)}, u32[]{:S(2)}) collective-permute-start(bf16[16,8960]{1,0:T(8,128)(2,1)S(1)} %get-tuple-element.296), channel_id=1, source_target_pairs={{0,2},{1,3},{2,0},{3,1},{4,6},{5,7},{6,4},{7,5},{8,10},{9,11},{10,... | collective-permute-start | bytes 860168 | tf_op jit(solution)/shard_map/ppermute | solution.py:226
  78.1 24.7 %collective-permute-start.32 = (bf16[32,8960]{1,0:T(8,128)(2,1)S(1)}, bf16[32,8960]{1,0:T(8,128)(2,1)S(1)}, u32[]{:S(2)}, u32[]{:S(2)}) collective-permute-start(bf16[32,8960]{1,0:T(8,128)(2,1)S(1)} %add_convert_fusion.3), channel_id=1, source_target_pairs={{0,2},{1,3},{2,0},{3,1},{4,6},{5,7},{6,4},{7,5},{8,10},{9,11},{10,... | collective-permute-start | bytes 1720328 | tf_op jit(solution)/shard_map/ppermute | solution.py:226
  90.3 12.4 %collective-permute-start.28 = (bf16[16,8960]{1,0:T(8,128)(2,1)S(1)}, bf16[16,8960]{1,0:T(8,128)(2,1)S(1)}, u32[]{:S(2)}, u32[]{:S(2)}) collective-permute-start(bf16[16,8960]{1,0:T(8,128)(2,1)S(1)} %get-tuple-element.337), channel_id=1, source_target_pairs={{0,28},{4,24},{8,20},{12,16},{16,12},{20,8},{24,4},{28,0},{1,29},{... | collective-permute-start | bytes 860168 | tf_op jit(solution)/shard_map/ppermute | solution.py:223
  95.8 12.9 %collective-permute-start.31 = (bf16[16,8960]{1,0:T(8,128)(2,1)S(1)}, bf16[16,8960]{1,0:T(8,128)(2,1)S(1)}, u32[]{:S(2)}, u32[]{:S(2)}) collective-permute-start(bf16[16,8960]{1,0:T(8,128)(2,1)S(1)} %get-tuple-element.348), channel_id=1, source_target_pairs={{0,2},{1,3},{2,0},{3,1},{4,6},{5,7},{6,4},{7,5},{8,10},{9,11},{10,... | collective-permute-start | bytes 860168 | tf_op jit(solution)/shard_map/ppermute | solution.py:226
  96.2 17.8 %collective-permute-start.30 = (bf16[16,8960]{1,0:T(8,128)(2,1)S(1)}, bf16[16,8960]{1,0:T(8,128)(2,1)S(1)}, u32[]{:S(2)}, u32[]{:S(2)}) collective-permute-start(bf16[16,8960]{1,0:T(8,128)(2,1)S(1)} %get-tuple-element.347), channel_id=1, source_target_pairs={{0,2},{1,3},{2,0},{3,1},{4,6},{5,7},{6,4},{7,5},{8,10},{9,11},{10,... | collective-permute-start | bytes 860168 | tf_op jit(solution)/shard_map/ppermute | solution.py:226
  97.9 32.5 %collective-permute-start.38 = (bf16[16,8960]{1,0:T(8,128)(2,1)S(1)}, bf16[16,8960]{1,0:T(8,128)(2,1)S(1)}, u32[]{:S(2)}, u32[]{:S(2)}) collective-permute-start(bf16[16,8960]{1,0:T(8,128)(2,1)S(1)} %get-tuple-element.368), channel_id=1, source_target_pairs={{0,24},{4,28},{8,16},{12,20},{16,8},{20,12},{24,0},{28,4},{1,25},{... | collective-permute-start | bytes 860168 | tf_op jit(solution)/shard_map/ppermute | solution.py:223
  113.9 14.1 %collective-permute-start.29 = (bf16[32,8960]{1,0:T(8,128)(2,1)S(1)}, bf16[32,8960]{1,0:T(8,128)(2,1)S(1)}, u32[]{:S(2)}, u32[]{:S(2)}) collective-permute-start(bf16[32,8960]{1,0:T(8,128)(2,1)S(1)} %add_convert_fusion.5), channel_id=1, source_target_pairs={{0,2},{1,3},{2,0},{3,1},{4,6},{5,7},{6,4},{7,5},{8,10},{9,11},{10,... | collective-permute-start | bytes 1720328 | tf_op jit(solution)/shard_map/ppermute | solution.py:226
  115.5 22.6 %collective-permute-start.37 = (bf16[16,8960]{1,0:T(8,128)(2,1)S(1)}, bf16[16,8960]{1,0:T(8,128)(2,1)S(1)}, u32[]{:S(2)}, u32[]{:S(2)}) collective-permute-start(bf16[16,8960]{1,0:T(8,128)(2,1)S(1)} %fusion), channel_id=1, source_target_pairs={{0,16},{4,20},{8,24},{12,28},{16,0},{20,4},{24,8},{28,12},{1,17},{... | collective-permute-start | bytes 860168 | tf_op jit(solution)/shard_map/ppermute | solution.py:223
  116.0 27.0 %collective-permute-start.36 = (bf16[16,8960]{1,0:T(8,128)(2,1)S(1)}, bf16[16,8960]{1,0:T(8,128)(2,1)S(1)}, u32[]{:S(2)}, u32[]{:S(2)}) collective-permute-start(bf16[16,8960]{1,0:T(8,128)(2,1)S(1)} %fusion.1), channel_id=1, source_target_pairs={{0,20},{4,16},{8,28},{12,24},{16,4},{20,0},{24,12},{28,8},{1,21},{... | collective-permute-start | bytes 860168 | tf_op jit(solution)/shard_map/ppermute | solution.py:223
  118.4 24.6 %collective-permute-start.35 = (bf16[16,8960]{1,0:T(8,128)(2,1)S(1)}, bf16[16,8960]{1,0:T(8,128)(2,1)S(1)}, u32[]{:S(2)}, u32[]{:S(2)}) collective-permute-start(bf16[16,8960]{1,0:T(8,128)(2,1)S(1)} %get-tuple-element.365), channel_id=1, source_target_pairs={{0,12},{4,8},{8,4},{12,0},{16,28},{20,24},{24,20},{28,16},{1,13},{... | collective-permute-start | bytes 860168 | tf_op jit(solution)/shard_map/ppermute | solution.py:223
  128.1 18.0 %collective-permute-start.34 = (bf16[16,8960]{1,0:T(8,128)(2,1)S(1)}, bf16[16,8960]{1,0:T(8,128)(2,1)S(1)}, u32[]{:S(2)}, u32[]{:S(2)}) collective-permute-start(bf16[16,8960]{1,0:T(8,128)(2,1)S(1)} %get-tuple-element.364), channel_id=1, source_target_pairs={{0,8},{4,12},{8,0},{12,4},{16,24},{20,28},{24,16},{28,20},{1,9},{5... | collective-permute-start | bytes 860168 | tf_op jit(solution)/shard_map/ppermute | solution.py:223
  130.4 15.7 %collective-permute-start.33 = (bf16[16,8960]{1,0:T(8,128)(2,1)S(1)}, bf16[16,8960]{1,0:T(8,128)(2,1)S(1)}, u32[]{:S(2)}, u32[]{:S(2)}) collective-permute-start(bf16[16,8960]{1,0:T(8,128)(2,1)S(1)} %get-tuple-element.363), channel_id=1, source_target_pairs={{0,4},{4,0},{8,12},{12,8},{16,20},{20,16},{24,28},{28,24},{1,5},{5... | collective-permute-start | bytes 860168 | tf_op jit(solution)/shard_map/ppermute | solution.py:223
  (24 other events, 151.8 us)

commit v6 on v5

--- a/solution.py
+++ b/solution.py
@@ -73,11 +73,11 @@
 
 
 def combine_kernel(groups, main, me_ref, target_ref, scale_ref, *refs):
-    back_refs, out_ref = refs[:-2], refs[-1]
+    back_refs, (_, out_hbm, out_ref, sems) = refs[:-4], refs[-4:]
     unit = main // FOLD
     rows = groups * main
-    tok, width = out_ref.shape
-    piece = width // FOLD
+    tok, piece = out_ref.shape[1:]
+    width = piece * FOLD
     main_slot, tail_slot = slots_of(target_ref[...], me_ref[0], groups, main)
     pick_main = onehot_rows(main_slot, rows)
     square = lax.broadcasted_iota(jnp.int32, (tok, tok), 0) == lax.broadcasted_iota(
@@ -93,6 +93,7 @@
 
     tail = joined(slice(width, width + piece))
     over_slots = (((0,), (0,)), ((), ()))
+    stores = []
     for q in range(FOLD):
         columns = slice(q * piece, (q + 1) * piece)
         value = lax.dot_general(
@@ -104,7 +105,11 @@
             over_slots,
             preferred_element_type=jnp.float32,
         )
-        out_ref[:, columns] = (scale * value).astype(jnp.bfloat16)
+        out_ref[q] = (scale * value).astype(jnp.bfloat16)
+        stores.append(pltpu.make_async_copy(out_ref.at[q], out_hbm.at[:, columns], sems.at[q]))
+        stores[q].start()
+    for store in stores:
+        store.wait()
 
 
 def expert_kernel(main, parts, gate_ref, up_ref, down_ref, *refs):
@@ -383,8 +388,12 @@
     return pl.pallas_call(
         functools.partial(combine_kernel, groups, main),
         in_specs=[scalar] + [vmem] * (2 + groups) + [pl.BlockSpec(memory_space=pl.ANY)],
-        out_specs=vmem,
+        out_specs=pl.BlockSpec(memory_space=pltpu.HBM),
         out_shape=jax.ShapeDtypeStruct((tok_count, width), jnp.bfloat16),
+        scratch_shapes=[
+            pltpu.VMEM((FOLD, tok_count, width // FOLD), jnp.bfloat16),
+            pltpu.SemaphoreType.DMA((FOLD,)),
+        ],
         compiler_params=pltpu.CompilerParams(vmem_limit_bytes=VMEM_LIMIT),
         cost_estimate=pl.CostEstimate(
             flops=4 * tok_count * tok_count * width,

time: 149 us -> 149 us (level)
  no operation moved by 1% of the time
where the time goes in v6:
time: 149 us; the launch traced here: 148 us
  waiting for transfers between devices  76.4 us (51%)
  starting transfers between devices  39.6 us (27%)
  Pallas kernels  22.3 us (15%)
  local copies, waits for them, and re-layouts  7.77 us (5%)
  other arithmetic  1.73 us (1%)
    ppermute x13, waiting for transfers between devices, to_chip(): return lax.ppermute(x, 'inner', [(i, i ^ 2 * offset) for i in range(inner)])  45.9 us
    ppermute x14, waiting for transfers between devices, to_group(): return lax.ppermute(x, 'group', [(i, i ^ offset) for i in range(groups)])  26.6 us
    ppermute x14, starting transfers between devices, to_group(): return lax.ppermute(x, 'group', [(i, i ^ offset) for i in range(groups)])  22.9 us
    pallas_call x4, Pallas kernels, run_experts(): pl.pallas_call(functools.partial(expert_kernel, main, parts), in_specs=[v...  18.9 us
    ppermute x13, starting transfers between devices, to_chip(): return lax.ppermute(x, 'inner', [(i, i ^ 2 * offset) for i in range(inner)])  14.5 us
    unnamed x23, local copies, waits for them, and re-layouts  7.47 us
    ppermute x12, waiting for transfers between devices, to_core(): return lax.ppermute(x, 'inner', [(i, i ^ 1) for i in range(inner)])  3.92 us
  transfers between devices with their start and end apart: 39, of which 22 were waited for; matrix products, arithmetic and copies ran while one was open for 1% of the time, Pallas kernels for 13%

profile of v6, /device:TPU:0, one launch (start us, length us, event | category | flops | bytes accessed | tf_op | source)
XLA Modules:
  0.0 148.3 jit_solution(12304326364776057727)
XLA Ops:
  3.5 3.0 %collective-permute-start.1 = (bf16[16,8960]{1,0:T(8,128)(2,1)S(1)}, bf16[16,8960]{1,0:T(8,128)(2,1)S(1)}, u32[]{:S(2)}, u32[]{:S(2)}) collective-permute-start(bf16[16,8960]{1,0:T(8,128)(2,1)S(1)} %get-tuple-element.208), channel_id=1, source_target_pairs={{0,2},{1,3},{2,0},{3,1},{4,6},{5,7},{6,4},{7,5},{8,10},{9,11},{10,... | collective-permute-start | bytes 860168 | tf_op jit(solution)/shard_map/ppermute | solution.py:231
  8.0 3.5 %collective-permute-start.7 = (bf16[16,8960]{1,0:T(8,128)(2,1)S(1)}, bf16[16,8960]{1,0:T(8,128)(2,1)S(1)}, u32[]{:S(2)}, u32[]{:S(2)}) collective-permute-start(bf16[16,8960]{1,0:T(8,128)(2,1)S(1)} %get-tuple-element.225), channel_id=1, source_target_pairs={{0,28},{4,24},{8,20},{12,16},{16,12},{20,8},{24,4},{28,0},{1,29},{... | collective-permute-start | bytes 860168 | tf_op jit(solution)/shard_map/ppermute | solution.py:228
  13.1 3.1 %copy-done = bf16[1,7168,512]{2,1,0:T(8,128)(2,1)S(1)} copy-done((bf16[1,7168,512]{2,1,0:T(8,128)(2,1)S(1)}, bf16[1,7168,512]{2,1,0:T(8,128)(2,1)}, u32[]{:S(2)}) %copy-start) | copy-done | bytes 7340056
  17.2 2.1 %copy-done.1 = bf16[1,7168,512]{2,1,0:T(8,128)(2,1)S(1)} copy-done((bf16[1,7168,512]{2,1,0:T(8,128)(2,1)S(1)}, bf16[1,7168,512]{2,1,0:T(8,128)(2,1)}, u32[]{:S(2)}) %copy-start.1) | copy-done | bytes 7340056
  19.3 3.1 %collective-permute-done = bf16[16,8960]{1,0:T(8,128)(2,1)S(1)} collective-permute-done((bf16[16,8960]{1,0:T(8,128)(2,1)S(1)}, bf16[16,8960]{1,0:T(8,128)(2,1)S(1)}, u32[]{:S(2)}, u32[]{:S(2)}) %collective-permute-start) | collective-permute-done | bytes 286752 | tf_op jit(solution)/shard_map/ppermute | solution.py:228
  22.5 6.5 %collective-permute-done.2 = bf16[16,8960]{1,0:T(8,128)(2,1)S(1)} collective-permute-done((bf16[16,8960]{1,0:T(8,128)(2,1)S(1)}, bf16[16,8960]{1,0:T(8,128)(2,1)S(1)}, u32[]{:S(2)}, u32[]{:S(2)}) %collective-permute-start.2) | collective-permute-done | bytes 286752 | tf_op jit(solution)/shard_map/ppermute | solution.py:231
  34.6 2.4 %collective-permute-done.8 = bf16[16,8960]{1,0:T(8,128)(2,1)S(1)} collective-permute-done((bf16[16,8960]{1,0:T(8,128)(2,1)S(1)}, bf16[16,8960]{1,0:T(8,128)(2,1)S(1)}, u32[]{:S(2)}, u32[]{:S(2)}) %collective-permute-start.8) | collective-permute-done | bytes 286752 | tf_op jit(solution)/shard_map/ppermute | solution.py:228
  37.0 4.7 %experts.4 = (bf16[64,8960]{1,0:T(8,128)(2,1)S(1)}, bf16[64,8960]{1,0:T(8,128)(2,1)S(1)}) custom-call(bf16[7168,512]{1,0:T(8,128)(2,1)S(1)} %bitcast.9, bf16[7168,512]{1,0:T(8,128)(2,1)S(1)} %bitcast.14, bf16[512,7168]{1,0:T(8,128)(2,1)S(1)} %bitcast.19, bf16[32,8960]{1,0:T(8,128)(2,1)S(1)} %constant_dynamic-update-slice_fusion.refs_0_, ...), custom_call_target="tpu_custom_call" | custom-call | flops 3523215360 | bytes 4587520 | tf_op jit(solution)/shard_map/experts/pallas_call | solution.py:175
  44.0 7.6 %collective-permute-done.10 = bf16[16,8960]{1,0:T(8,128)(2,1)S(1)} collective-permute-done((bf16[16,8960]{1,0:T(8,128)(2,1)S(1)}, bf16[16,8960]{1,0:T(8,128)(2,1)S(1)}, u32[]{:S(2)}, u32[]{:S(2)}) %collective-permute-start.10) | collective-permute-done | bytes 286752 | tf_op jit(solution)/shard_map/ppermute | solution.py:231
  54.6 4.7 %experts.5 = (bf16[64,8960]{1,0:T(8,128)(2,1)S(1)}, bf16[64,8960]{1,0:T(8,128)(2,1)S(1)}) custom-call(bf16[7168,512]{1,0:T(8,128)(2,1)S(1)} %bitcast.10, bf16[7168,512]{1,0:T(8,128)(2,1)S(1)} %bitcast.15, bf16[512,7168]{1,0:T(8,128)(2,1)S(1)} %bitcast.20, bf16[32,8960]{1,0:T(8,128)(2,1)S(1)} %constant_dynamic-update-slice_fusion.4.refs_0_, ...), custom_call_target="tpu_custom_call" | custom-call | flops 3523215360 | bytes 4587520 | tf_op jit(solution)/shard_map/experts/pallas_call | solution.py:175
  64.4 4.7 %experts.6 = (bf16[64,8960]{1,0:T(8,128)(2,1)S(1)}, bf16[64,8960]{1,0:T(8,128)(2,1)S(1)}) custom-call(bf16[7168,512]{1,0:T(8,128)(2,1)S(1)} %bitcast.11, bf16[7168,512]{1,0:T(8,128)(2,1)S(1)} %bitcast.16, bf16[512,7168]{1,0:T(8,128)(2,1)S(1)} %bitcast.21, bf16[32,8960]{1,0:T(8,128)(2,1)S(1)} %pad_maximum_fusion.2.refs_0_, ...), custom_call_target="tpu_custom_call" | custom-call | flops 3523215360 | bytes 4587520 | tf_op jit(solution)/shard_map/experts/pallas_call | solution.py:175
  72.0 5.9 %collective-permute-done.23.refs_1_ = bf16[32,8960]{1,0:T(8,128)(2,1)S(1)} collective-permute-done((bf16[32,8960]{1,0:T(8,128)(2,1)S(1)}, bf16[32,8960]{1,0:T(8,128)(2,1)S(1)}, u32[]{:S(2)}, u32[]{:S(2)}) %collective-permute-start.23) | collective-permute-done | bytes 573472 | tf_op jit(solution)/shard_map/ppermute | solution.py:231
  79.9 4.7 %experts.7 = (bf16[64,8960]{1,0:T(8,128)(2,1)S(1)}, bf16[64,8960]{1,0:T(8,128)(2,1)S(1)}) custom-call(bf16[7168,512]{1,0:T(8,128)(2,1)S(1)} %bitcast.12, bf16[7168,512]{1,0:T(8,128)(2,1)S(1)} %bitcast.17, bf16[512,7168]{1,0:T(8,128)(2,1)S(1)} %bitcast.22, bf16[32,8960]{1,0:T(8,128)(2,1)S(1)} %collective-permute-done.18.refs_0_, ...), custom_call_target="tpu_custom_call" | custom-call | flops 3523215360 | bytes 4587520 | tf_op jit(solution)/shard_map/experts/pallas_call | solution.py:175
  84.9 5.4 %collective-permute-done.20 = bf16[16,8960]{1,0:T(8,128)(2,1)S(1)} collective-permute-done((bf16[16,8960]{1,0:T(8,128)(2,1)S(1)}, bf16[16,8960]{1,0:T(8,128)(2,1)S(1)}, u32[]{:S(2)}, u32[]{:S(2)}) %collective-permute-start.20) | collective-permute-done | bytes 286752 | tf_op jit(solution)/shard_map/ppermute | solution.py:231
  90.3 5.1 %collective-permute-start.28 = (bf16[16,8960]{1,0:T(8,128)(2,1)S(1)}, bf16[16,8960]{1,0:T(8,128)(2,1)S(1)}, u32[]{:S(2)}, u32[]{:S(2)}) collective-permute-start(bf16[16,8960]{1,0:T(8,128)(2,1)S(1)} %get-tuple-element.337), channel_id=1, source_target_pairs={{0,28},{4,24},{8,20},{12,16},{16,12},{20,8},{24,4},{28,0},{1,29},{... | collective-permute-start | bytes 860168 | tf_op jit(solution)/shard_map/ppermute | solution.py:228
  97.9 4.9 %collective-permute-done.28.refs_7_ = bf16[16,8960]{1,0:T(8,128)(2,1)S(1)} collective-permute-done((bf16[16,8960]{1,0:T(8,128)(2,1)S(1)}, bf16[16,8960]{1,0:T(8,128)(2,1)S(1)}, u32[]{:S(2)}, u32[]{:S(2)}) %collective-permute-start.28) | collective-permute-done | bytes 286752 | tf_op jit(solution)/shard_map/ppermute | solution.py:228
  103.0 5.6 %collective-permute-done.31 = bf16[16,8960]{1,0:T(8,128)(2,1)S(1)} collective-permute-done((bf16[16,8960]{1,0:T(8,128)(2,1)S(1)}, bf16[16,8960]{1,0:T(8,128)(2,1)S(1)}, u32[]{:S(2)}, u32[]{:S(2)}) %collective-permute-start.31) | collective-permute-done | bytes 286752 | tf_op jit(solution)/shard_map/ppermute | solution.py:231
  108.7 5.2 %collective-permute-done.30 = bf16[16,8960]{1,0:T(8,128)(2,1)S(1)} collective-permute-done((bf16[16,8960]{1,0:T(8,128)(2,1)S(1)}, bf16[16,8960]{1,0:T(8,128)(2,1)S(1)}, u32[]{:S(2)}, u32[]{:S(2)}) %collective-permute-start.30) | collective-permute-done | bytes 286752 | tf_op jit(solution)/shard_map/ppermute | solution.py:231
  116.0 2.4 %collective-permute-start.36 = (bf16[16,8960]{1,0:T(8,128)(2,1)S(1)}, bf16[16,8960]{1,0:T(8,128)(2,1)S(1)}, u32[]{:S(2)}, u32[]{:S(2)}) collective-permute-start(bf16[16,8960]{1,0:T(8,128)(2,1)S(1)} %fusion.1), channel_id=1, source_target_pairs={{0,20},{4,16},{8,28},{12,24},{16,4},{20,0},{24,12},{28,8},{1,21},{... | collective-permute-start | bytes 860168 | tf_op jit(solution)/shard_map/ppermute | solution.py:228
  118.4 2.7 %collective-permute-start.35 = (bf16[16,8960]{1,0:T(8,128)(2,1)S(1)}, bf16[16,8960]{1,0:T(8,128)(2,1)S(1)}, u32[]{:S(2)}, u32[]{:S(2)}) collective-permute-start(bf16[16,8960]{1,0:T(8,128)(2,1)S(1)} %get-tuple-element.365), channel_id=1, source_target_pairs={{0,12},{4,8},{8,4},{12,0},{16,28},{20,24},{24,20},{28,16},{1,13},{... | collective-permute-start | bytes 860168 | tf_op jit(solution)/shard_map/ppermute | solution.py:228
  121.1 7.0 %collective-permute-done.29 = bf16[32,8960]{1,0:T(8,128)(2,1)S(1)} collective-permute-done((bf16[32,8960]{1,0:T(8,128)(2,1)S(1)}, bf16[32,8960]{1,0:T(8,128)(2,1)S(1)}, u32[]{:S(2)}, u32[]{:S(2)}) %collective-permute-start.29) | collective-permute-done | bytes 573472 | tf_op jit(solution)/shard_map/ppermute | solution.py:231
  131.0 7.1 %collective-permute-done.37.refs_4_ = bf16[16,8960]{1,0:T(8,128)(2,1)S(1)} collective-permute-done((bf16[16,8960]{1,0:T(8,128)(2,1)S(1)}, bf16[16,8960]{1,0:T(8,128)(2,1)S(1)}, u32[]{:S(2)}, u32[]{:S(2)}) %collective-permute-start.37) | collective-permute-done | bytes 286752 | tf_op jit(solution)/shard_map/ppermute | solution.py:228
  138.1 4.9 %collective-permute-done.36.refs_5_ = bf16[16,8960]{1,0:T(8,128)(2,1)S(1)} collective-permute-done((bf16[16,8960]{1,0:T(8,128)(2,1)S(1)}, bf16[16,8960]{1,0:T(8,128)(2,1)S(1)}, u32[]{:S(2)}, u32[]{:S(2)}) %collective-permute-start.36) | collective-permute-done | bytes 286752 | tf_op jit(solution)/shard_map/ppermute | solution.py:228
  143.0 3.0 %collective-permute-done.34.refs_2_ = bf16[16,8960]{1,0:T(8,128)(2,1)S(1)} collective-permute-done((bf16[16,8960]{1,0:T(8,128)(2,1)S(1)}, bf16[16,8960]{1,0:T(8,128)(2,1)S(1)}, u32[]{:S(2)}, u32[]{:S(2)}) %collective-permute-start.34) | collective-permute-done | bytes 286752 | tf_op jit(solution)/shard_map/ppermute | solution.py:228
  (109 shorter events, 38.3 us)
Async XLA Ops:
  3.5 12.7 %collective-permute-start.1 = (bf16[16,8960]{1,0:T(8,128)(2,1)S(1)}, bf16[16,8960]{1,0:T(8,128)(2,1)S(1)}, u32[]{:S(2)}, u32[]{:S(2)}) collective-permute-start(bf16[16,8960]{1,0:T(8,128)(2,1)S(1)} %get-tuple-element.208), channel_id=1, source_target_pairs={{0,2},{1,3},{2,0},{3,1},{4,6},{5,7},{6,4},{7,5},{8,10},{9,11},{10,... | collective-permute-start | bytes 860168 | tf_op jit(solution)/shard_map/ppermute | solution.py:231
  6.5 15.9 %collective-permute-start = (bf16[16,8960]{1,0:T(8,128)(2,1)S(1)}, bf16[16,8960]{1,0:T(8,128)(2,1)S(1)}, u32[]{:S(2)}, u32[]{:S(2)}) collective-permute-start(bf16[16,8960]{1,0:T(8,128)(2,1)S(1)} %get-tuple-element.199), channel_id=1, source_target_pairs={{0,4},{4,0},{8,12},{12,8},{16,20},{20,16},{24,28},{28,24},{1,5},{5... | collective-permute-start | bytes 860168 | tf_op jit(solution)/shard_map/ppermute | solution.py:228
  8.0 23.1 %collective-permute-start.7 = (bf16[16,8960]{1,0:T(8,128)(2,1)S(1)}, bf16[16,8960]{1,0:T(8,128)(2,1)S(1)}, u32[]{:S(2)}, u32[]{:S(2)}) collective-permute-start(bf16[16,8960]{1,0:T(8,128)(2,1)S(1)} %get-tuple-element.225), channel_id=1, source_target_pairs={{0,28},{4,24},{8,20},{12,16},{16,12},{20,8},{24,4},{28,0},{1,29},{... | collective-permute-start | bytes 860168 | tf_op jit(solution)/shard_map/ppermute | solution.py:228
  11.5 20.4 %collective-permute-start.6 = (bf16[32,8960]{1,0:T(8,128)(2,1)S(1)}, bf16[32,8960]{1,0:T(8,128)(2,1)S(1)}, u32[]{:S(2)}, u32[]{:S(2)}) collective-permute-start(bf16[32,8960]{1,0:T(8,128)(2,1)S(1)} %pad_maximum_fusion), channel_id=1, source_target_pairs={{0,8},{4,12},{8,0},{12,4},{16,24},{20,28},{24,16},{28,20},{1,9},{5... | collective-permute-start | bytes 1720328 | tf_op jit(solution)/shard_map/ppermute | solution.py:228
  11.5 20.4 %collective-permute-start.5 = (bf16[16,8960]{1,0:T(8,128)(2,1)S(1)}, bf16[16,8960]{1,0:T(8,128)(2,1)S(1)}, u32[]{:S(2)}, u32[]{:S(2)}) collective-permute-start(bf16[16,8960]{1,0:T(8,128)(2,1)S(1)} %get-tuple-element.223), channel_id=1, source_target_pairs={{0,4},{4,0},{8,12},{12,8},{16,20},{20,16},{24,28},{28,24},{1,5},{5... | collective-permute-start | bytes 860168 | tf_op jit(solution)/shard_map/ppermute | solution.py:228
  16.2 20.8 %collective-permute-start.8 = (bf16[16,8960]{1,0:T(8,128)(2,1)S(1)}, bf16[16,8960]{1,0:T(8,128)(2,1)S(1)}, u32[]{:S(2)}, u32[]{:S(2)}) collective-permute-start(bf16[16,8960]{1,0:T(8,128)(2,1)S(1)} %get-tuple-element.235), channel_id=1, source_target_pairs={{0,24},{4,28},{8,16},{12,20},{16,8},{20,12},{24,0},{28,4},{1,25},{... | collective-permute-start | bytes 860168 | tf_op jit(solution)/shard_map/ppermute | solution.py:228
  32.1 9.9 %collective-permute-start.11 = (bf16[16,8960]{1,0:T(8,128)(2,1)S(1)}, bf16[16,8960]{1,0:T(8,128)(2,1)S(1)}, u32[]{:S(2)}, u32[]{:S(2)}) collective-permute-start(bf16[16,8960]{1,0:T(8,128)(2,1)S(1)} %get-tuple-element.249), channel_id=1, source_target_pairs={{0,4},{4,0},{8,12},{12,8},{16,20},{20,16},{24,28},{28,24},{1,5},{5... | collective-permute-start | bytes 860168 | tf_op jit(solution)/shard_map/ppermute | solution.py:228
  33.5 18.0 %collective-permute-start.12 = (bf16[16,8960]{1,0:T(8,128)(2,1)S(1)}, bf16[16,8960]{1,0:T(8,128)(2,1)S(1)}, u32[]{:S(2)}, u32[]{:S(2)}) collective-permute-start(bf16[16,8960]{1,0:T(8,128)(2,1)S(1)} %collective-permute-done.7), channel_id=1, source_target_pairs={{0,2},{1,3},{2,0},{3,1},{4,6},{5,7},{6,4},{7,5},{8,10},{9,11},{10,... | collective-permute-start | bytes 860168 | tf_op jit(solution)/shard_map/ppermute | solution.py:231
  34.2 27.3 %collective-permute-start.18 = (bf16[32,8960]{1,0:T(8,128)(2,1)S(1)}, bf16[32,8960]{1,0:T(8,128)(2,1)S(1)}, u32[]{:S(2)}, u32[]{:S(2)}) collective-permute-start(bf16[32,8960]{1,0:T(8,128)(2,1)S(1)} %pad_maximum_fusion.1), channel_id=1, source_target_pairs={{0,16},{4,20},{8,24},{12,28},{16,0},{20,4},{24,8},{28,12},{1,17},{... | collective-permute-start | bytes 1720328 | tf_op jit(solution)/shard_map/ppermute | solution.py:228
  42.0 12.7 %collective-permute-start.15 = (bf16[16,8960]{1,0:T(8,128)(2,1)S(1)}, bf16[16,8960]{1,0:T(8,128)(2,1)S(1)}, u32[]{:S(2)}, u32[]{:S(2)}) collective-permute-start(bf16[16,8960]{1,0:T(8,128)(2,1)S(1)} %get-tuple-element.268), channel_id=1, source_target_pairs={{0,2},{1,3},{2,0},{3,1},{4,6},{5,7},{6,4},{7,5},{8,10},{9,11},{10,... | collective-permute-start | bytes 860168 | tf_op jit(solution)/shard_map/ppermute | solution.py:231
  62.1 15.8 %collective-permute-start.23 = (bf16[32,8960]{1,0:T(8,128)(2,1)S(1)}, bf16[32,8960]{1,0:T(8,128)(2,1)S(1)}, u32[]{:S(2)}, u32[]{:S(2)}) collective-permute-start(bf16[32,8960]{1,0:T(8,128)(2,1)S(1)} %collective-permute-done.18.refs_0_), channel_id=1, source_target_pairs={{0,2},{1,3},{2,0},{3,1},{4,6},{5,7},{6,4},{7,5},{8,10},{9,11},{10,... | collective-permute-start | bytes 1720328 | tf_op jit(solution)/shard_map/ppermute | solution.py:231
  69.9 15.0 %collective-permute-start.22 = (bf16[16,8960]{1,0:T(8,128)(2,1)S(1)}, bf16[16,8960]{1,0:T(8,128)(2,1)S(1)}, u32[]{:S(2)}, u32[]{:S(2)}) collective-permute-start(bf16[16,8960]{1,0:T(8,128)(2,1)S(1)} %get-tuple-element.309), channel_id=1, source_target_pairs={{0,2},{1,3},{2,0},{3,1},{4,6},{5,7},{6,4},{7,5},{8,10},{9,11},{10,... | collective-permute-start | bytes 860168 | tf_op jit(solution)/shard_map/ppermute | solution.py:231
  71.4 18.8 %collective-permute-start.20 = (bf16[16,8960]{1,0:T(8,128)(2,1)S(1)}, bf16[16,8960]{1,0:T(8,128)(2,1)S(1)}, u32[]{:S(2)}, u32[]{:S(2)}) collective-permute-start(bf16[16,8960]{1,0:T(8,128)(2,1)S(1)} %get-tuple-element.296), channel_id=1, source_target_pairs={{0,2},{1,3},{2,0},{3,1},{4,6},{5,7},{6,4},{7,5},{8,10},{9,11},{10,... | collective-permute-start | bytes 860168 | tf_op jit(solution)/shard_map/ppermute | solution.py:231
  78.1 24.7 %collective-permute-start.32 = (bf16[32,8960]{1,0:T(8,128)(2,1)S(1)}, bf16[32,8960]{1,0:T(8,128)(2,1)S(1)}, u32[]{:S(2)}, u32[]{:S(2)}) collective-permute-start(bf16[32,8960]{1,0:T(8,128)(2,1)S(1)} %add_convert_fusion.3), channel_id=1, source_target_pairs={{0,2},{1,3},{2,0},{3,1},{4,6},{5,7},{6,4},{7,5},{8,10},{9,11},{10,... | collective-permute-start | bytes 1720328 | tf_op jit(solution)/shard_map/ppermute | solution.py:231
  90.3 12.4 %collective-permute-start.28 = (bf16[16,8960]{1,0:T(8,128)(2,1)S(1)}, bf16[16,8960]{1,0:T(8,128)(2,1)S(1)}, u32[]{:S(2)}, u32[]{:S(2)}) collective-permute-start(bf16[16,8960]{1,0:T(8,128)(2,1)S(1)} %get-tuple-element.337), channel_id=1, source_target_pairs={{0,28},{4,24},{8,20},{12,16},{16,12},{20,8},{24,4},{28,0},{1,29},{... | collective-permute-start | bytes 860168 | tf_op jit(solution)/shard_map/ppermute | solution.py:228
  95.8 12.9 %collective-permute-start.31 = (bf16[16,8960]{1,0:T(8,128)(2,1)S(1)}, bf16[16,8960]{1,0:T(8,128)(2,1)S(1)}, u32[]{:S(2)}, u32[]{:S(2)}) collective-permute-start(bf16[16,8960]{1,0:T(8,128)(2,1)S(1)} %get-tuple-element.348), channel_id=1, source_target_pairs={{0,2},{1,3},{2,0},{3,1},{4,6},{5,7},{6,4},{7,5},{8,10},{9,11},{10,... | collective-permute-start | bytes 860168 | tf_op jit(solution)/shard_map/ppermute | solution.py:231
  96.2 17.8 %collective-permute-start.30 = (bf16[16,8960]{1,0:T(8,128)(2,1)S(1)}, bf16[16,8960]{1,0:T(8,128)(2,1)S(1)}, u32[]{:S(2)}, u32[]{:S(2)}) collective-permute-start(bf16[16,8960]{1,0:T(8,128)(2,1)S(1)} %get-tuple-element.347), channel_id=1, source_target_pairs={{0,2},{1,3},{2,0},{3,1},{4,6},{5,7},{6,4},{7,5},{8,10},{9,11},{10,... | collective-permute-start | bytes 860168 | tf_op jit(solution)/shard_map/ppermute | solution.py:231
  97.9 32.5 %collective-permute-start.38 = (bf16[16,8960]{1,0:T(8,128)(2,1)S(1)}, bf16[16,8960]{1,0:T(8,128)(2,1)S(1)}, u32[]{:S(2)}, u32[]{:S(2)}) collective-permute-start(bf16[16,8960]{1,0:T(8,128)(2,1)S(1)} %get-tuple-element.368), channel_id=1, source_target_pairs={{0,24},{4,28},{8,16},{12,20},{16,8},{20,12},{24,0},{28,4},{1,25},{... | collective-permute-start | bytes 860168 | tf_op jit(solution)/shard_map/ppermute | solution.py:228
  113.9 14.1 %collective-permute-start.29 = (bf16[32,8960]{1,0:T(8,128)(2,1)S(1)}, bf16[32,8960]{1,0:T(8,128)(2,1)S(1)}, u32[]{:S(2)}, u32[]{:S(2)}) collective-permute-start(bf16[32,8960]{1,0:T(8,128)(2,1)S(1)} %add_convert_fusion.5), channel_id=1, source_target_pairs={{0,2},{1,3},{2,0},{3,1},{4,6},{5,7},{6,4},{7,5},{8,10},{9,11},{10,... | collective-permute-start | bytes 1720328 | tf_op jit(solution)/shard_map/ppermute | solution.py:231
  115.5 22.6 %collective-permute-start.37 = (bf16[16,8960]{1,0:T(8,128)(2,1)S(1)}, bf16[16,8960]{1,0:T(8,128)(2,1)S(1)}, u32[]{:S(2)}, u32[]{:S(2)}) collective-permute-start(bf16[16,8960]{1,0:T(8,128)(2,1)S(1)} %fusion), channel_id=1, source_target_pairs={{0,16},{4,20},{8,24},{12,28},{16,0},{20,4},{24,8},{28,12},{1,17},{... | collective-permute-start | bytes 860168 | tf_op jit(solution)/shard_map/ppermute | solution.py:228
  116.0 27.0 %collective-permute-start.36 = (bf16[16,8960]{1,0:T(8,128)(2,1)S(1)}, bf16[16,8960]{1,0:T(8,128)(2,1)S(1)}, u32[]{:S(2)}, u32[]{:S(2)}) collective-permute-start(bf16[16,8960]{1,0:T(8,128)(2,1)S(1)} %fusion.1), channel_id=1, source_target_pairs={{0,20},{4,16},{8,28},{12,24},{16,4},{20,0},{24,12},{28,8},{1,21},{... | collective-permute-start | bytes 860168 | tf_op jit(solution)/shard_map/ppermute | solution.py:228
  118.4 24.6 %collective-permute-start.35 = (bf16[16,8960]{1,0:T(8,128)(2,1)S(1)}, bf16[16,8960]{1,0:T(8,128)(2,1)S(1)}, u32[]{:S(2)}, u32[]{:S(2)}) collective-permute-start(bf16[16,8960]{1,0:T(8,128)(2,1)S(1)} %get-tuple-element.365), channel_id=1, source_target_pairs={{0,12},{4,8},{8,4},{12,0},{16,28},{20,24},{24,20},{28,16},{1,13},{... | collective-permute-start | bytes 860168 | tf_op jit(solution)/shard_map/ppermute | solution.py:228
  128.1 18.0 %collective-permute-start.34 = (bf16[16,8960]{1,0:T(8,128)(2,1)S(1)}, bf16[16,8960]{1,0:T(8,128)(2,1)S(1)}, u32[]{:S(2)}, u32[]{:S(2)}) collective-permute-start(bf16[16,8960]{1,0:T(8,128)(2,1)S(1)} %get-tuple-element.364), channel_id=1, source_target_pairs={{0,8},{4,12},{8,0},{12,4},{16,24},{20,28},{24,16},{28,20},{1,9},{5... | collective-permute-start | bytes 860168 | tf_op jit(solution)/shard_map/ppermute | solution.py:228
  130.4 15.7 %collective-permute-start.33 = (bf16[16,8960]{1,0:T(8,128)(2,1)S(1)}, bf16[16,8960]{1,0:T(8,128)(2,1)S(1)}, u32[]{:S(2)}, u32[]{:S(2)}) collective-permute-start(bf16[16,8960]{1,0:T(8,128)(2,1)S(1)} %get-tuple-element.363), channel_id=1, source_target_pairs={{0,4},{4,0},{8,12},{12,8},{16,20},{20,16},{24,28},{28,24},{1,5},{5... | collective-permute-start | bytes 860168 | tf_op jit(solution)/shard_map/ppermute | solution.py:228
  (24 other events, 151.8 us)
